TPU v7x, 32 devices: a whole 2x2x4 slice. The times are simulated.
32 devices in a mesh: ex: 8 (over z, x), feat: 4 (over y, core).
Axes of the slice: x: 2, y: 2, z: 4, core: 2. Of those that a mesh axis runs over, the one named last changes fastest.
Arguments:
- train_grads: bfloat16 [4096, 32768], P('ex', 'feat'), may hold values from -0.03125 to 0.03125
- audit_grads: bfloat16 [2, 8, 32, 32768], P(None, 'ex', None, 'feat'), may hold values from -6 to 6
- owner_map: int32 [16], replicated, may hold values from 0 to 15, as said below
- pair_blocks: int32 [8, 8], P('ex'), may hold values from 0 to 15, as said below
- pair_counts: int32 [8], P('ex'), may hold values from 1 to 8, as said below
Outputs:
- tiles: float32 [8, 8, 32, 512], P('ex', 'feat')
Inputs may be any that keep to these rules, and one draw needn't show every extreme that they name: `owner_map`: a permutation of the audit blocks. `pair_blocks`: the 8 entries of each training block name audit blocks whose stored blocks lie on 8 different indices of ex (owner_map[a] % 8 differs); entries at or after pair_counts are not live. `pair_counts`: some training block has all 8 pairs live.
All inputs are finite; a program needn't handle non-finite values.
Results may differ from a plain program's by a relative error of at most 0.0003.
Values may be sent and summed in bfloat16 or wider, within the bound.
No kernel may reach another device: no remote copies, remote signals or barrier semaphores. Data moves between devices by JAX's collectives and lax.ppermute only.
A program may use at most 64 MiB of HBM per device.

v0:
```python
import jax
import jax.numpy as jnp
from jax import lax
from jax.sharding import PartitionSpec as P


def shards(train_grads, audit_grads, owner_map, pair_blocks, pair_counts):
    peers = lax.axis_size("ex")
    stored = jnp.take(owner_map, pair_blocks[0])
    holder = stored % peers
    local = stored // peers
    order = jnp.arange(peers, dtype=jnp.int32)
    live = (order < pair_counts[0]).astype(jnp.float32)
    wanted = jnp.sum(jnp.where(holder[None, :] == order[:, None], local[None, :], 0), axis=1)
    asked = lax.all_to_all(wanted.reshape(peers, 1), "ex", split_axis=0, concat_axis=0, tiled=True)
    own_blocks = audit_grads[:, 0]
    reply = jnp.take(own_blocks, asked[:, 0], axis=0)
    fetched = lax.all_to_all(reply, "ex", split_axis=0, concat_axis=0, tiled=True)
    rows = jnp.take(fetched, holder, axis=0)
    scores = jnp.einsum("kaf,tf->kat", rows, train_grads, preferred_element_type=jnp.float32)
    tiles = lax.psum_scatter(scores * live[:, None, None], "feat", scatter_dimension=0, tiled=True)
    return tiles[None]


def solution(mesh):
    in_specs = (P("ex", "feat"), P(None, "ex", None, "feat"), P(), P("ex", None), P("ex"))
    out_specs = P("ex", "feat", None, None)
    return jax.shard_map(shards, mesh=mesh, in_specs=in_specs, out_specs=out_specs, check_vma=False)
```

profile of v0, /device:TPU:0, one launch (start us, length us, event | category | flops | bytes accessed | tf_op | source)
XLA Modules:
  0.0 167.9 jit_solution(5021916730537087910)
XLA Ops:
  6.5 0.0 copy-start
  6.5 0.7 fusion.17
  7.3 1.3 gather_fusion
  8.6 0.7 fusion.10
  9.3 0.1 select_reduce_fusion
  9.4 0.1 copy.8
  9.5 13.5 %all_to_all.20 = s32[8,1,1]{2,1,0:T(1,128)S(1)} all-to-all(s32[8,1,1]{2,1,0:T(1,128)S(1)} %copy.8), channel_id=1, replica_groups=mesh['ex'=8,'feat'=4] {'ex'}, dimensions={0} | all-to-all | bytes 64 | tf_op jit(solution)/shard_map/all_to_all | solution.py:15
  23.0 0.2 reduce
  23.3 0.0 copy-done
  23.3 2.8 %gather_fusion.1 = bf16[8,32,8192]{2,1,0:T(8,128)(2,1)} fusion(bf16[2,32,8192]{2,1,0:T(8,128)(2,1)S(1)} %bitcast.39, s32[1024]{0:T(1024)S(1)} %pad_clamp_fusion.1), kind=kCustom, calls=%fused_computation.1 | custom fusion | bytes 8388640 | tf_op jit(solution)/shard_map/jit(_take)/gather | solution.py:17
  26.0 4.6 %broadcast_select_fusion = bf16[8,32,8192]{2,1,0:T(8,128)(2,1)} fusion(bf16[8,32,8192]{2,1,0:T(8,128)(2,1)} %gather_fusion.1, pred[8]{0:T(512)(128)(4,1)S(1)} %compare_and_fusion), kind=kLoop, calls=%fused_computation.6 | loop fusion | flops 2097152 | bytes 8388616 | tf_op jit(solution)/shard_map/jit(_take)/select_n | solution.py:17
  30.7 0.0 copy-start.1
  30.7 4.7 %all-to-all-start.1 = ((bf16[8,32,8192]{2,1,0:T(8,128)(2,1)}), bf16[8,32,8192]{2,1,0:T(8,128)(2,1)}, u32[]{:S(2)}, u32[]{:S(2)}) async-start(bf16[8,32,8192]{2,1,0:T(8,128)(2,1)} %broadcast_select_fusion), calls=%async_computation.1 | async-start | bytes 8388608 | tf_op jit(solution)/shard_map/all_to_all | solution.py:18
  35.3 0.0 reduce-scatter.2.cloned.1.call-start
  36.0 0.0 copy-done.1
  36.1 91.3 %all-to-all-done.1 = bf16[8,32,8192]{2,1,0:T(8,128)(2,1)} async-done(((bf16[8,32,8192]{2,1,0:T(8,128)(2,1)}), bf16[8,32,8192]{2,1,0:T(8,128)(2,1)}, u32[]{:S(2)}, u32[]{:S(2)}) %all-to-all-start.1) | async-done | bytes 4194336 | tf_op jit(solution)/shard_map/all_to_all | solution.py:18
  127.4 5.0 %gather_fusion.2 = bf16[8,32,8192]{2,1,0:T(8,128)(2,1)} fusion(bf16[8,32,8192]{2,1,0:T(8,128)(2,1)} %all-to-all-done.1, s32[1024]{0:T(1024)S(1)} %pad_clamp_fusion), kind=kCustom, calls=%fused_computation.2 | custom fusion | bytes 8388640 | tf_op jit(solution)/shard_map/jit(_take)/gather | solution.py:19
  132.3 7.8 %fusion.5 = f32[8,32,512]{2,1,0:T(8,128)} fusion(bf16[512,8192]{1,0:T(8,128)(2,1)} %param.5, bf16[8,32,8192]{2,1,0:T(8,128)(2,1)} %gather_fusion.2, pred[8]{0:T(512)(128)(4,1)S(1)} %get-tuple-element.8, f32[8]{0:T(128)S(1)} %get-tuple-element.7), kind=kOutput, calls=%fused_computation.9 | convolution fusion | flops 2149711872 | bytes 13107240 | tf_op jit(solution)/shard_map/kaf,tf->kat/dot_general | solution.py:20
  140.1 0.0 reduce-scatter.2.cloned.1.call-update
  140.2 20.9 %reduce-scatter.2.cloned.1.call-done = f32[2,32,512]{2,1,0:T(8,128)} async-done(((f32[8,32,512]{2,1,0:T(8,128)}), f32[2,32,512]{2,1,0:T(8,128)}) %reduce-scatter.2.cloned.1.call-update) | async-done | bytes 131088 | tf_op jit(solution)/shard_map/reduce_scatter | solution.py:21
  (8 shorter events, 0.1 us)
Async XLA Ops:
  6.5 16.7 %copy-start = (bf16[2,1,32,8192]{3,2,1,0:T(8,128)(2,1)S(1)}, bf16[2,1,32,8192]{3,2,1,0:T(8,128)(2,1)}, u32[]{:S(2)}) copy-start(bf16[2,1,32,8192]{3,2,1,0:T(8,128)(2,1)} %param.6) | copy-start | bytes 3145732
  30.7 5.4 %copy-start.1 = (s32[1,8]{1,0:T(1,128)S(1)}, s32[1,8]{1,0:T(1,128)}, u32[]{:S(2)}) copy-start(s32[1,8]{1,0:T(1,128)} %param.8) | copy-start | bytes 100
  30.7 96.7 %all-to-all-start.1 = ((bf16[8,32,8192]{2,1,0:T(8,128)(2,1)}), bf16[8,32,8192]{2,1,0:T(8,128)(2,1)}, u32[]{:S(2)}, u32[]{:S(2)}) async-start(bf16[8,32,8192]{2,1,0:T(8,128)(2,1)} %broadcast_select_fusion), calls=%async_computation.1 | async-start | bytes 8388608 | tf_op jit(solution)/shard_map/all_to_all | solution.py:18
  35.3 125.7 %reduce-scatter.2.cloned.1.call-start = ((), (), s32[]{:S(2)}) async-start(), calls=%async_computation.3 | async-start | bytes 655360 | tf_op jit(solution)/shard_map/reduce_scatter | solution.py:21
Sparse Core Ops, SparseCore 0:
  140.3 20.7 reduce-scatter.1
where the time goes:
time: 168 us
  waiting for transfers between devices  112 us (67%)
  between operations  14.1 us (8%)
  blocking collectives  13.5 us (8%)
  local copies, waits for them, and re-layouts  9.13 us (5%)
  matrix products  7.81 us (5%)
  other arithmetic  6.46 us (4%)
  starting transfers between devices  4.71 us (3%)
    all_to_all x1, waiting for transfers between devices, shards(): lax.all_to_all(reply, 'ex', split_axis=0, concat_axis=0, tiled=True)  91.3 us
    reduce_scatter x1, waiting for transfers between devices, shards(): lax.psum_scatter(scores * live[:, None, None], 'feat', scatter_dimension=...  20.9 us
    all_to_all x1, blocking collectives, shards(): lax.all_to_all(wanted.reshape(peers, 1), 'ex', split_axis=0, concat_axis=...  13.5 us
    dot_general x1, matrix products, shards(): jnp.einsum('kaf,tf->kat', rows, train_grads, preferred_element_type=jnp.f...  7.81 us
    gather x1, local copies, waits for them, and re-layouts, shards(): rows = jnp.take(fetched, holder, axis=0)  4.97 us
    all_to_all x1, starting transfers between devices, shards(): lax.all_to_all(reply, 'ex', split_axis=0, concat_axis=0, tiled=True)  4.67 us
    select_n x2, other arithmetic, shards(): reply = jnp.take(own_blocks, asked[:, 0], axis=0)  4.62 us
  transfers between devices with their start and end apart: 2, of which 2 were waited for; matrix products, arithmetic and copies ran while one was open for 0% of the time, Pallas kernels for 0%

commit v1 on v0

v1 whole, which is shorter than its diff:
```python
import functools

import jax
import jax.numpy as jnp
from jax import lax
from jax.experimental import pallas as pl
from jax.experimental.pallas import tpu as pltpu
from jax.sharding import PartitionSpec as P

PAIR = 2
PARTS = 2


def matmul_kernel(rows_ref, train_ref, *rest):
    out_ref = rest[-1]

    @pl.when(pl.program_id(0) == 0)
    def _():
        out_ref[...] = rest[0][...] if len(rest) == 2 else jnp.zeros_like(out_ref)

    out_ref[...] += lax.dot_general(
        rows_ref[...], train_ref[...], (((1,), (1,)), ((), ())), preferred_element_type=jnp.float32
    )


def block_scores(rows, train, part, before):
    count, width = rows.shape
    examples = train.shape[0]
    step = min(width, 1024)
    steps = width // step
    whole = pl.BlockSpec((count, examples), lambda k: (0, 0))
    in_specs = [
        pl.BlockSpec((count, step), lambda k: (0, k)),
        pl.BlockSpec((examples, step), lambda k: (0, part * steps + k)),
    ]
    operands = [rows, train]
    if before is not None:
        in_specs.append(whole)
        operands.append(before)
    return pl.pallas_call(
        matmul_kernel,
        grid=(steps,),
        in_specs=in_specs,
        out_specs=whole,
        out_shape=jax.ShapeDtypeStruct((count, examples), jnp.float32),
        cost_estimate=pl.CostEstimate(
            flops=2 * count * examples * width,
            bytes_accessed=2 * (count + examples) * width + 4 * count * examples,
            transcendentals=0,
        ),
        compiler_params=pltpu.CompilerParams(vmem_limit_bytes=24 * 2**20),
    )(*operands)


def pick(blocks, index):
    return lax.dynamic_index_in_dim(blocks, index, 0, keepdims=False)


def shards(train_grads, audit_grads, owner_map, pair_blocks, pair_counts):
    peers = lax.axis_size("ex")
    feats = lax.axis_size("feat")
    chain = peers // PAIR
    me = lax.axis_index("ex")
    place, column = me // PAIR, me % PAIR
    own = audit_grads[:, 0]
    width = own.shape[-1] // PARTS
    across = [(i, i ^ 1) for i in range(peers)]
    upward = [(i, i + PAIR) for i in range(peers - PAIR)]
    downward = [(i + PAIR, i) for i in range(peers - PAIR)]

    stored = jnp.take(owner_map, pair_blocks[0])
    holder, local = stored % peers, stored // peers
    order = jnp.arange(peers, dtype=jnp.int32)
    wanted = jnp.sum(jnp.where(holder[None, :] == order[:, None], local[None, :], 0), axis=1)
    asked = lax.ppermute(wanted, "ex", across)

    above, below = {}, {}
    for h in range(PARTS):
        above[0, h] = below[0, h] = own[:, :, h * width : (h + 1) * width]
    for s in range(1, chain):
        for h in range(PARTS):
            below[s, h] = lax.ppermute(below[s - 1, h], "ex", upward)
            above[s, h] = lax.ppermute(above[s - 1, h], "ex", downward)

    short = jnp.minimum(place, chain - 1 - place)

    def nearest(j):
        paired = j <= 2 * short
        distance = jnp.where(paired, (j + 1) // 2, j - short)
        from_below = jnp.where(paired, j % 2 == 1, place > chain - 1 - place)
        return distance, from_below

    items = []
    items.append((place, [
        (pick(own, wanted[me])[:, h * width : (h + 1) * width],
         lax.ppermute(pick(own, asked[me])[:, h * width : (h + 1) * width], "ex", across))
        for h in range(PARTS)
    ]))
    for j in range(1, chain):
        distance, from_below = nearest(j)
        there = jnp.where(from_below, place - distance, place + distance)
        source = there * PAIR + column

        def arrived(h, index):
            result = None
            for d in sorted({(j + 1) // 2} | {j - m for m in range((j + 1) // 2)}):
                for table, side in ((below, from_below), (above, jnp.logical_not(from_below))):
                    block = pick(table[d, h], index)
                    result = block if result is None else jnp.where(
                        jnp.logical_and(side, distance == d), block, result)
            return result

        items.append((there, [
            (arrived(h, wanted[source]), lax.ppermute(arrived(h, asked[source]), "ex", across))
            for h in range(PARTS)
        ]))

    batches = [[0, 1]] + [[j] for j in range(2, chain)]
    scores, place_of = [], []
    for batch in batches:
        total = None
        for h in range(PARTS):
            rows = jnp.concatenate([r for j in batch for r in items[j][1][h]])
            total = block_scores(rows, train_grads, h, total)
        scores.append(total.reshape(len(batch) * PAIR, -1, total.shape[-1]))
        for j in batch:
            place_of += [items[j][0] * PAIR + column, items[j][0] * PAIR + (PAIR - 1 - column)]
    scores = jnp.concatenate(scores)
    where = jnp.sum(jnp.where(holder[:, None] == jnp.stack(place_of)[None, :], order[None, :], 0), axis=1)
    live = (order < pair_counts[0]).astype(jnp.float32)

    tiles = jnp.take(scores, where, axis=0) * live[:, None, None]
    f = lax.axis_index("feat")
    tiles = tiles.reshape(feats // 2, 2, peers // feats, *tiles.shape[1:])
    core = f % 2
    mine = lax.dynamic_index_in_dim(tiles, core, 1, keepdims=False)
    theirs = lax.dynamic_index_in_dim(tiles, 1 - core, 1, keepdims=False)
    mine = mine + lax.ppermute(theirs, "feat", [(i, i ^ 1) for i in range(feats)])
    half = feats // 2
    row = f // 2
    result = lax.dynamic_index_in_dim(mine, row, 0, keepdims=False)
    for k in range(1, half):
        to = (row + k) % half
        send = lax.dynamic_index_in_dim(mine, to, 0, keepdims=False)
        result = result + lax.ppermute(send, "feat", [(i, (i + 2 * k) % feats) for i in range(feats)])
    return result[None]


def solution(mesh):
    in_specs = (P("ex", "feat"), P(None, "ex", None, "feat"), P(), P("ex", None), P("ex"))
    out_specs = P("ex", "feat", None, None)
    return jax.shard_map(shards, mesh=mesh, in_specs=in_specs, out_specs=out_specs, check_vma=False)
```

time: 168 us -> 139 us (0.83)
  waiting for transfers between devices: 112 us -> 47.9 us
  starting transfers between devices: 4.71 us -> 47 us
  Pallas kernels: 0 us -> 13.5 us
  blocking collectives: 13.5 us -> 0 us
  matrix products: 7.81 us -> 0 us
  local copies, waits for them, and re-layouts: 9.13 us -> 6.8 us
  between operations: 14.1 us -> 16.2 us
    all_to_all x1 -> x0, waiting for transfers between devices: 91.3 us -> none  [shards(): lax.all_to_all(reply, 'ex', split_axis=0, concat_axis=0, tiled=True)]
    ppermute x0 -> x23, waiting for transfers between devices: none -> 47.9 us  [the longest x6 24 us: shards(): lax.ppermute(arrived(h, asked[source]), 'ex', across)]
    ppermute x0 -> x23, starting transfers between devices: none -> 47 us  [the longest x6 29.9 us: shards(): below[s, h] = lax.ppermute(below[s - 1, h], 'ex', upward)]
    reduce_scatter x1 -> x0, waiting for transfers between devices: 20.9 us -> none  [shards(): lax.psum_scatter(scores * live[:, None, None], 'feat', scatter_dimension=...]
    all_to_all x1 -> x0, blocking collectives: 13.5 us -> none  [shards(): lax.all_to_all(wanted.reshape(peers, 1), 'ex', split_axis=0, concat_axis=...]
    pallas_call x0 -> x6, Pallas kernels: none -> 13.5 us  [block_scores(): pl.pallas_call(matmul_kernel, grid=(steps,), in_specs=in_specs, out_specs...]
    dot_general x1 -> x0, matrix products: 7.81 us -> none  [shards(): jnp.einsum('kaf,tf->kat', rows, train_grads, preferred_element_type=jnp.f...]
    gather x2 -> x1, local copies, waits for them, and re-layouts: 7.75 us -> 0.58 us  [shards(): tiles = jnp.take(scores, where, axis=0) * live[:, None, None]]
  transfers between devices with their start and end apart: 2 -> 23, of which waited for: 2 -> 11; matrix products, arithmetic and copies ran while one was open for 0% -> 6% of each run, Pallas kernels for 0% -> 8%
where the time goes in v1:
time: 139 us; the launch traced here: 138 us
  waiting for transfers between devices  47.9 us (34%)
  starting transfers between devices  47 us (34%)
  between operations  16.2 us (12%)
  Pallas kernels  13.5 us (10%)
  local copies, waits for them, and re-layouts  6.8 us (5%)
  other arithmetic  6.58 us (5%)
    ppermute x6, starting transfers between devices, shards(): below[s, h] = lax.ppermute(below[s - 1, h], 'ex', upward)  29.9 us
    ppermute x6, waiting for transfers between devices, shards(): lax.ppermute(arrived(h, asked[source]), 'ex', across)  24 us
    ppermute x6, waiting for transfers between devices, shards(): below[s, h] = lax.ppermute(below[s - 1, h], 'ex', upward)  14.8 us
    pallas_call x6, Pallas kernels, block_scores(): pl.pallas_call(matmul_kernel, grid=(steps,), in_specs=in_specs, out_specs...  13.5 us
    ppermute x6, starting transfers between devices, shards(): above[s, h] = lax.ppermute(above[s - 1, h], 'ex', downward)  7.72 us
    ppermute x6, starting transfers between devices, shards(): lax.ppermute(arrived(h, asked[source]), 'ex', across)  5.03 us
    select_n x2, other arithmetic, arrived(): jnp.where(jnp.logical_and(side, distance == d), block, result)  4.07 us
    ppermute x1, waiting for transfers between devices, shards(): lax.ppermute(send, 'feat', [(i, (i + 2 * k) % feats) for i in range(feats)])  4.02 us
  transfers between devices with their start and end apart: 23, of which 11 were waited for; matrix products, arithmetic and copies ran while one was open for 6% of the time, Pallas kernels for 8%

profile of v1, /device:TPU:0, one launch (start us, length us, event | category | flops | bytes accessed | tf_op | source)
XLA Modules:
  0.0 137.9 jit_solution(10501860018420954842)
XLA Ops:
  0.0 2.4 %fusion.6 = (bf16[2,32,4096]{2,1,0:T(8,128)(2,1)}, bf16[2,32,4096]{2,1,0:T(8,128)(2,1)}) fusion(bf16[2,32,8192]{2,1,0:T(8,128)(2,1)} %bitcast.87), kind=kLoop, calls=%fused_computation.56 | loop fusion | bytes 2097152 | tf_op jit(solution)/shard_map/slice | solution.py:79
  2.4 4.9 %collective-permute-start.3 = (bf16[2,32,4096]{2,1,0:T(8,128)(2,1)}, bf16[2,32,4096]{2,1,0:T(8,128)(2,1)S(1)}, u32[]{:S(2)}, u32[]{:S(2)}) collective-permute-start(bf16[2,32,4096]{2,1,0:T(8,128)(2,1)} %get-tuple-element.26), channel_id=1, source_target_pairs={{0,8},{4,12},{8,16},{12,20},{16,24},{20,28},{1,9},{5,13},{9,17},{1... | collective-permute-start | bytes 1572872 | tf_op jit(solution)/shard_map/ppermute | solution.py:82
  7.3 1.3 collective-permute-start.2
  8.6 4.6 %collective-permute-start.7 = (bf16[2,32,4096]{2,1,0:T(8,128)(2,1)}, bf16[2,32,4096]{2,1,0:T(8,128)(2,1)S(1)}, u32[]{:S(2)}, u32[]{:S(2)}) collective-permute-start(bf16[2,32,4096]{2,1,0:T(8,128)(2,1)} %get-tuple-element.25), channel_id=1, source_target_pairs={{0,8},{4,12},{8,16},{12,20},{16,24},{20,28},{1,9},{5,13},{9,17},{1... | collective-permute-start | bytes 1572872 | tf_op jit(solution)/shard_map/ppermute | solution.py:82
  13.2 1.3 collective-permute-start.6
  15.4 1.5 %collective-permute-start = (s32[8]{0:T(128)S(1)}, s32[8]{0:T(128)S(1)}, u32[]{:S(2)}, u32[]{:S(2)}) collective-permute-start(s32[8]{0:T(128)S(1)} %select_reduce_fusion), channel_id=1, source_target_pairs={{0,4},{4,0},{8,12},{12,8},{16,20},{20,16},{24,28},{28,24},{1,5},{5... | collective-permute-start | bytes 104 | tf_op jit(solution)/shard_map/ppermute | solution.py:75
  28.9 4.6 %collective-permute-start.10 = (bf16[2,32,4096]{2,1,0:T(8,128)(2,1)S(1)}, bf16[2,32,4096]{2,1,0:T(8,128)(2,1)S(1)}, u32[]{:S(2)}, u32[]{:S(2)}) collective-permute-start(bf16[2,32,4096]{2,1,0:T(8,128)(2,1)S(1)} %collective-permute-done.3), channel_id=1, source_target_pairs={{0,8},{4,12},{8,16},{12,20},{16,24},{20,28},{1,9},{5,13},{9,17},{1... | collective-permute-start | bytes 1572872 | tf_op jit(solution)/shard_map/ppermute | solution.py:82
  33.5 1.3 collective-permute-start.9
  34.8 5.4 %collective-permute-start.13 = (bf16[2,32,4096]{2,1,0:T(8,128)(2,1)S(1)}, bf16[2,32,4096]{2,1,0:T(8,128)(2,1)}, u32[]{:S(2)}, u32[]{:S(2)}) collective-permute-start(bf16[2,32,4096]{2,1,0:T(8,128)(2,1)S(1)} %collective-permute-done.7), channel_id=1, source_target_pairs={{0,8},{4,12},{8,16},{12,20},{16,24},{20,28},{1,9},{5,13},{9,17},{1... | collective-permute-start | bytes 1572872 | tf_op jit(solution)/shard_map/ppermute | solution.py:82
  42.8 3.0 %collective-permute-done.10 = bf16[2,32,4096]{2,1,0:T(8,128)(2,1)S(1)} collective-permute-done((bf16[2,32,4096]{2,1,0:T(8,128)(2,1)S(1)}, bf16[2,32,4096]{2,1,0:T(8,128)(2,1)S(1)}, u32[]{:S(2)}, u32[]{:S(2)}) %collective-permute-start.10) | collective-permute-done | bytes 524320 | tf_op jit(solution)/shard_map/ppermute | solution.py:82
  45.8 5.2 %collective-permute-start.16 = (bf16[2,32,4096]{2,1,0:T(8,128)(2,1)S(1)}, bf16[2,32,4096]{2,1,0:T(8,128)(2,1)}, u32[]{:S(2)}, u32[]{:S(2)}) collective-permute-start(bf16[2,32,4096]{2,1,0:T(8,128)(2,1)S(1)} %collective-permute-done.10), channel_id=1, source_target_pairs={{0,8},{4,12},{8,16},{12,20},{16,24},{20,28},{1,9},{5,13},{9,17},{1... | collective-permute-start | bytes 1572872 | tf_op jit(solution)/shard_map/ppermute | solution.py:82
  52.3 4.8 %collective-permute-done.13 = bf16[2,32,4096]{2,1,0:T(8,128)(2,1)} collective-permute-done((bf16[2,32,4096]{2,1,0:T(8,128)(2,1)S(1)}, bf16[2,32,4096]{2,1,0:T(8,128)(2,1)}, u32[]{:S(2)}, u32[]{:S(2)}) %collective-permute-start.13) | collective-permute-done | bytes 524320 | tf_op jit(solution)/shard_map/ppermute | solution.py:82
  57.0 5.3 %collective-permute-start.19 = (bf16[2,32,4096]{2,1,0:T(8,128)(2,1)}, bf16[2,32,4096]{2,1,0:T(8,128)(2,1)}, u32[]{:S(2)}, u32[]{:S(2)}) collective-permute-start(bf16[2,32,4096]{2,1,0:T(8,128)(2,1)} %collective-permute-done.13), channel_id=1, source_target_pairs={{0,8},{4,12},{8,16},{12,20},{16,24},{20,28},{1,9},{5,13},{9,17},{1... | collective-permute-start | bytes 1572872 | tf_op jit(solution)/shard_map/ppermute | solution.py:82
  70.1 7.0 %collective-permute-done.19 = bf16[2,32,4096]{2,1,0:T(8,128)(2,1)} collective-permute-done((bf16[2,32,4096]{2,1,0:T(8,128)(2,1)}, bf16[2,32,4096]{2,1,0:T(8,128)(2,1)}, u32[]{:S(2)}, u32[]{:S(2)}) %collective-permute-start.19) | collective-permute-done | bytes 524320 | tf_op jit(solution)/shard_map/ppermute | solution.py:82
  77.6 3.6 %collective-permute-done.18 = bf16[2,32,4096]{2,1,0:T(8,128)(2,1)} collective-permute-done((bf16[2,32,4096]{2,1,0:T(8,128)(2,1)}, bf16[2,32,4096]{2,1,0:T(8,128)(2,1)}, u32[]{:S(2)}, u32[]{:S(2)}) %collective-permute-start.18) | collective-permute-done | bytes 524320 | tf_op jit(solution)/shard_map/ppermute | solution.py:83
  81.2 2.3 %select_bitcast_fusion.5 = (bf16[32,4096]{1,0:T(8,128)(2,1)S(1)}, bf16[32,4096]{1,0:T(8,128)(2,1)S(1)}, bf16[32,4096]{1,0:T(8,128)(2,1)S(1)}, bf16[32,4096]{1,0:...) fusion(bf16[2,32,4096]{2,1,0:T(8,128)(2,1)S(1)} %collective-permute-done.7, ...), kind=kLoop, calls=%fused_computation.19 | loop fusion | flops 1835008 | bytes 6815775 | tf_op jit(solution)/shard_map/jit(_where)/select_n | solution.py:109
  84.1 1.7 %select_bitcast_fusion.7 = (bf16[32,4096]{1,0:T(8,128)(2,1)S(1)}, bf16[32,4096]{1,0:T(8,128)(2,1)S(1)}, bf16[32,4096]{1,0:T(8,128)(2,1)S(1)}, bf16[32,4096]{1,0:...) fusion(bf16[2,32,4096]{2,1,0:T(8,128)(2,1)S(1)} %collective-permute-done.3, ...), kind=kLoop, calls=%fused_computation.21 | loop fusion | flops 1835008 | bytes 6815775 | tf_op jit(solution)/shard_map/jit(_where)/select_n | solution.py:109
  85.9 1.3 collective-permute-start.17
  89.2 3.6 %collective-permute-done.8 = bf16[32,4096]{1,0:T(8,128)(2,1)S(1)} collective-permute-done((bf16[32,4096]{1,0:T(8,128)(2,1)S(1)}, bf16[32,4096]{1,0:T(8,128)(2,1)S(1)}, u32[]{:S(2)}, u32[]{:S(2)}) %collective-permute-start.8) | collective-permute-done | bytes 262176 | tf_op jit(solution)/shard_map/ppermute | solution.py:114
  93.5 5.0 %collective-permute-done.17 = bf16[32,4096]{1,0:T(8,128)(2,1)S(1)} collective-permute-done((bf16[32,4096]{1,0:T(8,128)(2,1)S(1)}, bf16[32,4096]{1,0:T(8,128)(2,1)S(1)}, u32[]{:S(2)}, u32[]{:S(2)}) %collective-permute-start.17) | collective-permute-done | bytes 262176 | tf_op jit(solution)/shard_map/ppermute | solution.py:114
  99.0 5.0 %collective-permute-done.20 = bf16[32,4096]{1,0:T(8,128)(2,1)S(1)} collective-permute-done((bf16[32,4096]{1,0:T(8,128)(2,1)S(1)}, bf16[32,4096]{1,0:T(8,128)(2,1)S(1)}, u32[]{:S(2)}, u32[]{:S(2)}) %collective-permute-start.20) | collective-permute-done | bytes 262176 | tf_op jit(solution)/shard_map/ppermute | solution.py:114
  104.1 5.6 %collective-permute-done.11 = bf16[32,4096]{1,0:T(8,128)(2,1)S(1)} collective-permute-done((bf16[32,4096]{1,0:T(8,128)(2,1)S(1)}, bf16[32,4096]{1,0:T(8,128)(2,1)S(1)}, u32[]{:S(2)}, u32[]{:S(2)}) %collective-permute-start.11) | collective-permute-done | bytes 262176 | tf_op jit(solution)/shard_map/ppermute | solution.py:114
  109.7 4.8 %collective-permute-done.14 = bf16[32,4096]{1,0:T(8,128)(2,1)S(1)} collective-permute-done((bf16[32,4096]{1,0:T(8,128)(2,1)S(1)}, bf16[32,4096]{1,0:T(8,128)(2,1)S(1)}, u32[]{:S(2)}, u32[]{:S(2)}) %collective-permute-start.14) | collective-permute-done | bytes 262176 | tf_op jit(solution)/shard_map/ppermute | solution.py:114
  114.6 2.2 %shard_map.59.rest_0_ = f32[64,512]{1,0:T(8,128)S(1)} custom-call(bf16[64,4096]{1,0:T(8,128)(2,1)S(1)} %pad_maximum_fusion.5.rows_ref, bf16[512,8192]{1,0:T(8,128)(2,1)S(1)} %bitcast.83), custom_call_target="tpu_custom_call" | custom-call | flops 268435456 | bytes 4849664 | tf_op jit(solution)/shard_map/pallas_call | solution.py:40
  116.7 2.2 %shard_map.57.rest_0_ = f32[64,512]{1,0:T(8,128)S(1)} custom-call(bf16[64,4096]{1,0:T(8,128)(2,1)S(1)} %pad_maximum_fusion.3.rows_ref, bf16[512,8192]{1,0:T(8,128)(2,1)S(1)} %bitcast.83), custom_call_target="tpu_custom_call" | custom-call | flops 268435456 | bytes 4849664 | tf_op jit(solution)/shard_map/pallas_call | solution.py:40
  118.9 2.2 %shard_map.60 = f32[64,512]{1,0:T(8,128)S(1)} custom-call(bf16[64,4096]{1,0:T(8,128)(2,1)S(1)} %pad_maximum_fusion.4.rows_ref, bf16[512,8192]{1,0:T(8,128)(2,1)S(1)} %bitcast.83, f32[64,512]{1,0:T(8,128)S(1)} %shard_map.59.rest_0_), custom_call_target="tpu_custom_call" | custom-call | flops 268435456 | bytes 4849664 | tf_op jit(solution)/shard_map/pallas_call | solution.py:40
  121.1 2.2 %shard_map.58 = f32[64,512]{1,0:T(8,128)S(1)} custom-call(bf16[64,4096]{1,0:T(8,128)(2,1)S(1)} %pad_maximum_fusion.2.rows_ref, bf16[512,8192]{1,0:T(8,128)(2,1)S(1)} %bitcast.83, f32[64,512]{1,0:T(8,128)S(1)} %shard_map.57.rest_0_), custom_call_target="tpu_custom_call" | custom-call | flops 268435456 | bytes 4849664 | tf_op jit(solution)/shard_map/pallas_call | solution.py:40
  123.3 2.4 %shard_map.55.rest_0_ = f32[128,512]{1,0:T(8,128)S(1)} custom-call(bf16[128,4096]{1,0:T(8,128)(2,1)S(1)} %pad_maximum_fusion.1.rows_ref, bf16[512,8192]{1,0:T(8,128)(2,1)S(1)} %bitcast.83), custom_call_target="tpu_custom_call" | custom-call | flops 536870912 | bytes 5505024 | tf_op jit(solution)/shard_map/pallas_call | solution.py:40
  126.7 2.4 %shard_map.56 = f32[128,512]{1,0:T(8,128)S(1)} custom-call(bf16[128,4096]{1,0:T(8,128)(2,1)S(1)} %pad_maximum_fusion.rows_ref, bf16[512,8192]{1,0:T(8,128)(2,1)S(1)} %bitcast.83, f32[128,512]{1,0:T(8,128)S(1)} %shard_map.55.rest_0_), custom_call_target="tpu_custom_call" | custom-call | flops 536870912 | bytes 5505024 | tf_op jit(solution)/shard_map/pallas_call | solution.py:40
  130.1 1.5 %collective-permute-done.21 = f32[2,2,32,512]{3,2,1,0:T(8,128)S(1)} collective-permute-done((f32[2,2,32,512]{3,2,1,0:T(8,128)S(1)}, f32[2,2,32,512]{3,2,1,0:T(8,128)S(1)}, u32[]{:S(2)}, u32[]{:S(2)}) %collective-permute-start.21) | collective-permute-done | bytes 262176 | tf_op jit(solution)/shard_map/ppermute | solution.py:138
  131.6 1.6 %collective-permute-start.22 = (f32[2,32,512]{2,1,0:T(8,128)S(1)}, f32[2,32,512]{2,1,0:T(8,128)S(1)}, u32[]{:S(2)}, u32[]{:S(2)}) collective-permute-start(f32[2,32,512]{2,1,0:T(8,128)S(1)} %dynamic-slice_bitcast_fusion.3), channel_id=1, source_target_pairs={{0,2},{1,3},{2,0},{3,1},{4,6},{5,7},{6,4},{7,5},{8,10},{9,11},{10,... | collective-permute-start | bytes 393224 | tf_op jit(solution)/shard_map/ppermute | solution.py:145
  133.2 4.0 %collective-permute-done.22 = f32[2,32,512]{2,1,0:T(8,128)S(1)} collective-permute-done((f32[2,32,512]{2,1,0:T(8,128)S(1)}, f32[2,32,512]{2,1,0:T(8,128)S(1)}, u32[]{:S(2)}, u32[]{:S(2)}) %collective-permute-start.22) | collective-permute-done | bytes 131104 | tf_op jit(solution)/shard_map/ppermute | solution.py:145
  (67 shorter events, 15.6 us)
Async XLA Ops:
  0.0 14.6 %copy-start = (s32[16]{0:T(128)S(1)}, s32[16]{0:T(128)}, u32[]{:S(2)}) copy-start(s32[16]{0:T(128)} %param.7) | copy-start | bytes 196
  0.0 28.8 %copy-start.1 = (bf16[2,1,32,8192]{3,2,1,0:T(8,128)(2,1)S(1)}, bf16[2,1,32,8192]{3,2,1,0:T(8,128)(2,1)}, u32[]{:S(2)}) copy-start(bf16[2,1,32,8192]{3,2,1,0:T(8,128)(2,1)} %param.6) | copy-start | bytes 3145732
  0.0 14.5 %copy-start.3 = (s32[1,8]{1,0:T(1,128)S(1)}, s32[1,8]{1,0:T(1,128)}, u32[]{:S(2)}) copy-start(s32[1,8]{1,0:T(1,128)} %param.8) | copy-start | bytes 100
  2.4 26.5 %collective-permute-start.3 = (bf16[2,32,4096]{2,1,0:T(8,128)(2,1)}, bf16[2,32,4096]{2,1,0:T(8,128)(2,1)S(1)}, u32[]{:S(2)}, u32[]{:S(2)}) collective-permute-start(bf16[2,32,4096]{2,1,0:T(8,128)(2,1)} %get-tuple-element.26), channel_id=1, source_target_pairs={{0,8},{4,12},{8,16},{12,20},{16,24},{20,28},{1,9},{5,13},{9,17},{1... | collective-permute-start | bytes 1572872 | tf_op jit(solution)/shard_map/ppermute | solution.py:82
  7.3 26.1 %collective-permute-start.2 = (bf16[2,32,4096]{2,1,0:T(8,128)(2,1)}, bf16[2,32,4096]{2,1,0:T(8,128)(2,1)S(1)}, u32[]{:S(2)}, u32[]{:S(2)}) collective-permute-start(bf16[2,32,4096]{2,1,0:T(8,128)(2,1)} %get-tuple-element.26), channel_id=1, source_target_pairs={{8,0},{12,4},{16,8},{20,12},{24,16},{28,20},{9,1},{13,5},{17,9},{2... | collective-permute-start | bytes 1572872 | tf_op jit(solution)/shard_map/ppermute | solution.py:83
  8.6 26.2 %collective-permute-start.7 = (bf16[2,32,4096]{2,1,0:T(8,128)(2,1)}, bf16[2,32,4096]{2,1,0:T(8,128)(2,1)S(1)}, u32[]{:S(2)}, u32[]{:S(2)}) collective-permute-start(bf16[2,32,4096]{2,1,0:T(8,128)(2,1)} %get-tuple-element.25), channel_id=1, source_target_pairs={{0,8},{4,12},{8,16},{12,20},{16,24},{20,28},{1,9},{5,13},{9,17},{1... | collective-permute-start | bytes 1572872 | tf_op jit(solution)/shard_map/ppermute | solution.py:82
  13.2 26.9 %collective-permute-start.6 = (bf16[2,32,4096]{2,1,0:T(8,128)(2,1)}, bf16[2,32,4096]{2,1,0:T(8,128)(2,1)S(1)}, u32[]{:S(2)}, u32[]{:S(2)}) collective-permute-start(bf16[2,32,4096]{2,1,0:T(8,128)(2,1)} %get-tuple-element.25), channel_id=1, source_target_pairs={{8,0},{12,4},{16,8},{20,12},{24,16},{28,20},{9,1},{13,5},{17,9},{2... | collective-permute-start | bytes 1572872 | tf_op jit(solution)/shard_map/ppermute | solution.py:83
  15.4 10.8 %collective-permute-start = (s32[8]{0:T(128)S(1)}, s32[8]{0:T(128)S(1)}, u32[]{:S(2)}, u32[]{:S(2)}) collective-permute-start(s32[8]{0:T(128)S(1)} %select_reduce_fusion), channel_id=1, source_target_pairs={{0,4},{4,0},{8,12},{12,8},{16,20},{20,16},{24,28},{28,24},{1,5},{5... | collective-permute-start | bytes 104 | tf_op jit(solution)/shard_map/ppermute | solution.py:75
  28.9 16.9 %collective-permute-start.10 = (bf16[2,32,4096]{2,1,0:T(8,128)(2,1)S(1)}, bf16[2,32,4096]{2,1,0:T(8,128)(2,1)S(1)}, u32[]{:S(2)}, u32[]{:S(2)}) collective-permute-start(bf16[2,32,4096]{2,1,0:T(8,128)(2,1)S(1)} %collective-permute-done.3), channel_id=1, source_target_pairs={{0,8},{4,12},{8,16},{12,20},{16,24},{20,28},{1,9},{5,13},{9,17},{1... | collective-permute-start | bytes 1572872 | tf_op jit(solution)/shard_map/ppermute | solution.py:82
  33.5 17.5 %collective-permute-start.9 = (bf16[2,32,4096]{2,1,0:T(8,128)(2,1)S(1)}, bf16[2,32,4096]{2,1,0:T(8,128)(2,1)S(1)}, u32[]{:S(2)}, u32[]{:S(2)}) collective-permute-start(bf16[2,32,4096]{2,1,0:T(8,128)(2,1)S(1)} %collective-permute-done.2), channel_id=1, source_target_pairs={{8,0},{12,4},{16,8},{20,12},{24,16},{28,20},{9,1},{13,5},{17,9},{2... | collective-permute-start | bytes 1572872 | tf_op jit(solution)/shard_map/ppermute | solution.py:83
  34.8 22.2 %collective-permute-start.13 = (bf16[2,32,4096]{2,1,0:T(8,128)(2,1)S(1)}, bf16[2,32,4096]{2,1,0:T(8,128)(2,1)}, u32[]{:S(2)}, u32[]{:S(2)}) collective-permute-start(bf16[2,32,4096]{2,1,0:T(8,128)(2,1)S(1)} %collective-permute-done.7), channel_id=1, source_target_pairs={{0,8},{4,12},{8,16},{12,20},{16,24},{20,28},{1,9},{5,13},{9,17},{1... | collective-permute-start | bytes 1572872 | tf_op jit(solution)/shard_map/ppermute | solution.py:82
  40.2 22.2 %collective-permute-start.12 = (bf16[2,32,4096]{2,1,0:T(8,128)(2,1)S(1)}, bf16[2,32,4096]{2,1,0:T(8,128)(2,1)}, u32[]{:S(2)}, u32[]{:S(2)}) collective-permute-start(bf16[2,32,4096]{2,1,0:T(8,128)(2,1)S(1)} %collective-permute-done.6), channel_id=1, source_target_pairs={{8,0},{12,4},{16,8},{20,12},{24,16},{28,20},{9,1},{13,5},{17,9},{2... | collective-permute-start | bytes 1572872 | tf_op jit(solution)/shard_map/ppermute | solution.py:83
  42.3 83.4 %collective-permute-start.1 = (bf16[32,4096]{1,0:T(8,128)(2,1)}, bf16[32,4096]{1,0:T(8,128)(2,1)}, u32[]{:S(2)}, u32[]{:S(2)}) collective-permute-start(bf16[32,4096]{1,0:T(8,128)(2,1)} %get-tuple-element.30), channel_id=1, source_target_pairs={{0,4},{4,0},{8,12},{12,8},{16,20},{20,16},{24,28},{28,24},{1,5},{5... | collective-permute-start | bytes 786440 | tf_op jit(solution)/shard_map/ppermute | solution.py:96
  45.8 38.3 %collective-permute-start.16 = (bf16[2,32,4096]{2,1,0:T(8,128)(2,1)S(1)}, bf16[2,32,4096]{2,1,0:T(8,128)(2,1)}, u32[]{:S(2)}, u32[]{:S(2)}) collective-permute-start(bf16[2,32,4096]{2,1,0:T(8,128)(2,1)S(1)} %collective-permute-done.10), channel_id=1, source_target_pairs={{0,8},{4,12},{8,16},{12,20},{16,24},{20,28},{1,9},{5,13},{9,17},{1... | collective-permute-start | bytes 1572872 | tf_op jit(solution)/shard_map/ppermute | solution.py:82
  51.0 33.2 %collective-permute-start.15 = (bf16[2,32,4096]{2,1,0:T(8,128)(2,1)S(1)}, bf16[2,32,4096]{2,1,0:T(8,128)(2,1)}, u32[]{:S(2)}, u32[]{:S(2)}) collective-permute-start(bf16[2,32,4096]{2,1,0:T(8,128)(2,1)S(1)} %collective-permute-done.9), channel_id=1, source_target_pairs={{8,0},{12,4},{16,8},{20,12},{24,16},{28,20},{9,1},{13,5},{17,9},{2... | collective-permute-start | bytes 1572872 | tf_op jit(solution)/shard_map/ppermute | solution.py:83
  57.0 20.0 %collective-permute-start.19 = (bf16[2,32,4096]{2,1,0:T(8,128)(2,1)}, bf16[2,32,4096]{2,1,0:T(8,128)(2,1)}, u32[]{:S(2)}, u32[]{:S(2)}) collective-permute-start(bf16[2,32,4096]{2,1,0:T(8,128)(2,1)} %collective-permute-done.13), channel_id=1, source_target_pairs={{0,8},{4,12},{8,16},{12,20},{16,24},{20,28},{1,9},{5,13},{9,17},{1... | collective-permute-start | bytes 1572872 | tf_op jit(solution)/shard_map/ppermute | solution.py:82
  62.3 18.8 %collective-permute-start.18 = (bf16[2,32,4096]{2,1,0:T(8,128)(2,1)}, bf16[2,32,4096]{2,1,0:T(8,128)(2,1)}, u32[]{:S(2)}, u32[]{:S(2)}) collective-permute-start(bf16[2,32,4096]{2,1,0:T(8,128)(2,1)} %collective-permute-done.12), channel_id=1, source_target_pairs={{8,0},{12,4},{16,8},{20,12},{24,16},{28,20},{9,1},{13,5},{17,9},{2... | collective-permute-start | bytes 1572872 | tf_op jit(solution)/shard_map/ppermute | solution.py:83
  77.0 11.0 %collective-permute-start.5 = (bf16[32,4096]{1,0:T(8,128)(2,1)}, bf16[32,4096]{1,0:T(8,128)(2,1)S(1)}, u32[]{:S(2)}, u32[]{:S(2)}) collective-permute-start(bf16[32,4096]{1,0:T(8,128)(2,1)} %get-tuple-element.29), channel_id=1, source_target_pairs={{0,4},{4,0},{8,12},{12,8},{16,20},{20,16},{24,28},{28,24},{1,5},{5... | collective-permute-start | bytes 786440 | tf_op jit(solution)/shard_map/ppermute | solution.py:96
  81.2 33.4 %slice-start = ((s8[8388608]{0:T(1024)(128)(4,1)}), s8[4194304]{0:T(1024)(128)(4,1)S(1)}, s32[]{:S(2)}) async-start(s8[8388608]{0:T(1024)(128)(4,1)} %bitcast.82), calls=%async_computation | async-start | bytes 8388608
  83.5 9.9 %copy-start.2 = (bf16[32,4096]{1,0:T(8,128)(2,1)S(1)}, bf16[32,4096]{1,0:T(8,128)(2,1)}, u32[]{:S(2)}) copy-start(bf16[32,4096]{1,0:T(8,128)(2,1)} %get-tuple-element.27) | copy-start | bytes 786436
  83.5 31.0 %slice-start.1 = ((s8[8388608]{0:T(1024)(128)(4,1)}), s8[4194304]{0:T(1024)(128)(4,1)S(1)}, s32[]{:S(2)}) async-start(s8[8388608]{0:T(1024)(128)(4,1)} %bitcast.82), calls=%async_computation.1 | async-start | bytes 8388608
  83.5 9.3 %collective-permute-start.8 = (bf16[32,4096]{1,0:T(8,128)(2,1)S(1)}, bf16[32,4096]{1,0:T(8,128)(2,1)S(1)}, u32[]{:S(2)}, u32[]{:S(2)}) collective-permute-start(bf16[32,4096]{1,0:T(8,128)(2,1)S(1)} %get-tuple-element.18), channel_id=1, source_target_pairs={{0,4},{4,0},{8,12},{12,8},{16,20},{20,16},{24,28},{28,24},{1,5},{5... | collective-permute-start | bytes 786440 | tf_op jit(solution)/shard_map/ppermute | solution.py:114
  85.9 12.6 %collective-permute-start.17 = (bf16[32,4096]{1,0:T(8,128)(2,1)S(1)}, bf16[32,4096]{1,0:T(8,128)(2,1)S(1)}, u32[]{:S(2)}, u32[]{:S(2)}) collective-permute-start(bf16[32,4096]{1,0:T(8,128)(2,1)S(1)} %get-tuple-element.22), channel_id=1, source_target_pairs={{0,4},{4,0},{8,12},{12,8},{16,20},{20,16},{24,28},{28,24},{1,5},{5... | collective-permute-start | bytes 786440 | tf_op jit(solution)/shard_map/ppermute | solution.py:114
  87.2 16.9 %collective-permute-start.20 = (bf16[32,4096]{1,0:T(8,128)(2,1)S(1)}, bf16[32,4096]{1,0:T(8,128)(2,1)S(1)}, u32[]{:S(2)}, u32[]{:S(2)}) collective-permute-start(bf16[32,4096]{1,0:T(8,128)(2,1)S(1)} %get-tuple-element.16), channel_id=1, source_target_pairs={{0,4},{4,0},{8,12},{12,8},{16,20},{20,16},{24,28},{28,24},{1,5},{5... | collective-permute-start | bytes 786440 | tf_op jit(solution)/shard_map/ppermute | solution.py:114
  88.0 21.7 %collective-permute-start.11 = (bf16[32,4096]{1,0:T(8,128)(2,1)S(1)}, bf16[32,4096]{1,0:T(8,128)(2,1)S(1)}, u32[]{:S(2)}, u32[]{:S(2)}) collective-permute-start(bf16[32,4096]{1,0:T(8,128)(2,1)S(1)} %get-tuple-element.10), channel_id=1, source_target_pairs={{0,4},{4,0},{8,12},{12,8},{16,20},{20,16},{24,28},{28,24},{1,5},{5... | collective-permute-start | bytes 786440 | tf_op jit(solution)/shard_map/ppermute | solution.py:114
  92.8 21.7 %collective-permute-start.14 = (bf16[32,4096]{1,0:T(8,128)(2,1)S(1)}, bf16[32,4096]{1,0:T(8,128)(2,1)S(1)}, u32[]{:S(2)}, u32[]{:S(2)}) collective-permute-start(bf16[32,4096]{1,0:T(8,128)(2,1)S(1)} %get-tuple-element.8), channel_id=1, source_target_pairs={{0,4},{4,0},{8,12},{12,8},{16,20},{20,16},{24,28},{28,24},{1,5},{5... | collective-permute-start | bytes 786440 | tf_op jit(solution)/shard_map/ppermute | solution.py:114
  98.5 27.2 %collective-permute-start.4 = (bf16[32,4096]{1,0:T(8,128)(2,1)S(1)}, bf16[32,4096]{1,0:T(8,128)(2,1)S(1)}, u32[]{:S(2)}, u32[]{:S(2)}) collective-permute-start(bf16[32,4096]{1,0:T(8,128)(2,1)S(1)} %get-tuple-element.24), channel_id=1, source_target_pairs={{0,4},{4,0},{8,12},{12,8},{16,20},{20,16},{24,28},{28,24},{1,5},{5... | collective-permute-start | bytes 786440 | tf_op jit(solution)/shard_map/ppermute | solution.py:114
  129.9 1.6 %collective-permute-start.21 = (f32[2,2,32,512]{3,2,1,0:T(8,128)S(1)}, f32[2,2,32,512]{3,2,1,0:T(8,128)S(1)}, u32[]{:S(2)}, u32[]{:S(2)}) collective-permute-start(f32[2,2,32,512]{3,2,1,0:T(8,128)S(1)} %dynamic-slice_bitcast_fusion.2), channel_id=1, source_target_pairs={{0,1},{1,0},{2,3},{3,2},{4,5},{5,4},{6,7},{7,6},{8,9},{9,8},{10,11... | collective-permute-start | bytes 786440 | tf_op jit(solution)/shard_map/ppermute | solution.py:138
  131.6 5.6 %collective-permute-start.22 = (f32[2,32,512]{2,1,0:T(8,128)S(1)}, f32[2,32,512]{2,1,0:T(8,128)S(1)}, u32[]{:S(2)}, u32[]{:S(2)}) collective-permute-start(f32[2,32,512]{2,1,0:T(8,128)S(1)} %dynamic-slice_bitcast_fusion.3), channel_id=1, source_target_pairs={{0,2},{1,3},{2,0},{3,1},{4,6},{5,7},{6,4},{7,5},{8,10},{9,11},{10,... | collective-permute-start | bytes 393224 | tf_op jit(solution)/shard_map/ppermute | solution.py:145

commit v2 on v0

v2 whole, which is shorter than its diff:
```python
import functools

import jax
import jax.numpy as jnp
from jax import lax
from jax.experimental import pallas as pl
from jax.experimental.pallas import tpu as pltpu
from jax.sharding import PartitionSpec as P

PAIR = 2
PARTS = 2
STEP = 1024
SMALL_LIMIT = 8 * 2**20
VMEM_LIMIT = 48 * 2**20
COST = pl.CostEstimate(flops=10**9, bytes_accessed=8 * 2**20, transcendentals=0)
SMEM = pl.BlockSpec(memory_space=pltpu.SMEM)
VMEM = pl.BlockSpec(memory_space=pltpu.VMEM)
ANY = pl.BlockSpec(memory_space=pl.ANY)


def slots_of(chain):
    first = [(d, False) for d in range(1, chain - 1)]
    return [(0, False)] + first + [(d, True) for d in range((chain - 1) // 2, 0, -1)]


def plan_kernel(peers, me_ref, owner_ref, pairs_ref, counts_ref, wanted_ref, rows_ref):
    chain = peers // PAIR
    slots = len(slots_of(chain))
    me = me_ref[0]
    place, column = me // PAIR, lax.rem(me, PAIR)
    for k in range(peers):
        stored = owner_ref[pairs_ref[0, k]]
        holder = lax.rem(stored, peers)
        wanted_ref[holder] = stored // peers
        there = holder // PAIR
        far = jnp.abs(there - place)
        second = jnp.logical_and(there > place, place >= far)
        slot = jnp.where(far == chain - 1, slots - 1, jnp.where(second, slots - far, far))
        row = slot * PAIR + (lax.rem(holder, PAIR) != column).astype(jnp.int32)
        rows_ref[k] = jnp.where(k < counts_ref[0], row, -1)


def plan(me, owner_map, pair_blocks, pair_counts, peers):
    shape = jax.ShapeDtypeStruct((peers,), jnp.int32)
    return pl.pallas_call(
        functools.partial(plan_kernel, peers), in_specs=[SMEM] * 4, out_specs=[SMEM] * 2, out_shape=[shape] * 2
    )(me, owner_map, pair_blocks, pair_counts)


def relay_kernel(d, sides, me_ref, wanted_ref, asked_ref, *refs):
    sources, (mine_ref, theirs_ref, sems) = refs[: len(sides) * PARTS], refs[len(sides) * PARTS :]
    me = me_ref[0]
    place, column = me // PAIR, lax.rem(me, PAIR)
    for i, side in enumerate(sides):
        source = (place + side * d) * PAIR + column

        @pl.when((place >= d) == (side < 0))
        def _():
            copies = []
            for h in range(PARTS):
                ref = sources[i * PARTS + h]
                copies += [
                    pltpu.make_async_copy(ref.at[asked_ref[source]], theirs_ref.at[h], sems.at[2 * h]),
                    pltpu.make_async_copy(ref.at[wanted_ref[source]], mine_ref.at[h], sems.at[2 * h + 1]),
                ]
            for copy in copies:
                copy.start()
            for copy in copies:
                copy.wait()


def second_kernel(chain, d, me_ref, wanted_ref, asked_ref, *refs):
    sources, (mine_ref, theirs_ref, sems) = refs[:PARTS], refs[PARTS:]
    me = me_ref[0]
    source = jnp.minimum(me + d * PAIR, chain * PAIR - 1)
    copies = []
    for h, ref in enumerate(sources):
        copies += [
            pltpu.make_async_copy(ref.at[asked_ref[source]], theirs_ref.at[h], sems.at[2 * h]),
            pltpu.make_async_copy(ref.at[wanted_ref[source]], mine_ref.at[h], sems.at[2 * h + 1]),
        ]
    for copy in copies:
        copy.start()
    for copy in copies:
        copy.wait()


def relay(me, wanted, asked, above, below, d, second, chain):
    parts = range(PARTS)
    if second:
        kernel = functools.partial(second_kernel, chain, d)
        blocks = [above[d, h] for h in parts]
    else:
        kernel = functools.partial(relay_kernel, d, (-1, 1))
        blocks = [below[d, h] for h in parts] + [above[d, h] for h in parts]
    shape = jax.ShapeDtypeStruct((PARTS,) + blocks[0].shape[1:], blocks[0].dtype)
    return pl.pallas_call(
        kernel,
        in_specs=[SMEM] * 3 + [ANY] * len(blocks),
        out_specs=[VMEM] * 2,
        out_shape=[shape] * 2,
        scratch_shapes=[pltpu.SemaphoreType.DMA((2 * PARTS,))],
        cost_estimate=COST,
        compiler_params=pltpu.CompilerParams(vmem_limit_bytes=SMALL_LIMIT),
    )(me, wanted, asked, *blocks)


def own_kernel(me_ref, wanted_ref, asked_ref, own_ref, mine_ref, theirs_ref, sems):
    me = me_ref[0]
    width = mine_ref.shape[-1]
    copies = []
    for h in range(PARTS):
        at = slice(h * width, (h + 1) * width)
        copies += [
            pltpu.make_async_copy(own_ref.at[asked_ref[me], :, at], theirs_ref.at[h], sems.at[2 * h]),
            pltpu.make_async_copy(own_ref.at[wanted_ref[me], :, at], mine_ref.at[h], sems.at[2 * h + 1]),
        ]
    for copy in copies:
        copy.start()
    for copy in copies:
        copy.wait()


def relay_own(me, wanted, asked, own):
    shape = jax.ShapeDtypeStruct((PARTS, own.shape[1], own.shape[2] // PARTS), own.dtype)
    return pl.pallas_call(
        own_kernel,
        in_specs=[SMEM] * 3 + [ANY],
        out_specs=[VMEM] * 2,
        out_shape=[shape] * 2,
        scratch_shapes=[pltpu.SemaphoreType.DMA((2 * PARTS,))],
        cost_estimate=COST,
        compiler_params=pltpu.CompilerParams(vmem_limit_bytes=SMALL_LIMIT),
    )(me, wanted, asked, own)


def hand_kernel(chain, me_ref, notes_ref, above_ref, below_ref, out_ref, sems):
    me = me_ref[0]
    place, column = me // PAIR, lax.rem(me, PAIR)
    for ref, source in ((above_ref, (chain - 1) * PAIR + column), (below_ref, column)):

        @pl.when((place < chain // 2) == (source is not column))
        def _():
            copies = [
                pltpu.make_async_copy(ref.at[notes_ref[i, source]], out_ref.at[i], sems.at[i]) for i in range(PAIR)
            ]
            for copy in copies:
                copy.start()
            for copy in copies:
                copy.wait()


def hand(me, notes, above, below, chain):
    return pl.pallas_call(
        functools.partial(hand_kernel, chain),
        in_specs=[SMEM] * 2 + [ANY] * 2,
        out_specs=VMEM,
        out_shape=jax.ShapeDtypeStruct((PAIR,) + above.shape[1:], above.dtype),
        scratch_shapes=[pltpu.SemaphoreType.DMA((PAIR,))],
        cost_estimate=COST,
        compiler_params=pltpu.CompilerParams(vmem_limit_bytes=SMALL_LIMIT),
    )(me, notes, above, below)


def contract(rows, train):
    return lax.dot_general(rows, train, (((1,), (1,)), ((), ())), preferred_element_type=jnp.float32)


def scores_kernel(peers, feats, count, me_ref, rows_ref, *refs):
    blocks, refs = refs[:count], refs[count:]
    (far_refs, over_refs), refs = (refs[:PARTS], refs[PARTS : 2 * PARTS]), refs[2 * PARTS :]
    train_ref, keep_ref, give_ref, total_ref, rows_v, train_v, sems = refs
    _, size, width = blocks[0].shape
    step = min(width, STEP)
    chunks = [(h, at) for h in range(PARTS) for at in range(0, width, step)]
    place = me_ref[0] // PAIR
    end = jnp.logical_or(place == 0, place == peers // PAIR - 1)
    copies, near, away = [], [], []
    for i, (h, at) in enumerate(chunks):
        to = slice(h * width + at, h * width + at + step)
        train = pltpu.make_async_copy(train_ref.at[:, to], train_v.at[:, to], sems.at[i, count])
        rows = [
            pltpu.make_async_copy(
                ref.at[h, :, at : at + step], rows_v.at[b * size : (b + 1) * size, to], sems.at[i, b])
            for b, ref in enumerate(blocks)
        ]
        copies.append([train] + rows)
        near.append(rows[-PAIR:])
        away.append([
            pltpu.make_async_copy(
                ref.at[:, at : at + step], rows_v.at[b * size : (b + 1) * size, to], sems.at[i, b])
            for b, ref in ((count - PAIR, far_refs[h]), (count - PAIR + 1, over_refs[h]))
        ])
    for chunk in copies:
        for copy in chunk[:-PAIR]:
            copy.start()

    @pl.when(end)
    def _():
        for chunk in away:
            for copy in chunk:
                copy.start()

    @pl.when(jnp.logical_not(end))
    def _():
        for chunk in near:
            for copy in chunk:
                copy.start()

    for i, (chunk, (h, at)) in enumerate(zip(copies, chunks)):
        for copy in chunk:
            copy.wait()
        to = slice(h * width + at, h * width + at + step)
        value = lax.dot_general(
            rows_v[:, to], train_v[:, to], (((1,), (1,)), ((), ())), preferred_element_type=jnp.float32)
        total_ref[...] = value if i == 0 else total_ref[...] + value

    f = me_ref[1]
    core, line = lax.rem(f, 2), f // 2
    lines, each = feats // 2, peers // feats
    for away in range(lines):
        to = lax.rem(line + away, lines) * 2
        for i in range(each):
            for ref, c in ((keep_ref, core), (give_ref, 1 - core)):
                row = rows_ref[(to + c) * each + i]
                block = total_ref[pl.ds(pl.multiple_of(jnp.maximum(row, 0) * size, size), size), :]
                ref[away * each + i] = jnp.where(row >= 0, block, 0.0)


def pair_scores(me, rows, blocks, far, over, train, peers, feats):
    _, size, width = blocks[0].shape
    examples, features = train.shape
    count = len(blocks)
    return pl.pallas_call(
        functools.partial(scores_kernel, peers, feats, count),
        in_specs=[SMEM] * 2 + [ANY] * (count + 2 * PARTS + 1),
        out_specs=[VMEM] * 2,
        out_shape=[jax.ShapeDtypeStruct((peers // 2, size, examples), jnp.float32)] * 2,
        scratch_shapes=[
            pltpu.VMEM((count * size, examples), jnp.float32),
            pltpu.VMEM((count * size, features), train.dtype),
            pltpu.VMEM((examples, features), train.dtype),
            pltpu.SemaphoreType.DMA((PARTS * (width // min(width, STEP)), count + 1)),
        ],
        cost_estimate=pl.CostEstimate(
            flops=2 * count * size * examples * features,
            bytes_accessed=2 * (count * size + examples) * features,
            transcendentals=0,
        ),
        compiler_params=pltpu.CompilerParams(vmem_limit_bytes=VMEM_LIMIT),
    )(me, rows, *blocks, *far, *over, train)


def shards(train_grads, audit_grads, owner_map, pair_blocks, pair_counts):
    peers, feats = lax.axis_size("ex"), lax.axis_size("feat")
    chain = peers // PAIR
    me = jnp.stack([lax.axis_index("ex"), lax.axis_index("feat")]).astype(jnp.int32)
    own = audit_grads[:, 0]
    width = own.shape[-1] // PARTS
    parts = range(PARTS)
    across = [(i, i ^ 1) for i in range(peers)]
    upward = [(i, i + PAIR) for i in range(peers - PAIR)]
    downward = [(i + PAIR, i) for i in range(peers - PAIR)]
    reach = peers - PAIR
    ends = [(i, i + reach) for i in range(PAIR)] + [(i + reach, i) for i in range(PAIR)]

    half = [own[:, :, h * width : (h + 1) * width] for h in parts]
    above, below = {(0, h): half[h] for h in parts}, {(0, h): half[h] for h in parts}

    def along(s, h):
        below[s, h] = lax.ppermute(below[s - 1, h], "ex", upward[(s - 1) * PAIR :])
        above[s, h] = lax.ppermute(above[s - 1, h], "ex", downward[: len(downward) - (s - 1) * PAIR])

    for h in parts:
        along(1, h)
    below[1, 0], above[1, 0], pair_blocks = lax.optimization_barrier((below[1, 0], above[1, 0], pair_blocks))
    wanted, rows = plan(me, owner_map, pair_blocks, pair_counts, peers)
    asked = lax.ppermute(wanted, "ex", across)
    ends = [(i, i + PAIR) for i in range(PAIR)] + [(i, i - PAIR) for i in range(peers - PAIR, peers)]
    notes = lax.ppermute(jnp.stack([asked, wanted]), "ex", ends)
    for s in range(2, chain - 1):
        for h in parts:
            if s == 2 and h == PARTS - 1:
                below[1, h], above[1, h], notes = lax.optimization_barrier((below[1, h], above[1, h], notes))
            along(s, h)
    last = chain - 2

    sides = [(j, i) for i, j in ends]
    beyond = [i for i in across if not PAIR <= i[0] < peers - PAIR]
    far, over = [], []
    for h in parts:
        given = hand(me, notes, above[last, h], below[last, h], chain)
        if h < PARTS - 1:
            given = lax.ppermute(given, "ex", sides)
        else:
            given = [lax.ppermute(given[i], "ex", sides) for i in range(PAIR)]
        over.append(lax.ppermute(given[0], "ex", beyond))
        far.append(given[1])

    slots = slots_of(chain)
    blocks = {}
    for slot in slots:
        d, second = slot
        if d == 0:
            mine, theirs = relay_own(me, wanted, asked, own)
        else:
            mine, theirs = relay(me, wanted, asked, above, below, d, second, chain)
        other = [(i, j) for i, j in across if not second or d <= i // PAIR < chain - d]
        blocks[slot] = [mine, lax.ppermute(theirs, "ex", other)]

    blocks = [block for slot in slots for block in blocks[slot]]
    keep, give = pair_scores(me, rows, blocks, far, over, train_grads, peers, feats)

    total = keep + lax.ppermute(give, "feat", [(i, i ^ 1) for i in range(feats)])
    lines, each = feats // 2, peers // feats
    result = total[:each]
    for away in range(1, lines):
        send = total[away * each : (away + 1) * each]
        result = result + lax.ppermute(send, "feat", [(i, (i + 2 * away) % feats) for i in range(feats)])
    return result[None]


def solution(mesh):
    in_specs = (P("ex", "feat"), P(None, "ex", None, "feat"), P(), P("ex", None), P("ex"))
    out_specs = P("ex", "feat", None, None)
    return jax.shard_map(shards, mesh=mesh, in_specs=in_specs, out_specs=out_specs, check_vma=False)
```

time: 168 us -> 104 us (0.62)
  waiting for transfers between devices: 112 us -> 43.4 us
  starting transfers between devices: 4.71 us -> 42.3 us
  blocking collectives: 13.5 us -> 0 us
  between operations: 14.1 us -> 1.01 us
  Pallas kernels: 0 us -> 11 us
  matrix products: 7.81 us -> 0 us
  local copies, waits for them, and re-layouts: 9.13 us -> 3.83 us
  other arithmetic: 6.46 us -> 1.96 us
    all_to_all x1 -> x0, waiting for transfers between devices: 91.3 us -> none  [shards(): lax.all_to_all(reply, 'ex', split_axis=0, concat_axis=0, tiled=True)]
    ppermute x0 -> x21, waiting for transfers between devices: none -> 43.4 us  [the longest x1 14.3 us: shards(): given = lax.ppermute(given, 'ex', sides)]
    ppermute x0 -> x21, starting transfers between devices: none -> 42.3 us  [the longest x4 11.5 us: along(): below[s, h] = lax.ppermute(below[s - 1, h], 'ex', upward[(s - 1) * PAIR:])]
    reduce_scatter x1 -> x0, waiting for transfers between devices: 20.9 us -> none  [shards(): lax.psum_scatter(scores * live[:, None, None], 'feat', scatter_dimension=...]
    all_to_all x1 -> x0, blocking collectives: 13.5 us -> none  [shards(): lax.all_to_all(wanted.reshape(peers, 1), 'ex', split_axis=0, concat_axis=...]
    pallas_call x0 -> x8, Pallas kernels: none -> 11 us  [the longest x1 5.68 us: pair_scores(): pl.pallas_call(functools.partial(scores_kernel, peers, feats, count), in_...]
    gather x3 -> x0, local copies, waits for them, and re-layouts: 9.04 us -> none  [the longest x1 4.97 us: shards(): rows = jnp.take(fetched, holder, axis=0)]
    dot_general x1 -> x0, matrix products: 7.81 us -> none  [shards(): jnp.einsum('kaf,tf->kat', rows, train_grads, preferred_element_type=jnp.f...]
  transfers between devices with their start and end apart: 2 -> 21, of which waited for: 2 -> 10; matrix products, arithmetic and copies ran while one was open for 0% -> 1% of each run, Pallas kernels for 0% -> 5%
where the time goes in v2:
time: 104 us; the launch traced here: 103 us
  waiting for transfers between devices  43.4 us (42%)
  starting transfers between devices  42.3 us (41%)
  Pallas kernels  11 us (11%)
  local copies, waits for them, and re-layouts  3.83 us (4%)
  other arithmetic  1.96 us (2%)
    ppermute x1, waiting for transfers between devices, shards(): given = lax.ppermute(given, 'ex', sides)  14.3 us
    ppermute x4, starting transfers between devices, along(): below[s, h] = lax.ppermute(below[s - 1, h], 'ex', upward[(s - 1) * PAIR:])  11.5 us
    ppermute x2, waiting for transfers between devices, shards(): over.append(lax.ppermute(given[0], 'ex', beyond))  9.77 us
    ppermute x4, waiting for transfers between devices, along(): lax.ppermute(above[s - 1, h], 'ex', downward[:len(downward) - (s - 1) * P...  8.51 us
    ppermute x1, starting transfers between devices, shards(): notes = lax.ppermute(jnp.stack([asked, wanted]), 'ex', ends)  7.82 us
    ppermute x2, starting transfers between devices, shards(): over.append(lax.ppermute(given[0], 'ex', beyond))  5.83 us
    pallas_call x1, Pallas kernels, pair_scores(): pl.pallas_call(functools.partial(scores_kernel, peers, feats, count), in_...  5.68 us
    ppermute x4, starting transfers between devices, along(): lax.ppermute(above[s - 1, h], 'ex', downward[:len(downward) - (s - 1) * P...  5.17 us
  transfers between devices with their start and end apart: 21, of which 10 were waited for; matrix products, arithmetic and copies ran while one was open for 1% of the time, Pallas kernels for 5%

profile of v2, /device:TPU:0, one launch (start us, length us, event | category | flops | bytes accessed | tf_op | source)
XLA Modules:
  0.0 103.4 jit_solution(16808894129198850662)
XLA Ops:
  0.0 1.3 %fusion.1 = (bf16[2,32,4096]{2,1,0:T(8,128)(2,1)S(1)}, bf16[2,32,4096]{2,1,0:T(8,128)(2,1)S(1)}) fusion(bf16[2,32,8192]{2,1,0:T(8,128)(2,1)} %bitcast.15), kind=kLoop, calls=%fused_computation.8 | loop fusion | bytes 2097152 | tf_op jit(solution)/shard_map/slice | solution.py:267
  1.3 1.3 %collective-permute-start.1 = (bf16[2,32,4096]{2,1,0:T(8,128)(2,1)S(1)}, bf16[2,32,4096]{2,1,0:T(8,128)(2,1)S(1)}, u32[]{:S(2)}, u32[]{:S(2)}) collective-permute-start(bf16[2,32,4096]{2,1,0:T(8,128)(2,1)S(1)} %get-tuple-element.42), channel_id=1, source_target_pairs={{8,0},{12,4},{16,8},{20,12},{24,16},{28,20},{9,1},{13,5},{17,9},{2... | collective-permute-start | bytes 1572872 | tf_op jit(solution)/shard_map/ppermute | solution.py:272
  2.6 5.6 %collective-permute-start = (bf16[2,32,4096]{2,1,0:T(8,128)(2,1)S(1)}, bf16[2,32,4096]{2,1,0:T(8,128)(2,1)S(1)}, u32[]{:S(2)}, u32[]{:S(2)}) collective-permute-start(bf16[2,32,4096]{2,1,0:T(8,128)(2,1)S(1)} %get-tuple-element.42), channel_id=1, source_target_pairs={{0,8},{4,12},{8,16},{12,20},{16,24},{20,28},{1,9},{5,13},{9,17},{1... | collective-permute-start | bytes 1572872 | tf_op jit(solution)/shard_map/ppermute | solution.py:271
  8.2 1.3 %collective-permute-start.5 = (bf16[2,32,4096]{2,1,0:T(8,128)(2,1)S(1)}, bf16[2,32,4096]{2,1,0:T(8,128)(2,1)S(1)}, u32[]{:S(2)}, u32[]{:S(2)}) collective-permute-start(bf16[2,32,4096]{2,1,0:T(8,128)(2,1)S(1)} %get-tuple-element.41), channel_id=1, source_target_pairs={{8,0},{12,4},{16,8},{20,12},{24,16},{28,20},{9,1},{13,5},{17,9},{2... | collective-permute-start | bytes 1572872 | tf_op jit(solution)/shard_map/ppermute | solution.py:272
  9.5 4.6 %collective-permute-start.4 = (bf16[2,32,4096]{2,1,0:T(8,128)(2,1)S(1)}, bf16[2,32,4096]{2,1,0:T(8,128)(2,1)S(1)}, u32[]{:S(2)}, u32[]{:S(2)}) collective-permute-start(bf16[2,32,4096]{2,1,0:T(8,128)(2,1)S(1)} %get-tuple-element.41), channel_id=1, source_target_pairs={{0,8},{4,12},{8,16},{12,20},{16,24},{20,28},{1,9},{5,13},{9,17},{1... | collective-permute-start | bytes 1572872 | tf_op jit(solution)/shard_map/ppermute | solution.py:271
  15.3 3.7 %collective-permute-done.1.refs_2_.refs_0_ = bf16[2,32,4096]{2,1,0:T(8,128)(2,1)S(1)} collective-permute-done((bf16[2,32,4096]{2,1,0:T(8,128)(2,1)S(1)}, bf16[2,32,4096]{2,1,0:T(8,128)(2,1)S(1)}, u32[]{:S(2)}, u32[]{:S(2)}) %collective-permute-start.1) | collective-permute-done | bytes 524320 | tf_op jit(solution)/shard_map/ppermute | solution.py:272
  18.9 1.5 %collective-permute-done.refs_0_ = bf16[2,32,4096]{2,1,0:T(8,128)(2,1)S(1)} collective-permute-done((bf16[2,32,4096]{2,1,0:T(8,128)(2,1)S(1)}, bf16[2,32,4096]{2,1,0:T(8,128)(2,1)S(1)}, u32[]{:S(2)}, u32[]{:S(2)}) %collective-permute-start) | collective-permute-done | bytes 524320 | tf_op jit(solution)/shard_map/ppermute | solution.py:271
  20.4 1.3 %shard_map.55 = (s32[8]{0:T(128)}, s32[8]{0:T(128)}) custom-call(s32[2]{0:T(128)} %pad_add_fusion.1.me_ref, s32[16]{0:T(128)} %owner_ref.1, s32[1,8]{1,0:T(1,128)} %pairs_ref, s32[1]{0:T(128)S(6)} %copy.6.counts_ref), custom_call_target="tpu_custom_call" | custom-call | tf_op jit(solution)/shard_map/pallas_call | solution.py:45
  21.8 2.0 %collective-permute-start.2 = (s32[8]{0:T(128)}, s32[8]{0:T(128)S(1)}, u32[]{:S(2)}, u32[]{:S(2)}) collective-permute-start(s32[8]{0:T(128)} %get-tuple-element.25.wanted_ref), channel_id=1, source_target_pairs={{0,4},{4,0},{8,12},{12,8},{16,20},{20,16},{24,28},{28,24},{1,5},{5... | collective-permute-start | bytes 104 | tf_op jit(solution)/shard_map/ppermute | solution.py:278
  24.5 1.3 %collective-permute-start.10 = (bf16[2,32,4096]{2,1,0:T(8,128)(2,1)S(1)}, bf16[2,32,4096]{2,1,0:T(8,128)(2,1)S(1)}, u32[]{:S(2)}, u32[]{:S(2)}) collective-permute-start(bf16[2,32,4096]{2,1,0:T(8,128)(2,1)S(1)} %collective-permute-done.1.refs_2_.refs_0_), channel_id=1, source_target_pairs={{8,0},{12,4},{16,8},{20,12},{9,1},{13,5},{17,9},{21,13},{10,2},{14... | collective-permute-start | bytes 1572872 | tf_op jit(solution)/shard_map/ppermute | solution.py:272
  26.5 7.8 %collective-permute-start.6 = (s32[2,8]{1,0:T(2,128)S(1)}, s32[2,8]{1,0:T(2,128)S(1)}, u32[]{:S(2)}, u32[]{:S(2)}) collective-permute-start(s32[2,8]{1,0:T(2,128)S(1)} %pad_add_fusion), channel_id=1, source_target_pairs={{0,8},{4,12},{24,16},{28,20},{1,9},{5,13},{25,17},{29,21},{2,10},{... | collective-permute-start | bytes 200 | tf_op jit(solution)/shard_map/ppermute | solution.py:280
  34.3 1.3 %collective-permute-done.6.notes_ref = s32[2,8]{1,0:T(2,128)S(1)} collective-permute-done((s32[2,8]{1,0:T(2,128)S(1)}, s32[2,8]{1,0:T(2,128)S(1)}, u32[]{:S(2)}, u32[]{:S(2)}) %collective-permute-start.6) | collective-permute-done | bytes 96 | tf_op jit(solution)/shard_map/ppermute | solution.py:280
  36.3 1.3 %collective-permute-start.11 = (bf16[2,32,4096]{2,1,0:T(8,128)(2,1)S(1)}, bf16[2,32,4096]{2,1,0:T(8,128)(2,1)S(1)}, u32[]{:S(2)}, u32[]{:S(2)}) collective-permute-start(bf16[2,32,4096]{2,1,0:T(8,128)(2,1)S(1)} %collective-permute-done.5.refs_3_.refs_1_), channel_id=1, source_target_pairs={{8,0},{12,4},{16,8},{20,12},{9,1},{13,5},{17,9},{21,13},{10,2},{14... | collective-permute-start | bytes 1572872 | tf_op jit(solution)/shard_map/ppermute | solution.py:272
  37.6 1.2 %copy-done = bf16[2,1,32,8192]{3,2,1,0:T(8,128)(2,1)S(1)} copy-done((bf16[2,1,32,8192]{3,2,1,0:T(8,128)(2,1)S(1)}, bf16[2,1,32,8192]{3,2,1,0:T(8,128)(2,1)}, u32[]{:S(2)}) %copy-start) | copy-done | bytes 1048600
  42.8 0.7 collective-permute-start.13
  43.5 1.6 %collective-permute-start.7 = (bf16[2,32,4096]{2,1,0:T(8,128)(2,1)S(1)}, bf16[2,32,4096]{2,1,0:T(8,128)(2,1)S(1)}, u32[]{:S(2)}, u32[]{:S(2)}) collective-permute-start(bf16[2,32,4096]{2,1,0:T(8,128)(2,1)S(1)} %get-tuple-element.33), channel_id=1, source_target_pairs={{0,4},{4,0},{8,12},{12,8},{16,20},{20,16},{24,28},{28,24},{1,5},{5... | collective-permute-start | bytes 1572872 | tf_op jit(solution)/shard_map/ppermute | solution.py:309
  45.7 1.3 %collective-permute-start.14 = (bf16[2,32,4096]{2,1,0:T(8,128)(2,1)S(1)}, bf16[2,32,4096]{2,1,0:T(8,128)(2,1)S(1)}, u32[]{:S(2)}, u32[]{:S(2)}) collective-permute-start(bf16[2,32,4096]{2,1,0:T(8,128)(2,1)S(1)} %shard_map.60), channel_id=1, source_target_pairs={{8,0},{12,4},{16,24},{20,28},{9,1},{13,5},{17,25},{21,29},{10,2},{... | collective-permute-start | bytes 1572872 | tf_op jit(solution)/shard_map/ppermute | solution.py:294
  47.0 4.8 %collective-permute-done.11.refs_3_.above_ref = bf16[2,32,4096]{2,1,0:T(8,128)(2,1)S(1)} collective-permute-done((bf16[2,32,4096]{2,1,0:T(8,128)(2,1)S(1)}, bf16[2,32,4096]{2,1,0:T(8,128)(2,1)S(1)}, u32[]{:S(2)}, u32[]{:S(2)}) %collective-permute-start.11) | collective-permute-done | bytes 524320 | tf_op jit(solution)/shard_map/ppermute | solution.py:272
  52.5 1.3 %collective-permute-start.17 = (bf16[32,4096]{1,0:T(8,128)(2,1)S(1)}, bf16[32,4096]{1,0:T(8,128)(2,1)S(1)}, u32[]{:S(2)}, u32[]{:S(2)}) collective-permute-start(bf16[32,4096]{1,0:T(8,128)(2,1)S(1)} %get-tuple-element.43), channel_id=1, source_target_pairs={{8,0},{12,4},{16,24},{20,28},{9,1},{13,5},{17,25},{21,29},{10,2},{... | collective-permute-start | bytes 786440 | tf_op jit(solution)/shard_map/ppermute | solution.py:296
  53.8 0.7 shard_map.58
  54.5 14.3 %collective-permute-done.14 = bf16[2,32,4096]{2,1,0:T(8,128)(2,1)S(1)} collective-permute-done((bf16[2,32,4096]{2,1,0:T(8,128)(2,1)S(1)}, bf16[2,32,4096]{2,1,0:T(8,128)(2,1)S(1)}, u32[]{:S(2)}, u32[]{:S(2)}) %collective-permute-start.14) | collective-permute-done | bytes 524320 | tf_op jit(solution)/shard_map/ppermute | solution.py:294
  68.8 1.5 %collective-permute-start.12 = (bf16[2,32,4096]{2,1,0:T(8,128)(2,1)S(1)}, bf16[2,32,4096]{2,1,0:T(8,128)(2,1)S(1)}, u32[]{:S(2)}, u32[]{:S(2)}) collective-permute-start(bf16[2,32,4096]{2,1,0:T(8,128)(2,1)S(1)} %get-tuple-element.35), channel_id=1, source_target_pairs={{0,4},{4,0},{8,12},{12,8},{16,20},{20,16},{24,28},{28,24},{1,5},{5... | collective-permute-start | bytes 1572872 | tf_op jit(solution)/shard_map/ppermute | solution.py:309
  70.4 1.3 %collective-permute-start.15 = (bf16[32,4096]{1,0:T(8,128)(2,1)S(1)}, bf16[32,4096]{1,0:T(8,128)(2,1)S(1)}, u32[]{:S(2)}, u32[]{:S(2)}) collective-permute-start(bf16[32,4096]{1,0:T(8,128)(2,1)S(1)} %get-tuple-element.44), channel_id=1, source_target_pairs={{8,0},{12,4},{16,24},{20,28},{9,1},{13,5},{17,25},{21,29},{10,2},{... | collective-permute-start | bytes 786440 | tf_op jit(solution)/shard_map/ppermute | solution.py:296
  71.7 2.5 %collective-permute-done.17 = bf16[32,4096]{1,0:T(8,128)(2,1)S(1)} collective-permute-done((bf16[32,4096]{1,0:T(8,128)(2,1)S(1)}, bf16[32,4096]{1,0:T(8,128)(2,1)S(1)}, u32[]{:S(2)}, u32[]{:S(2)}) %collective-permute-start.17) | collective-permute-done | bytes 262176 | tf_op jit(solution)/shard_map/ppermute | solution.py:296
  74.2 3.7 %collective-permute-start.18 = (bf16[32,4096]{1,0:T(8,128)(2,1)S(1)}, bf16[32,4096]{1,0:T(8,128)(2,1)S(1)}, u32[]{:S(2)}, u32[]{:S(2)}) collective-permute-start(bf16[32,4096]{1,0:T(8,128)(2,1)S(1)} %collective-permute-done.17), channel_id=1, source_target_pairs={{0,4},{4,0},{24,28},{28,24},{1,5},{5,1},{25,29},{29,25},{2,6},{6,2... | collective-permute-start | bytes 786440 | tf_op jit(solution)/shard_map/ppermute | solution.py:297
  77.9 2.1 %collective-permute-start.16 = (bf16[32,4096]{1,0:T(8,128)(2,1)S(1)}, bf16[32,4096]{1,0:T(8,128)(2,1)S(1)}, u32[]{:S(2)}, u32[]{:S(2)}) collective-permute-start(bf16[32,4096]{1,0:T(8,128)(2,1)S(1)} %get-tuple-element.45), channel_id=1, source_target_pairs={{0,4},{4,0},{24,28},{28,24},{1,5},{5,1},{25,29},{29,25},{2,6},{6,2... | collective-permute-start | bytes 786440 | tf_op jit(solution)/shard_map/ppermute | solution.py:297
  80.0 7.0 %collective-permute-done.18.refs_11_ = bf16[32,4096]{1,0:T(8,128)(2,1)S(1)} collective-permute-done((bf16[32,4096]{1,0:T(8,128)(2,1)S(1)}, bf16[32,4096]{1,0:T(8,128)(2,1)S(1)}, u32[]{:S(2)}, u32[]{:S(2)}) %collective-permute-start.18) | collective-permute-done | bytes 262176 | tf_op jit(solution)/shard_map/ppermute | solution.py:297
  87.0 2.8 %collective-permute-done.16.refs_10_ = bf16[32,4096]{1,0:T(8,128)(2,1)S(1)} collective-permute-done((bf16[32,4096]{1,0:T(8,128)(2,1)S(1)}, bf16[32,4096]{1,0:T(8,128)(2,1)S(1)}, u32[]{:S(2)}, u32[]{:S(2)}) %collective-permute-start.16) | collective-permute-done | bytes 262176 | tf_op jit(solution)/shard_map/ppermute | solution.py:297
  89.8 5.7 %shard_map.62 = (f32[4,32,512]{2,1,0:T(8,128)S(1)}, f32[4,32,512]{2,1,0:T(8,128)S(1)}) custom-call(s32[2]{0:T(128)S(1)} %copy-done.2, s32[8]{0:T(128)S(1)} %copy-done.3, bf16[2,32,4096]{2,1,0:T(8,128)(2,1)S(1)} %get-tuple-element.26.refs_0_, bf16[2,32,4096]{2,1,0:T(8,128)(2,1)S(1)} %collective-permute-done.3.refs_1_, ...), custom_call_target="tpu_custom_call" | custom-call | flops 2147483648 | bytes 12582912 | tf_op jit(solution)/shard_map/pallas_call | solution.py:234
  95.6 1.5 %collective-permute-done.19 = f32[4,32,512]{2,1,0:T(8,128)S(1)} collective-permute-done((f32[4,32,512]{2,1,0:T(8,128)S(1)}, f32[4,32,512]{2,1,0:T(8,128)S(1)}, u32[]{:S(2)}, u32[]{:S(2)}) %collective-permute-start.19) | collective-permute-done | bytes 262176 | tf_op jit(solution)/shard_map/ppermute | solution.py:314
  97.2 1.6 %collective-permute-start.20 = (f32[2,32,512]{2,1,0:T(8,128)S(1)}, f32[2,32,512]{2,1,0:T(8,128)S(1)}, u32[]{:S(2)}, u32[]{:S(2)}) collective-permute-start(f32[2,32,512]{2,1,0:T(8,128)S(1)} %slice.39), channel_id=1, source_target_pairs={{0,2},{1,3},{2,0},{3,1},{4,6},{5,7},{6,4},{7,5},{8,10},{9,11},{10,... | collective-permute-start | bytes 393224 | tf_op jit(solution)/shard_map/ppermute | solution.py:319
  98.7 4.0 %collective-permute-done.20 = f32[2,32,512]{2,1,0:T(8,128)S(1)} collective-permute-done((f32[2,32,512]{2,1,0:T(8,128)S(1)}, f32[2,32,512]{2,1,0:T(8,128)S(1)}, u32[]{:S(2)}, u32[]{:S(2)}) %collective-permute-start.20) | collective-permute-done | bytes 131104 | tf_op jit(solution)/shard_map/ppermute | solution.py:319
  (38 shorter events, 8.7 us)
Async XLA Ops:
  1.3 17.7 %collective-permute-start.1 = (bf16[2,32,4096]{2,1,0:T(8,128)(2,1)S(1)}, bf16[2,32,4096]{2,1,0:T(8,128)(2,1)S(1)}, u32[]{:S(2)}, u32[]{:S(2)}) collective-permute-start(bf16[2,32,4096]{2,1,0:T(8,128)(2,1)S(1)} %get-tuple-element.42), channel_id=1, source_target_pairs={{8,0},{12,4},{16,8},{20,12},{24,16},{28,20},{9,1},{13,5},{17,9},{2... | collective-permute-start | bytes 1572872 | tf_op jit(solution)/shard_map/ppermute | solution.py:272
  2.6 17.9 %collective-permute-start = (bf16[2,32,4096]{2,1,0:T(8,128)(2,1)S(1)}, bf16[2,32,4096]{2,1,0:T(8,128)(2,1)S(1)}, u32[]{:S(2)}, u32[]{:S(2)}) collective-permute-start(bf16[2,32,4096]{2,1,0:T(8,128)(2,1)S(1)} %get-tuple-element.42), channel_id=1, source_target_pairs={{0,8},{4,12},{8,16},{12,20},{16,24},{20,28},{1,9},{5,13},{9,17},{1... | collective-permute-start | bytes 1572872 | tf_op jit(solution)/shard_map/ppermute | solution.py:271
  8.2 26.1 %collective-permute-start.5 = (bf16[2,32,4096]{2,1,0:T(8,128)(2,1)S(1)}, bf16[2,32,4096]{2,1,0:T(8,128)(2,1)S(1)}, u32[]{:S(2)}, u32[]{:S(2)}) collective-permute-start(bf16[2,32,4096]{2,1,0:T(8,128)(2,1)S(1)} %get-tuple-element.41), channel_id=1, source_target_pairs={{8,0},{12,4},{16,8},{20,12},{24,16},{28,20},{9,1},{13,5},{17,9},{2... | collective-permute-start | bytes 1572872 | tf_op jit(solution)/shard_map/ppermute | solution.py:272
  9.5 24.9 %collective-permute-start.4 = (bf16[2,32,4096]{2,1,0:T(8,128)(2,1)S(1)}, bf16[2,32,4096]{2,1,0:T(8,128)(2,1)S(1)}, u32[]{:S(2)}, u32[]{:S(2)}) collective-permute-start(bf16[2,32,4096]{2,1,0:T(8,128)(2,1)S(1)} %get-tuple-element.41), channel_id=1, source_target_pairs={{0,8},{4,12},{8,16},{12,20},{16,24},{20,28},{1,9},{5,13},{9,17},{1... | collective-permute-start | bytes 1572872 | tf_op jit(solution)/shard_map/ppermute | solution.py:271
  21.8 4.0 %collective-permute-start.2 = (s32[8]{0:T(128)}, s32[8]{0:T(128)S(1)}, u32[]{:S(2)}, u32[]{:S(2)}) collective-permute-start(s32[8]{0:T(128)} %get-tuple-element.25.wanted_ref), channel_id=1, source_target_pairs={{0,4},{4,0},{8,12},{12,8},{16,20},{20,16},{24,28},{28,24},{1,5},{5... | collective-permute-start | bytes 104 | tf_op jit(solution)/shard_map/ppermute | solution.py:278
  23.8 18.9 %collective-permute-start.8 = (bf16[2,32,4096]{2,1,0:T(8,128)(2,1)S(1)}, bf16[2,32,4096]{2,1,0:T(8,128)(2,1)S(1)}, u32[]{:S(2)}, u32[]{:S(2)}) collective-permute-start(bf16[2,32,4096]{2,1,0:T(8,128)(2,1)S(1)} %collective-permute-done.refs_0_), channel_id=1, source_target_pairs={{8,16},{12,20},{16,24},{20,28},{9,17},{13,21},{17,25},{21,29},{10,... | collective-permute-start | bytes 1572872 | tf_op jit(solution)/shard_map/ppermute | solution.py:271
  24.5 19.0 %collective-permute-start.10 = (bf16[2,32,4096]{2,1,0:T(8,128)(2,1)S(1)}, bf16[2,32,4096]{2,1,0:T(8,128)(2,1)S(1)}, u32[]{:S(2)}, u32[]{:S(2)}) collective-permute-start(bf16[2,32,4096]{2,1,0:T(8,128)(2,1)S(1)} %collective-permute-done.1.refs_2_.refs_0_), channel_id=1, source_target_pairs={{8,0},{12,4},{16,8},{20,12},{9,1},{13,5},{17,9},{21,13},{10,2},{14... | collective-permute-start | bytes 1572872 | tf_op jit(solution)/shard_map/ppermute | solution.py:272
  26.5 9.1 %collective-permute-start.6 = (s32[2,8]{1,0:T(2,128)S(1)}, s32[2,8]{1,0:T(2,128)S(1)}, u32[]{:S(2)}, u32[]{:S(2)}) collective-permute-start(s32[2,8]{1,0:T(2,128)S(1)} %pad_add_fusion), channel_id=1, source_target_pairs={{0,8},{4,12},{24,16},{28,20},{1,9},{5,13},{25,17},{29,21},{2,10},{... | collective-permute-start | bytes 200 | tf_op jit(solution)/shard_map/ppermute | solution.py:280
  35.6 10.1 %collective-permute-start.9 = (bf16[2,32,4096]{2,1,0:T(8,128)(2,1)S(1)}, bf16[2,32,4096]{2,1,0:T(8,128)(2,1)S(1)}, u32[]{:S(2)}, u32[]{:S(2)}) collective-permute-start(bf16[2,32,4096]{2,1,0:T(8,128)(2,1)S(1)} %collective-permute-done.4.refs_1_), channel_id=1, source_target_pairs={{8,16},{12,20},{16,24},{20,28},{9,17},{13,21},{17,25},{21,29},{10,... | collective-permute-start | bytes 1572872 | tf_op jit(solution)/shard_map/ppermute | solution.py:271
  36.3 15.5 %collective-permute-start.11 = (bf16[2,32,4096]{2,1,0:T(8,128)(2,1)S(1)}, bf16[2,32,4096]{2,1,0:T(8,128)(2,1)S(1)}, u32[]{:S(2)}, u32[]{:S(2)}) collective-permute-start(bf16[2,32,4096]{2,1,0:T(8,128)(2,1)S(1)} %collective-permute-done.5.refs_3_.refs_1_), channel_id=1, source_target_pairs={{8,0},{12,4},{16,8},{20,12},{9,1},{13,5},{17,9},{21,13},{10,2},{14... | collective-permute-start | bytes 1572872 | tf_op jit(solution)/shard_map/ppermute | solution.py:272
  37.6 1.2 %copy-start = (bf16[2,1,32,8192]{3,2,1,0:T(8,128)(2,1)S(1)}, bf16[2,1,32,8192]{3,2,1,0:T(8,128)(2,1)}, u32[]{:S(2)}) copy-start(bf16[2,1,32,8192]{3,2,1,0:T(8,128)(2,1)} %param.6) | copy-start | bytes 3145732
  38.8 0.6 copy-start.1
  39.4 0.7 copy-start.4
  40.7 13.1 %copy-start.2 = (s32[2]{0:T(128)S(1)}, s32[2]{0:T(128)}, u32[]{:S(2)}) copy-start(s32[2]{0:T(128)} %pad_add_fusion.1.me_ref) | copy-start | bytes 28
  40.7 13.1 %copy-start.5 = (s32[8]{0:T(128)S(1)}, s32[8]{0:T(128)}, u32[]{:S(2)}) copy-start(s32[8]{0:T(128)} %get-tuple-element.25.wanted_ref) | copy-start | bytes 100
  40.8 29.6 %collective-permute-start.3 = (bf16[2,32,4096]{2,1,0:T(8,128)(2,1)S(1)}, bf16[2,32,4096]{2,1,0:T(8,128)(2,1)S(1)}, u32[]{:S(2)}, u32[]{:S(2)}) collective-permute-start(bf16[2,32,4096]{2,1,0:T(8,128)(2,1)S(1)} %get-tuple-element.27), channel_id=1, source_target_pairs={{0,4},{4,0},{8,12},{12,8},{16,20},{20,16},{24,28},{28,24},{1,5},{5... | collective-permute-start | bytes 1572872 | tf_op jit(solution)/shard_map/ppermute | solution.py:309
  42.1 47.7 %copy-start.3 = (s32[8]{0:T(128)S(1)}, s32[8]{0:T(128)}, u32[]{:S(2)}) copy-start(s32[8]{0:T(128)} %get-tuple-element.24.rows_ref) | copy-start | bytes 100
  42.8 35.1 %collective-permute-start.13 = (bf16[2,32,4096]{2,1,0:T(8,128)(2,1)S(1)}, bf16[2,32,4096]{2,1,0:T(8,128)(2,1)S(1)}, u32[]{:S(2)}, u32[]{:S(2)}) collective-permute-start(bf16[2,32,4096]{2,1,0:T(8,128)(2,1)S(1)} %get-tuple-element.37), channel_id=1, source_target_pairs={{8,12},{12,8},{16,20},{20,16},{9,13},{13,9},{17,21},{21,17},{10,14... | collective-permute-start | bytes 1572872 | tf_op jit(solution)/shard_map/ppermute | solution.py:309
  43.5 36.5 %collective-permute-start.7 = (bf16[2,32,4096]{2,1,0:T(8,128)(2,1)S(1)}, bf16[2,32,4096]{2,1,0:T(8,128)(2,1)S(1)}, u32[]{:S(2)}, u32[]{:S(2)}) collective-permute-start(bf16[2,32,4096]{2,1,0:T(8,128)(2,1)S(1)} %get-tuple-element.33), channel_id=1, source_target_pairs={{0,4},{4,0},{8,12},{12,8},{16,20},{20,16},{24,28},{28,24},{1,5},{5... | collective-permute-start | bytes 1572872 | tf_op jit(solution)/shard_map/ppermute | solution.py:309
  45.7 23.2 %collective-permute-start.14 = (bf16[2,32,4096]{2,1,0:T(8,128)(2,1)S(1)}, bf16[2,32,4096]{2,1,0:T(8,128)(2,1)S(1)}, u32[]{:S(2)}, u32[]{:S(2)}) collective-permute-start(bf16[2,32,4096]{2,1,0:T(8,128)(2,1)S(1)} %shard_map.60), channel_id=1, source_target_pairs={{8,0},{12,4},{16,24},{20,28},{9,1},{13,5},{17,25},{21,29},{10,2},{... | collective-permute-start | bytes 1572872 | tf_op jit(solution)/shard_map/ppermute | solution.py:294
  52.5 21.6 %collective-permute-start.17 = (bf16[32,4096]{1,0:T(8,128)(2,1)S(1)}, bf16[32,4096]{1,0:T(8,128)(2,1)S(1)}, u32[]{:S(2)}, u32[]{:S(2)}) collective-permute-start(bf16[32,4096]{1,0:T(8,128)(2,1)S(1)} %get-tuple-element.43), channel_id=1, source_target_pairs={{8,0},{12,4},{16,24},{20,28},{9,1},{13,5},{17,25},{21,29},{10,2},{... | collective-permute-start | bytes 786440 | tf_op jit(solution)/shard_map/ppermute | solution.py:296
  68.8 18.2 %collective-permute-start.12 = (bf16[2,32,4096]{2,1,0:T(8,128)(2,1)S(1)}, bf16[2,32,4096]{2,1,0:T(8,128)(2,1)S(1)}, u32[]{:S(2)}, u32[]{:S(2)}) collective-permute-start(bf16[2,32,4096]{2,1,0:T(8,128)(2,1)S(1)} %get-tuple-element.35), channel_id=1, source_target_pairs={{0,4},{4,0},{8,12},{12,8},{16,20},{20,16},{24,28},{28,24},{1,5},{5... | collective-permute-start | bytes 1572872 | tf_op jit(solution)/shard_map/ppermute | solution.py:309
  70.4 9.6 %collective-permute-start.15 = (bf16[32,4096]{1,0:T(8,128)(2,1)S(1)}, bf16[32,4096]{1,0:T(8,128)(2,1)S(1)}, u32[]{:S(2)}, u32[]{:S(2)}) collective-permute-start(bf16[32,4096]{1,0:T(8,128)(2,1)S(1)} %get-tuple-element.44), channel_id=1, source_target_pairs={{8,0},{12,4},{16,24},{20,28},{9,1},{13,5},{17,25},{21,29},{10,2},{... | collective-permute-start | bytes 786440 | tf_op jit(solution)/shard_map/ppermute | solution.py:296
  74.2 12.8 %collective-permute-start.18 = (bf16[32,4096]{1,0:T(8,128)(2,1)S(1)}, bf16[32,4096]{1,0:T(8,128)(2,1)S(1)}, u32[]{:S(2)}, u32[]{:S(2)}) collective-permute-start(bf16[32,4096]{1,0:T(8,128)(2,1)S(1)} %collective-permute-done.17), channel_id=1, source_target_pairs={{0,4},{4,0},{24,28},{28,24},{1,5},{5,1},{25,29},{29,25},{2,6},{6,2... | collective-permute-start | bytes 786440 | tf_op jit(solution)/shard_map/ppermute | solution.py:297
  77.9 11.9 %collective-permute-start.16 = (bf16[32,4096]{1,0:T(8,128)(2,1)S(1)}, bf16[32,4096]{1,0:T(8,128)(2,1)S(1)}, u32[]{:S(2)}, u32[]{:S(2)}) collective-permute-start(bf16[32,4096]{1,0:T(8,128)(2,1)S(1)} %get-tuple-element.45), channel_id=1, source_target_pairs={{0,4},{4,0},{24,28},{28,24},{1,5},{5,1},{25,29},{29,25},{2,6},{6,2... | collective-permute-start | bytes 786440 | tf_op jit(solution)/shard_map/ppermute | solution.py:297
  95.5 1.6 %collective-permute-start.19 = (f32[4,32,512]{2,1,0:T(8,128)S(1)}, f32[4,32,512]{2,1,0:T(8,128)S(1)}, u32[]{:S(2)}, u32[]{:S(2)}) collective-permute-start(f32[4,32,512]{2,1,0:T(8,128)S(1)} %get-tuple-element.40), channel_id=1, source_target_pairs={{0,1},{1,0},{2,3},{3,2},{4,5},{5,4},{6,7},{7,6},{8,9},{9,8},{10,11... | collective-permute-start | bytes 786440 | tf_op jit(solution)/shard_map/ppermute | solution.py:314
  97.2 5.6 %collective-permute-start.20 = (f32[2,32,512]{2,1,0:T(8,128)S(1)}, f32[2,32,512]{2,1,0:T(8,128)S(1)}, u32[]{:S(2)}, u32[]{:S(2)}) collective-permute-start(f32[2,32,512]{2,1,0:T(8,128)S(1)} %slice.39), channel_id=1, source_target_pairs={{0,2},{1,3},{2,0},{3,1},{4,6},{5,7},{6,4},{7,5},{8,10},{9,11},{10,... | collective-permute-start | bytes 393224 | tf_op jit(solution)/shard_map/ppermute | solution.py:319

commit v3 on v0

v3 whole, which is shorter than its diff:
```python
import functools

import jax
import jax.numpy as jnp
from jax import lax
from jax.experimental import pallas as pl
from jax.experimental.pallas import tpu as pltpu
from jax.sharding import PartitionSpec as P

PAIR = 2
PARTS = 2
STEP = 1024
SMALL_LIMIT = 8 * 2**20
VMEM_LIMIT = 52 * 2**20
COST = pl.CostEstimate(flops=0, bytes_accessed=0, transcendentals=0)
SMEM = pl.BlockSpec(memory_space=pltpu.SMEM)
VMEM = pl.BlockSpec(memory_space=pltpu.VMEM)
ANY = pl.BlockSpec(memory_space=pl.ANY)


def slots_of(chain):
    first = [(d, False) for d in range(1, chain - 1)]
    return [(0, False)] + first + [(d, True) for d in range((chain - 1) // 2, 0, -1)]


def plan_kernel(peers, owner_ref, pairs_ref, counts_ref, wanted_ref, rows_ref):
    chain = peers // PAIR
    slots = len(slots_of(chain))
    me = lax.axis_index("ex")
    place, column = me // PAIR, lax.rem(me, PAIR)
    lane = lax.broadcasted_iota(jnp.int32, (1, peers), 1)
    wanted, rows = jnp.zeros((1, peers), jnp.int32), jnp.zeros((1, peers), jnp.int32)
    for k in range(peers):
        stored = owner_ref[pairs_ref[0, k]]
        holder = lax.rem(stored, peers)
        wanted = jnp.where(lane == holder, stored // peers, wanted)
        there = holder // PAIR
        far = jnp.abs(there - place)
        second = jnp.logical_and(there > place, place >= far)
        slot = jnp.where(far == chain - 1, slots - 1, jnp.where(second, slots - far, far))
        row = slot * PAIR + (lax.rem(holder, PAIR) != column).astype(jnp.int32)
        rows = jnp.where(lane == k, jnp.where(k < counts_ref[0], row, -1), rows)
    wanted_ref[...] = wanted
    rows_ref[...] = rows


def plan(owner_map, pair_blocks, pair_counts, peers):
    shape = jax.ShapeDtypeStruct((1, peers), jnp.int32)
    return pl.pallas_call(
        functools.partial(plan_kernel, peers), in_specs=[SMEM] * 3, out_specs=[VMEM] * 2, out_shape=[shape] * 2
    )(owner_map, pair_blocks, pair_counts)


def relay_kernel(chain, d, count, wanted_ref, asked_ref, *refs):
    sources, outs, sems = refs[: -2 * count - 1], refs[-2 * count - 1 : -1], refs[-1]
    above_refs, below_refs = sources[:PARTS], sources[PARTS:]
    me = lax.axis_index("ex")
    place, column = me // PAIR, lax.rem(me, PAIR)

    def copies(j, blocks, source):
        made = []
        for h, ref in enumerate(blocks):
            made += [
                pltpu.make_async_copy(ref.at[asked_ref[0, source]], outs[2 * j + 1].at[h], sems.at[j, 2 * h]),
                pltpu.make_async_copy(ref.at[wanted_ref[0, source]], outs[2 * j].at[h], sems.at[j, 2 * h + 1]),
            ]
        return made

    up = copies(0, above_refs, jnp.minimum(place + d, chain - 1) * PAIR + column)
    waits = list(up)
    if below_refs:
        down = copies(0, below_refs, jnp.maximum(place - d, 0) * PAIR + column)

        @pl.when(place >= d)
        def _():
            for copy in down:
                copy.start()

        @pl.when(place < d)
        def _():
            for copy in up:
                copy.start()
    else:
        for copy in up:
            copy.start()
    if count > 1:
        waits += copies(1, above_refs, jnp.minimum(place + d, chain - 1) * PAIR + column)
        for copy in waits[len(up) :]:
            copy.start()
    for copy in waits:
        copy.wait()


def relay(wanted, asked, above, below, d, count, chain):
    blocks = [above[d, h] for h in range(PARTS)] + ([below[d, h] for h in range(PARTS)] if d else [])
    shape = jax.ShapeDtypeStruct((PARTS,) + blocks[0].shape[1:], blocks[0].dtype)
    return pl.pallas_call(
        functools.partial(relay_kernel, chain, d, count),
        in_specs=[SMEM] * 2 + [ANY] * len(blocks),
        out_specs=[VMEM] * (2 * count),
        out_shape=[shape] * (2 * count),
        scratch_shapes=[pltpu.SemaphoreType.DMA((count, 2 * PARTS))],
        cost_estimate=COST,
        compiler_params=pltpu.CompilerParams(vmem_limit_bytes=SMALL_LIMIT),
    )(wanted, asked, *blocks)


def cut_kernel(own_ref, *refs):
    outs, sems = refs[:-1], refs[-1]
    width = outs[0].shape[-1]
    copies = [
        pltpu.make_async_copy(own_ref.at[:, :, h * width : (h + 1) * width], out, sems.at[h])
        for h, out in enumerate(outs)
    ]
    for copy in copies:
        copy.start()
    for copy in copies:
        copy.wait()


def cut(own):
    shape = jax.ShapeDtypeStruct(own.shape[:2] + (own.shape[2] // PARTS,), own.dtype)
    return pl.pallas_call(
        cut_kernel,
        in_specs=[ANY],
        out_specs=[VMEM] * PARTS,
        out_shape=[shape] * PARTS,
        scratch_shapes=[pltpu.SemaphoreType.DMA((PARTS,))],
        cost_estimate=COST,
        compiler_params=pltpu.CompilerParams(vmem_limit_bytes=VMEM_LIMIT),
    )(own)


def hand_kernel(chain, notes_ref, above_ref, below_ref, *refs):
    outs, sems = refs[:-1], refs[-1]
    outs = [outs[0].at[i] for i in range(PAIR)] if len(outs) == 1 else outs
    me = lax.axis_index("ex")
    place, column = me // PAIR, lax.rem(me, PAIR)
    for ref, source, upper in ((above_ref, (chain - 1) * PAIR + column, False), (below_ref, column, True)):

        @pl.when((place >= chain // 2) == upper)
        def _():
            copies = [
                pltpu.make_async_copy(ref.at[notes_ref[i, source]], out, sems.at[i]) for i, out in enumerate(outs)
            ]
            for copy in copies:
                copy.start()
            for copy in copies:
                copy.wait()


def hand(notes, above, below, chain, stacked):
    shape = above.shape[1:]
    return pl.pallas_call(
        functools.partial(hand_kernel, chain),
        in_specs=[SMEM] + [ANY] * 2,
        out_specs=VMEM if stacked else [VMEM] * PAIR,
        out_shape=jax.ShapeDtypeStruct((PAIR,) + shape, above.dtype)
        if stacked
        else [jax.ShapeDtypeStruct(shape, above.dtype)] * PAIR,
        scratch_shapes=[pltpu.SemaphoreType.DMA((PAIR,))],
        cost_estimate=COST,
        compiler_params=pltpu.CompilerParams(vmem_limit_bytes=SMALL_LIMIT),
    )(notes, above, below)


def product_kernel(chain, full, last_parts, finish, *refs):
    blocks, refs = refs[:full], refs[full:]
    near_refs, refs = (refs[:PAIR], refs[PAIR:]) if last_parts else ((), refs)
    away_refs, refs = refs[: PAIR * len(last_parts)], refs[PAIR * len(last_parts) :]
    train_ref, refs = refs[0], refs[1:]
    rows_v, train_v, sems = refs[-3:]
    size, width = (blocks or near_refs)[0].shape[1:]
    step = min(width, STEP)
    place = lax.axis_index("ex") // PAIR
    end = jnp.logical_or(place == 0, place == chain - 1)
    chunks, near, away, starts = [], [], [], []
    for h in range(PARTS):
        if not full and h not in last_parts:
            continue
        for at in range(0, width, step):
            i = len(chunks)
            to = slice(h * width + at, h * width + at + step)

            def rows(b, source):
                return pltpu.make_async_copy(source, rows_v.at[b * size : (b + 1) * size, to], sems.at[i, b])

            copies = [pltpu.make_async_copy(train_ref.at[:, to], train_v.at[:, to], sems.at[i, full + PAIR])]
            copies += [rows(b, ref.at[h, :, at : at + step]) for b, ref in enumerate(blocks)]
            starts.append(list(copies))
            if h in last_parts:
                pair = away_refs[last_parts.index(h) * PAIR :][:PAIR]
                away.append([rows(full + b, ref.at[:, at : at + step]) for b, ref in enumerate(pair)])
                near.append([rows(full + b, ref.at[h, :, at : at + step]) for b, ref in enumerate(near_refs)])
                copies += near[-1]
            chunks.append((to, slice(0 if full else full * size, (full + PAIR * (h in last_parts)) * size), copies))

    @pl.when(end)
    def _():
        for copies in away:
            for copy in copies:
                copy.start()

    @pl.when(jnp.logical_not(end))
    def _():
        for copies in near:
            for copy in copies:
                copy.start()

    for copies in starts:
        for copy in copies:
            copy.start()

    if finish is None:
        total_ref, base = refs[0], 0
        total_ref[...] = jnp.zeros_like(total_ref)
    else:
        peers, feats, early = finish
        early_refs, (rows_ref, keep_ref, give_ref, total_ref, early_sems) = refs[:early], refs[early:-3]
        base = total_ref.shape[0] - PAIR * size
        copies, at = [], 0
        for i, ref in enumerate(early_refs):
            copies.append(pltpu.make_async_copy(ref, total_ref.at[at : at + ref.shape[0]], early_sems.at[i]))
            at += ref.shape[0]
        for copy in copies:
            copy.start()
        for copy in copies:
            copy.wait()

    for to, rows, copies in chunks:
        for copy in copies:
            copy.wait()
        total_ref[base + rows.start : base + rows.stop] += lax.dot_general(
            rows_v[rows, to], train_v[:, to], (((1,), (1,)), ((), ())), preferred_element_type=jnp.float32)
    if finish is None:
        return

    f = lax.axis_index("feat")
    core, line = lax.rem(f, 2), f // 2
    lines, each = feats // 2, peers // feats
    for away in range(lines):
        to = lax.rem(line + away, lines) * 2
        for i in range(each):
            for ref, c in ((keep_ref, core), (give_ref, 1 - core)):
                row = rows_ref[0, (to + c) * each + i]
                block = total_ref[pl.ds(pl.multiple_of(jnp.maximum(row, 0) * size, size), size), :]
                ref[away * each + i] = jnp.where(row >= 0, block, 0.0)


def product(blocks, last, away, train, chain, finish=None):
    size, width = last[0].shape[1:]
    examples, features = train.shape
    full, last_parts = len(blocks), sorted(away)
    operands = [*blocks, *(last if away else ()), *[a for h in last_parts for a in away[h]], train]
    count = (full + (PAIR if away else 0)) * size
    scratch = [
        pltpu.VMEM((count, features), train.dtype),
        pltpu.VMEM((examples, features), train.dtype),
        pltpu.SemaphoreType.DMA((PARTS * (width // min(width, STEP)), full + PAIR + 1)),
    ]
    in_specs = [ANY] * len(operands)
    if finish is None:
        out_shape, out_specs = jax.ShapeDtypeStruct((count, examples), jnp.float32), VMEM
        sizes = None
    else:
        peers, feats, early, rows = finish
        sizes = peers, feats, len(early)
        operands += [*early, rows]
        in_specs += [ANY] * len(early) + [SMEM]
        out_shape = [jax.ShapeDtypeStruct((peers // 2, size, examples), jnp.float32)] * 2
        out_specs = [VMEM] * 2
        scratch = [
            pltpu.VMEM((len(slots_of(chain)) * PAIR * size, examples), jnp.float32),
            pltpu.SemaphoreType.DMA((len(early),)),
        ] + scratch
    return pl.pallas_call(
        functools.partial(product_kernel, chain, full, last_parts, sizes),
        in_specs=in_specs,
        out_specs=out_specs,
        out_shape=out_shape,
        scratch_shapes=scratch,
        cost_estimate=COST,
        compiler_params=pltpu.CompilerParams(vmem_limit_bytes=VMEM_LIMIT),
    )(*operands)


def shards(train_grads, audit_grads, owner_map, pair_blocks, pair_counts):
    peers, feats = lax.axis_size("ex"), lax.axis_size("feat")
    chain = peers // PAIR
    own = audit_grads[:, 0]
    parts = range(PARTS)
    across = [(i, i ^ 1) for i in range(peers)]
    upward = [(i, i + PAIR) for i in range(peers - PAIR)]
    downward = [(i + PAIR, i) for i in range(peers - PAIR)]

    half = cut(own)
    above, below = {(0, h): half[h] for h in parts}, {(0, h): half[h] for h in parts}

    def along(s, h):
        below[s, h] = lax.ppermute(below[s - 1, h], "ex", upward[(s - 1) * PAIR :])
        above[s, h] = lax.ppermute(above[s - 1, h], "ex", downward[: len(downward) - (s - 1) * PAIR])

    for h in parts:
        along(1, h)
    wanted, rows = plan(owner_map, pair_blocks, pair_counts, peers)
    asked = lax.ppermute(wanted, "ex", across)
    ends = [(i, i + PAIR) for i in range(PAIR)] + [(i, i - PAIR) for i in range(peers - PAIR, peers)]
    notes = lax.ppermute(jnp.concatenate([wanted, asked]), "ex", ends)
    last = chain - 2

    slots = slots_of(chain)
    blocks = {}

    def hand_over(d):
        count = 1 + ((d, True) in slots)
        made = relay(wanted, asked, above, below, d, count, chain)
        for j in range(count):
            blocks[d, j > 0] = list(made[2 * j : 2 * j + 2])

    def receive(d):
        for second in (False, True):
            if (d, second) in slots:
                mine, theirs = blocks[d, second]
                if second:
                    theirs, blocks[d, False][1] = lax.optimization_barrier((theirs, blocks[d, False][1]))
                pairs = [(i, j) for i, j in across if not second or d <= i // PAIR < chain - d]
                blocks[d, second] = [mine, lax.ppermute(theirs, "ex", pairs)]

    hand_over(0)
    receive(0)
    hand_over(1)
    for s in range(2, chain - 1):
        for h in parts:
            if s == 2 and h == PARTS - 1:
                early = [slot for slot in slots if slot in blocks]
                gate = [blocks[slot][1] for slot in early]
                below[1, h], above[1, h], notes, gate = lax.optimization_barrier((below[1, h], above[1, h], notes, gate))
                for slot, block in zip(early, gate):
                    blocks[slot][1] = block
            along(s, h)
    receive(1)

    straight = [(j, i) for i, j in ends]
    diagonal = [(j, i ^ 1) for i, j in ends]
    beyond = [(i, j) for i, j in across if not PAIR <= i < peers - PAIR]
    both = [lax.ppermute(hand(notes, above[last, h], below[last, h], chain, True), "ex", straight) for h in parts[:-1]]
    mine, theirs = hand(notes, above[last, PARTS - 1], below[last, PARTS - 1], chain, False)
    both, mine, theirs = lax.optimization_barrier((both, mine, theirs))
    tail = {PARTS - 1: (lax.ppermute(mine, "ex", straight), lax.ppermute(theirs, "ex", diagonal))}
    away = {h: (b[0], lax.ppermute(b[1], "ex", beyond)) for h, b in enumerate(both)}

    for d in range(2, chain - 1):
        hand_over(d)
        receive(d)

    def scores(group, away, finish=None):
        return product([b for s in group for b in blocks[s]], blocks[slots[-1]], away, train_grads, chain, finish)

    early = [scores(slots[:2], {}), scores(slots[2:-1], away)]
    keep, give = scores([], tail, (peers, feats, early, rows))

    total = keep + lax.ppermute(give, "feat", [(i, i ^ 1) for i in range(feats)])
    lines, each = feats // 2, peers // feats
    result = total[:each]
    for away in range(1, lines):
        send = total[away * each : (away + 1) * each]
        result = result + lax.ppermute(send, "feat", [(i, (i + 2 * away) % feats) for i in range(feats)])
    return result[None]


def solution(mesh):
    in_specs = (P("ex", "feat"), P(None, "ex", None, "feat"), P(), P("ex", None), P("ex"))
    out_specs = P("ex", "feat", None, None)
    return jax.shard_map(shards, mesh=mesh, in_specs=in_specs, out_specs=out_specs, check_vma=False)
```

time: 168 us -> 96 us (0.57)
  waiting for transfers between devices: 112 us -> 33.9 us
  starting transfers between devices: 4.71 us -> 36.4 us
  Pallas kernels: 0 us -> 19.4 us
  blocking collectives: 13.5 us -> 0 us
  between operations: 14.1 us -> 0.94 us
  matrix products: 7.81 us -> 0 us
  local copies, waits for them, and re-layouts: 9.13 us -> 3.58 us
  other arithmetic: 6.46 us -> 1.38 us
    all_to_all x1 -> x0, waiting for transfers between devices: 91.3 us -> none  [shards(): lax.all_to_all(reply, 'ex', split_axis=0, concat_axis=0, tiled=True)]
    ppermute x0 -> x20, starting transfers between devices: none -> 36.4 us  [the longest x4 10.9 us: along(): below[s, h] = lax.ppermute(below[s - 1, h], 'ex', upward[(s - 1) * PAIR:])]
    ppermute x0 -> x20, waiting for transfers between devices: none -> 33.9 us  [the longest x4 14.9 us: along(): lax.ppermute(above[s - 1, h], 'ex', downward[:len(downward) - (s - 1) * P...]
    reduce_scatter x1 -> x0, waiting for transfers between devices: 20.9 us -> none  [shards(): lax.psum_scatter(scores * live[:, None, None], 'feat', scatter_dimension=...]
    pallas_call x0 -> x10, Pallas kernels: none -> 19.4 us  [the longest x3 13.4 us: product(): pl.pallas_call(functools.partial(product_kernel, chain, full, last_parts,...]
    all_to_all x1 -> x0, blocking collectives: 13.5 us -> none  [shards(): lax.all_to_all(wanted.reshape(peers, 1), 'ex', split_axis=0, concat_axis=...]
    gather x3 -> x0, local copies, waits for them, and re-layouts: 9.04 us -> none  [the longest x1 4.97 us: shards(): rows = jnp.take(fetched, holder, axis=0)]
    dot_general x1 -> x0, matrix products: 7.81 us -> none  [shards(): jnp.einsum('kaf,tf->kat', rows, train_grads, preferred_element_type=jnp.f...]
  transfers between devices with their start and end apart: 2 -> 20, of which waited for: 2 -> 11; matrix products, arithmetic and copies ran while one was open for 0% -> 1% of each run, Pallas kernels for 0% -> 15%
where the time goes in v3:
time: 96 us; the launch traced here: 95.6 us
  starting transfers between devices  36.4 us (38%)
  waiting for transfers between devices  33.9 us (35%)
  Pallas kernels  19.4 us (20%)
  local copies, waits for them, and re-layouts  3.58 us (4%)
  other arithmetic  1.38 us (1%)
    ppermute x4, waiting for transfers between devices, along(): lax.ppermute(above[s - 1, h], 'ex', downward[:len(downward) - (s - 1) * P...  14.9 us
    pallas_call x3, Pallas kernels, product(): pl.pallas_call(functools.partial(product_kernel, chain, full, last_parts,...  13.4 us
    ppermute x4, starting transfers between devices, along(): below[s, h] = lax.ppermute(below[s - 1, h], 'ex', upward[(s - 1) * PAIR:])  10.9 us
    ppermute x1, waiting for transfers between devices, shards(): lax.ppermute(hand(notes, above[last, h], below[last, h], chain, True), 'e...  6.22 us
    ppermute x4, starting transfers between devices, receive(): blocks[d, second] = [mine, lax.ppermute(theirs, 'ex', pairs)]  5.29 us
    ppermute x4, starting transfers between devices, along(): lax.ppermute(above[s - 1, h], 'ex', downward[:len(downward) - (s - 1) * P...  5.14 us
    ppermute x1, starting transfers between devices, shards(): notes = lax.ppermute(jnp.concatenate([wanted, asked]), 'ex', ends)  4.61 us
    ppermute x1, waiting for transfers between devices, shards(): lax.ppermute(send, 'feat', [(i, (i + 2 * away) % feats) for i in range(fe...  4.01 us
  transfers between devices with their start and end apart: 20, of which 11 were waited for; matrix products, arithmetic and copies ran while one was open for 1% of the time, Pallas kernels for 15%

profile of v3, /device:TPU:0, one launch (start us, length us, event | category | flops | bytes accessed | tf_op | source)
XLA Modules:
  0.0 95.6 jit_solution(8234971039021607223)
XLA Ops:
  0.0 1.2 %shard_map.56 = (bf16[2,32,4096]{2,1,0:T(8,128)(2,1)S(1)}, bf16[2,32,4096]{2,1,0:T(8,128)(2,1)S(1)}) custom-call(bf16[2,32,8192]{2,1,0:T(8,128)(2,1)} %bitcast.7), custom_call_target="tpu_custom_call" | custom-call | tf_op jit(solution)/shard_map/pallas_call | solution.py:123
  1.2 5.0 %collective-permute-start.3 = (bf16[2,32,4096]{2,1,0:T(8,128)(2,1)S(1)}, bf16[2,32,4096]{2,1,0:T(8,128)(2,1)S(1)}, u32[]{:S(2)}, u32[]{:S(2)}) collective-permute-start(bf16[2,32,4096]{2,1,0:T(8,128)(2,1)S(1)} %get-tuple-element.33.refs_0_), channel_id=1, source_target_pairs={{0,8},{4,12},{8,16},{12,20},{16,24},{20,28},{1,9},{5,13},{9,17},{1... | collective-permute-start | bytes 1572872 | tf_op jit(solution)/shard_map/ppermute | solution.py:300
  6.2 1.3 %collective-permute-start.1 = (bf16[2,32,4096]{2,1,0:T(8,128)(2,1)S(1)}, bf16[2,32,4096]{2,1,0:T(8,128)(2,1)S(1)}, u32[]{:S(2)}, u32[]{:S(2)}) collective-permute-start(bf16[2,32,4096]{2,1,0:T(8,128)(2,1)S(1)} %get-tuple-element.33.refs_0_), channel_id=1, source_target_pairs={{8,0},{12,4},{16,8},{20,12},{24,16},{28,20},{9,1},{13,5},{17,9},{2... | collective-permute-start | bytes 1572872 | tf_op jit(solution)/shard_map/ppermute | solution.py:301
  7.5 4.6 %collective-permute-start.4 = (bf16[2,32,4096]{2,1,0:T(8,128)(2,1)S(1)}, bf16[2,32,4096]{2,1,0:T(8,128)(2,1)S(1)}, u32[]{:S(2)}, u32[]{:S(2)}) collective-permute-start(bf16[2,32,4096]{2,1,0:T(8,128)(2,1)S(1)} %get-tuple-element.34.refs_1_), channel_id=1, source_target_pairs={{0,8},{4,12},{8,16},{12,20},{16,24},{20,28},{1,9},{5,13},{9,17},{1... | collective-permute-start | bytes 1572872 | tf_op jit(solution)/shard_map/ppermute | solution.py:300
  12.1 1.3 %collective-permute-start.2 = (bf16[2,32,4096]{2,1,0:T(8,128)(2,1)S(1)}, bf16[2,32,4096]{2,1,0:T(8,128)(2,1)S(1)}, u32[]{:S(2)}, u32[]{:S(2)}) collective-permute-start(bf16[2,32,4096]{2,1,0:T(8,128)(2,1)S(1)} %get-tuple-element.34.refs_1_), channel_id=1, source_target_pairs={{8,0},{12,4},{16,8},{20,12},{24,16},{28,20},{9,1},{13,5},{17,9},{2... | collective-permute-start | bytes 1572872 | tf_op jit(solution)/shard_map/ppermute | solution.py:301
  14.0 1.4 %shard_map.55 = (s32[1,8]{1,0:T(1,128)}, s32[1,8]{1,0:T(1,128)}) custom-call(s32[16]{0:T(128)} %owner_ref.1, s32[1,8]{1,0:T(1,128)} %pairs_ref.1, s32[1]{0:T(128)S(6)} %copy.6.counts_ref), custom_call_target="tpu_custom_call" | custom-call | tf_op jit(solution)/shard_map/pallas_call | solution.py:49
  15.4 1.5 %collective-permute-start = (s32[1,8]{1,0:T(1,128)}, s32[1,8]{1,0:T(1,128)S(1)}, u32[]{:S(2)}, u32[]{:S(2)}) collective-permute-start(s32[1,8]{1,0:T(1,128)} %get-tuple-element.32.wanted_ref), channel_id=1, source_target_pairs={{0,4},{4,0},{8,12},{12,8},{16,20},{20,16},{24,28},{28,24},{1,5},{5... | collective-permute-start | bytes 104 | tf_op jit(solution)/shard_map/ppermute | solution.py:306
  16.9 2.2 %collective-permute-done.asked_ref = s32[1,8]{1,0:T(1,128)S(1)} collective-permute-done((s32[1,8]{1,0:T(1,128)}, s32[1,8]{1,0:T(1,128)S(1)}, u32[]{:S(2)}, u32[]{:S(2)}) %collective-permute-start) | collective-permute-done | bytes 64 | tf_op jit(solution)/shard_map/ppermute | solution.py:306
  20.4 1.6 %collective-permute-start.6 = (bf16[2,32,4096]{2,1,0:T(8,128)(2,1)S(1)}, bf16[2,32,4096]{2,1,0:T(8,128)(2,1)S(1)}, u32[]{:S(2)}, u32[]{:S(2)}) collective-permute-start(bf16[2,32,4096]{2,1,0:T(8,128)(2,1)S(1)} %get-tuple-element.36), channel_id=1, source_target_pairs={{0,4},{4,0},{8,12},{12,8},{16,20},{20,16},{24,28},{28,24},{1,5},{5... | collective-permute-start | bytes 1572872 | tf_op jit(solution)/shard_map/ppermute | solution.py:327
  22.9 1.3 %collective-permute-start.9 = (bf16[2,32,4096]{2,1,0:T(8,128)(2,1)S(1)}, bf16[2,32,4096]{2,1,0:T(8,128)(2,1)S(1)}, u32[]{:S(2)}, u32[]{:S(2)}) collective-permute-start(bf16[2,32,4096]{2,1,0:T(8,128)(2,1)S(1)} %collective-permute-done.1.refs_0_), channel_id=1, source_target_pairs={{8,0},{12,4},{16,8},{20,12},{9,1},{13,5},{17,9},{21,13},{10,2},{14... | collective-permute-start | bytes 1572872 | tf_op jit(solution)/shard_map/ppermute | solution.py:301
  24.9 3.7 %collective-permute-done.4.refs_3_ = bf16[2,32,4096]{2,1,0:T(8,128)(2,1)S(1)} collective-permute-done((bf16[2,32,4096]{2,1,0:T(8,128)(2,1)S(1)}, bf16[2,32,4096]{2,1,0:T(8,128)(2,1)S(1)}, u32[]{:S(2)}, u32[]{:S(2)}) %collective-permute-start.4) | collective-permute-done | bytes 524320 | tf_op jit(solution)/shard_map/ppermute | solution.py:300
  28.6 4.6 %collective-permute-start.5 = (s32[2,8]{1,0:T(2,128)S(1)}, s32[2,8]{1,0:T(2,128)S(1)}, u32[]{:S(2)}, u32[]{:S(2)}) collective-permute-start(s32[2,8]{1,0:T(2,128)S(1)} %pad_add_fusion), channel_id=1, source_target_pairs={{0,8},{4,12},{24,16},{28,20},{1,9},{5,13},{25,17},{29,21},{2,10},{... | collective-permute-start | bytes 200 | tf_op jit(solution)/shard_map/ppermute | solution.py:308
  33.2 1.0 %collective-permute-done.2.refs_1_ = bf16[2,32,4096]{2,1,0:T(8,128)(2,1)S(1)} collective-permute-done((bf16[2,32,4096]{2,1,0:T(8,128)(2,1)S(1)}, bf16[2,32,4096]{2,1,0:T(8,128)(2,1)S(1)}, u32[]{:S(2)}, u32[]{:S(2)}) %collective-permute-start.2) | collective-permute-done | bytes 524320 | tf_op jit(solution)/shard_map/ppermute | solution.py:301
  34.8 0.8 shard_map.57
  35.7 0.8 copy-done
  36.4 1.5 %collective-permute-start.7 = (bf16[2,32,4096]{2,1,0:T(8,128)(2,1)S(1)}, bf16[2,32,4096]{2,1,0:T(8,128)(2,1)S(1)}, u32[]{:S(2)}, u32[]{:S(2)}) collective-permute-start(bf16[2,32,4096]{2,1,0:T(8,128)(2,1)S(1)} %get-tuple-element.40), channel_id=1, source_target_pairs={{0,4},{4,0},{8,12},{12,8},{16,20},{20,16},{24,28},{28,24},{1,5},{5... | collective-permute-start | bytes 1572872 | tf_op jit(solution)/shard_map/ppermute | solution.py:327
  37.9 1.3 %collective-permute-start.12 = (bf16[2,32,4096]{2,1,0:T(8,128)(2,1)S(1)}, bf16[2,32,4096]{2,1,0:T(8,128)(2,1)S(1)}, u32[]{:S(2)}, u32[]{:S(2)}) collective-permute-start(bf16[2,32,4096]{2,1,0:T(8,128)(2,1)S(1)} %collective-permute-done.2.refs_1_), channel_id=1, source_target_pairs={{8,0},{12,4},{16,8},{20,12},{9,1},{13,5},{17,9},{21,13},{10,2},{14... | collective-permute-start | bytes 1572872 | tf_op jit(solution)/shard_map/ppermute | solution.py:301
  39.9 5.5 %collective-permute-done.9.above_ref.refs_0_ = bf16[2,32,4096]{2,1,0:T(8,128)(2,1)S(1)} collective-permute-done((bf16[2,32,4096]{2,1,0:T(8,128)(2,1)S(1)}, bf16[2,32,4096]{2,1,0:T(8,128)(2,1)S(1)}, u32[]{:S(2)}, u32[]{:S(2)}) %collective-permute-start.9) | collective-permute-done | bytes 524320 | tf_op jit(solution)/shard_map/ppermute | solution.py:301
  46.0 1.3 %collective-permute-start.11 = (bf16[2,32,4096]{2,1,0:T(8,128)(2,1)S(1)}, bf16[2,32,4096]{2,1,0:T(8,128)(2,1)S(1)}, u32[]{:S(2)}, u32[]{:S(2)}) collective-permute-start(bf16[2,32,4096]{2,1,0:T(8,128)(2,1)S(1)} %shard_map.59), channel_id=1, source_target_pairs={{8,0},{12,4},{16,24},{20,28},{9,1},{13,5},{17,25},{21,29},{10,2},{... | collective-permute-start | bytes 1572872 | tf_op jit(solution)/shard_map/ppermute | solution.py:346
  48.4 8.2 %collective-permute-done.12.above_ref.refs_1_ = bf16[2,32,4096]{2,1,0:T(8,128)(2,1)S(1)} collective-permute-done((bf16[2,32,4096]{2,1,0:T(8,128)(2,1)S(1)}, bf16[2,32,4096]{2,1,0:T(8,128)(2,1)S(1)}, u32[]{:S(2)}, u32[]{:S(2)}) %collective-permute-start.12) | collective-permute-done | bytes 524320 | tf_op jit(solution)/shard_map/ppermute | solution.py:301
  58.0 1.6 %collective-permute-start.16 = (bf16[2,32,4096]{2,1,0:T(8,128)(2,1)S(1)}, bf16[2,32,4096]{2,1,0:T(8,128)(2,1)S(1)}, u32[]{:S(2)}, u32[]{:S(2)}) collective-permute-start(bf16[2,32,4096]{2,1,0:T(8,128)(2,1)S(1)} %get-tuple-element.54), channel_id=1, source_target_pairs={{0,4},{4,0},{8,12},{12,8},{16,20},{20,16},{24,28},{28,24},{1,5},{5... | collective-permute-start | bytes 1572872 | tf_op jit(solution)/shard_map/ppermute | solution.py:327
  60.2 6.2 %collective-permute-done.11 = bf16[2,32,4096]{2,1,0:T(8,128)(2,1)S(1)} collective-permute-done((bf16[2,32,4096]{2,1,0:T(8,128)(2,1)S(1)}, bf16[2,32,4096]{2,1,0:T(8,128)(2,1)S(1)}, u32[]{:S(2)}, u32[]{:S(2)}) %collective-permute-start.11) | collective-permute-done | bytes 524320 | tf_op jit(solution)/shard_map/ppermute | solution.py:346
  66.5 3.4 %collective-permute-start.17 = (bf16[32,4096]{1,0:T(8,128)(2,1)S(1)}, bf16[32,4096]{1,0:T(8,128)(2,1)S(1)}, u32[]{:S(2)}, u32[]{:S(2)}) collective-permute-start(bf16[32,4096]{1,0:T(8,128)(2,1)S(1)} %get-tuple-element.59), channel_id=1, source_target_pairs={{0,4},{4,0},{24,28},{28,24},{1,5},{5,1},{25,29},{29,25},{2,6},{6,2... | collective-permute-start | bytes 786440 | tf_op jit(solution)/shard_map/ppermute | solution.py:350
  69.9 1.3 %collective-permute-start.14 = (bf16[32,4096]{1,0:T(8,128)(2,1)S(1)}, bf16[32,4096]{1,0:T(8,128)(2,1)S(1)}, u32[]{:S(2)}, u32[]{:S(2)}) collective-permute-start(bf16[32,4096]{1,0:T(8,128)(2,1)S(1)} %get-tuple-element.47), channel_id=1, source_target_pairs={{8,0},{12,4},{16,24},{20,28},{9,1},{13,5},{17,25},{21,29},{10,2},{... | collective-permute-start | bytes 786440 | tf_op jit(solution)/shard_map/ppermute | solution.py:349
  71.2 1.3 %collective-permute-start.15 = (bf16[32,4096]{1,0:T(8,128)(2,1)S(1)}, bf16[32,4096]{1,0:T(8,128)(2,1)S(1)}, u32[]{:S(2)}, u32[]{:S(2)}) collective-permute-start(bf16[32,4096]{1,0:T(8,128)(2,1)S(1)} %get-tuple-element.48), channel_id=1, source_target_pairs={{8,4},{12,0},{16,28},{20,24},{9,5},{13,1},{17,29},{21,25},{10,6},{... | collective-permute-start | bytes 786440 | tf_op jit(solution)/shard_map/ppermute | solution.py:349
  72.5 4.9 %shard_map.61.refs_5_ = f32[128,512]{1,0:T(8,128)S(1)} custom-call(bf16[2,32,4096]{2,1,0:T(8,128)(2,1)S(1)} %get-tuple-element.49.refs_0_, bf16[2,32,4096]{2,1,0:T(8,128)(2,1)S(1)} %collective-permute-done.6.refs_1_, bf16[2,32,4096]{2,1,0:T(8,128)(2,1)S(1)} %get-tuple-element.51.refs_2_, bf16[2,32,4096]{2,1,0:T(8,128)(2,1)} %copy-done.6, ...), custom_call_target="tpu_custom_call" | custom-call | tf_op jit(solution)/shard_map/pallas_call | solution.py:276
  78.2 4.8 %shard_map.63.refs_6_ = f32[128,512]{1,0:T(8,128)S(1)} custom-call(bf16[2,32,4096]{2,1,0:T(8,128)(2,1)S(1)} %get-tuple-element.53.refs_0_, bf16[2,32,4096]{2,1,0:T(8,128)(2,1)S(1)} %collective-permute-done.16.refs_1_, bf16[2,32,4096]{2,1,0:T(8,128)(2,1)} %copy-done, bf16[2,32,4096]{2,1,0:T(8,128)(2,1)} %copy-done.5, ...), custom_call_target="tpu_custom_call" | custom-call | tf_op jit(solution)/shard_map/pallas_call | solution.py:276
  83.0 0.9 collective-permute-done.15.refs_3_
  83.9 3.7 %shard_map.64 = (f32[4,32,512]{2,1,0:T(8,128)S(1)}, f32[4,32,512]{2,1,0:T(8,128)S(1)}) custom-call(bf16[2,32,4096]{2,1,0:T(8,128)(2,1)} %copy-done, bf16[2,32,4096]{2,1,0:T(8,128)(2,1)} %copy-done.5, bf16[32,4096]{1,0:T(8,128)(2,1)S(1)} %collective-permute-done.14.refs_2_, bf16[32,4096]{1,0:T(8,128)(2,1)S(1)} %collective-permute-done.15.refs_3_, ...), custom_call_target="tpu_custom_call" | custom-call | tf_op jit(solution)/shard_map/pallas_call | solution.py:276
  87.7 1.5 %collective-permute-done.18 = f32[4,32,512]{2,1,0:T(8,128)S(1)} collective-permute-done((f32[4,32,512]{2,1,0:T(8,128)S(1)}, f32[4,32,512]{2,1,0:T(8,128)S(1)}, u32[]{:S(2)}, u32[]{:S(2)}) %collective-permute-start.18) | collective-permute-done | bytes 262176 | tf_op jit(solution)/shard_map/ppermute | solution.py:362
  89.3 1.6 %collective-permute-start.19 = (f32[2,32,512]{2,1,0:T(8,128)S(1)}, f32[2,32,512]{2,1,0:T(8,128)S(1)}, u32[]{:S(2)}, u32[]{:S(2)}) collective-permute-start(f32[2,32,512]{2,1,0:T(8,128)S(1)} %slice.17), channel_id=1, source_target_pairs={{0,2},{1,3},{2,0},{3,1},{4,6},{5,7},{6,4},{7,5},{8,10},{9,11},{10,... | collective-permute-start | bytes 393224 | tf_op jit(solution)/shard_map/ppermute | solution.py:367
  90.9 4.0 %collective-permute-done.19 = f32[2,32,512]{2,1,0:T(8,128)S(1)} collective-permute-done((f32[2,32,512]{2,1,0:T(8,128)S(1)}, f32[2,32,512]{2,1,0:T(8,128)S(1)}, u32[]{:S(2)}, u32[]{:S(2)}) %collective-permute-start.19) | collective-permute-done | bytes 131104 | tf_op jit(solution)/shard_map/ppermute | solution.py:367
  (37 shorter events, 9.6 us)
Async XLA Ops:
  1.2 20.8 %collective-permute-start.3 = (bf16[2,32,4096]{2,1,0:T(8,128)(2,1)S(1)}, bf16[2,32,4096]{2,1,0:T(8,128)(2,1)S(1)}, u32[]{:S(2)}, u32[]{:S(2)}) collective-permute-start(bf16[2,32,4096]{2,1,0:T(8,128)(2,1)S(1)} %get-tuple-element.33.refs_0_), channel_id=1, source_target_pairs={{0,8},{4,12},{8,16},{12,20},{16,24},{20,28},{1,9},{5,13},{9,17},{1... | collective-permute-start | bytes 1572872 | tf_op jit(solution)/shard_map/ppermute | solution.py:300
  6.2 16.7 %collective-permute-start.1 = (bf16[2,32,4096]{2,1,0:T(8,128)(2,1)S(1)}, bf16[2,32,4096]{2,1,0:T(8,128)(2,1)S(1)}, u32[]{:S(2)}, u32[]{:S(2)}) collective-permute-start(bf16[2,32,4096]{2,1,0:T(8,128)(2,1)S(1)} %get-tuple-element.33.refs_0_), channel_id=1, source_target_pairs={{8,0},{12,4},{16,8},{20,12},{24,16},{28,20},{9,1},{13,5},{17,9},{2... | collective-permute-start | bytes 1572872 | tf_op jit(solution)/shard_map/ppermute | solution.py:301
  7.5 21.1 %collective-permute-start.4 = (bf16[2,32,4096]{2,1,0:T(8,128)(2,1)S(1)}, bf16[2,32,4096]{2,1,0:T(8,128)(2,1)S(1)}, u32[]{:S(2)}, u32[]{:S(2)}) collective-permute-start(bf16[2,32,4096]{2,1,0:T(8,128)(2,1)S(1)} %get-tuple-element.34.refs_1_), channel_id=1, source_target_pairs={{0,8},{4,12},{8,16},{12,20},{16,24},{20,28},{1,9},{5,13},{9,17},{1... | collective-permute-start | bytes 1572872 | tf_op jit(solution)/shard_map/ppermute | solution.py:300
  12.1 22.1 %collective-permute-start.2 = (bf16[2,32,4096]{2,1,0:T(8,128)(2,1)S(1)}, bf16[2,32,4096]{2,1,0:T(8,128)(2,1)S(1)}, u32[]{:S(2)}, u32[]{:S(2)}) collective-permute-start(bf16[2,32,4096]{2,1,0:T(8,128)(2,1)S(1)} %get-tuple-element.34.refs_1_), channel_id=1, source_target_pairs={{8,0},{12,4},{16,8},{20,12},{24,16},{28,20},{9,1},{13,5},{17,9},{2... | collective-permute-start | bytes 1572872 | tf_op jit(solution)/shard_map/ppermute | solution.py:301
  15.4 3.7 %collective-permute-start = (s32[1,8]{1,0:T(1,128)}, s32[1,8]{1,0:T(1,128)S(1)}, u32[]{:S(2)}, u32[]{:S(2)}) collective-permute-start(s32[1,8]{1,0:T(1,128)} %get-tuple-element.32.wanted_ref), channel_id=1, source_target_pairs={{0,4},{4,0},{8,12},{12,8},{16,20},{20,16},{24,28},{28,24},{1,5},{5... | collective-permute-start | bytes 104 | tf_op jit(solution)/shard_map/ppermute | solution.py:306
  19.1 0.7 copy-start.1
  20.4 16.0 %collective-permute-start.6 = (bf16[2,32,4096]{2,1,0:T(8,128)(2,1)S(1)}, bf16[2,32,4096]{2,1,0:T(8,128)(2,1)S(1)}, u32[]{:S(2)}, u32[]{:S(2)}) collective-permute-start(bf16[2,32,4096]{2,1,0:T(8,128)(2,1)S(1)} %get-tuple-element.36), channel_id=1, source_target_pairs={{0,4},{4,0},{8,12},{12,8},{16,20},{20,16},{24,28},{28,24},{1,5},{5... | collective-permute-start | bytes 1572872 | tf_op jit(solution)/shard_map/ppermute | solution.py:327
  22.0 17.9 %collective-permute-start.10 = (bf16[2,32,4096]{2,1,0:T(8,128)(2,1)S(1)}, bf16[2,32,4096]{2,1,0:T(8,128)(2,1)S(1)}, u32[]{:S(2)}, u32[]{:S(2)}) collective-permute-start(bf16[2,32,4096]{2,1,0:T(8,128)(2,1)S(1)} %collective-permute-done.3.refs_2_), channel_id=1, source_target_pairs={{8,16},{12,20},{16,24},{20,28},{9,17},{13,21},{17,25},{21,29},{10,... | collective-permute-start | bytes 1572872 | tf_op jit(solution)/shard_map/ppermute | solution.py:300
  22.9 22.5 %collective-permute-start.9 = (bf16[2,32,4096]{2,1,0:T(8,128)(2,1)S(1)}, bf16[2,32,4096]{2,1,0:T(8,128)(2,1)S(1)}, u32[]{:S(2)}, u32[]{:S(2)}) collective-permute-start(bf16[2,32,4096]{2,1,0:T(8,128)(2,1)S(1)} %collective-permute-done.1.refs_0_), channel_id=1, source_target_pairs={{8,0},{12,4},{16,8},{20,12},{9,1},{13,5},{17,9},{21,13},{10,2},{14... | collective-permute-start | bytes 1572872 | tf_op jit(solution)/shard_map/ppermute | solution.py:301
  28.6 7.9 %collective-permute-start.5 = (s32[2,8]{1,0:T(2,128)S(1)}, s32[2,8]{1,0:T(2,128)S(1)}, u32[]{:S(2)}, u32[]{:S(2)}) collective-permute-start(s32[2,8]{1,0:T(2,128)S(1)} %pad_add_fusion), channel_id=1, source_target_pairs={{0,8},{4,12},{24,16},{28,20},{1,9},{5,13},{25,17},{29,21},{2,10},{... | collective-permute-start | bytes 200 | tf_op jit(solution)/shard_map/ppermute | solution.py:308
  34.2 0.7 copy-start.2
  35.6 0.8 copy-start
  36.4 11.3 %collective-permute-start.7 = (bf16[2,32,4096]{2,1,0:T(8,128)(2,1)S(1)}, bf16[2,32,4096]{2,1,0:T(8,128)(2,1)S(1)}, u32[]{:S(2)}, u32[]{:S(2)}) collective-permute-start(bf16[2,32,4096]{2,1,0:T(8,128)(2,1)S(1)} %get-tuple-element.40), channel_id=1, source_target_pairs={{0,4},{4,0},{8,12},{12,8},{16,20},{20,16},{24,28},{28,24},{1,5},{5... | collective-permute-start | bytes 1572872 | tf_op jit(solution)/shard_map/ppermute | solution.py:327
  37.9 18.7 %collective-permute-start.12 = (bf16[2,32,4096]{2,1,0:T(8,128)(2,1)S(1)}, bf16[2,32,4096]{2,1,0:T(8,128)(2,1)S(1)}, u32[]{:S(2)}, u32[]{:S(2)}) collective-permute-start(bf16[2,32,4096]{2,1,0:T(8,128)(2,1)S(1)} %collective-permute-done.2.refs_1_), channel_id=1, source_target_pairs={{8,0},{12,4},{16,8},{20,12},{9,1},{13,5},{17,9},{21,13},{10,2},{14... | collective-permute-start | bytes 1572872 | tf_op jit(solution)/shard_map/ppermute | solution.py:301
  39.2 17.4 %collective-permute-start.13 = (bf16[2,32,4096]{2,1,0:T(8,128)(2,1)S(1)}, bf16[2,32,4096]{2,1,0:T(8,128)(2,1)S(1)}, u32[]{:S(2)}, u32[]{:S(2)}) collective-permute-start(bf16[2,32,4096]{2,1,0:T(8,128)(2,1)S(1)} %collective-permute-done.4.refs_3_), channel_id=1, source_target_pairs={{8,16},{12,20},{16,24},{20,28},{9,17},{13,21},{17,25},{21,29},{10,... | collective-permute-start | bytes 1572872 | tf_op jit(solution)/shard_map/ppermute | solution.py:300
  46.0 20.4 %collective-permute-start.11 = (bf16[2,32,4096]{2,1,0:T(8,128)(2,1)S(1)}, bf16[2,32,4096]{2,1,0:T(8,128)(2,1)S(1)}, u32[]{:S(2)}, u32[]{:S(2)}) collective-permute-start(bf16[2,32,4096]{2,1,0:T(8,128)(2,1)S(1)} %shard_map.59), channel_id=1, source_target_pairs={{8,0},{12,4},{16,24},{20,28},{9,1},{13,5},{17,25},{21,29},{10,2},{... | collective-permute-start | bytes 1572872 | tf_op jit(solution)/shard_map/ppermute | solution.py:346
  47.7 24.7 %copy-start.6 = (bf16[2,32,4096]{2,1,0:T(8,128)(2,1)}, bf16[2,32,4096]{2,1,0:T(8,128)(2,1)S(1)}, u32[]{:S(2)}) copy-start(bf16[2,32,4096]{2,1,0:T(8,128)(2,1)S(1)} %collective-permute-done.7.refs_3_) | copy-start | bytes 1572868
  47.7 29.6 %collective-permute-start.8 = (bf16[2,32,4096]{2,1,0:T(8,128)(2,1)S(1)}, bf16[2,32,4096]{2,1,0:T(8,128)(2,1)S(1)}, u32[]{:S(2)}, u32[]{:S(2)}) collective-permute-start(bf16[2,32,4096]{2,1,0:T(8,128)(2,1)S(1)} %get-tuple-element.41), channel_id=1, source_target_pairs={{8,12},{12,8},{16,20},{20,16},{9,13},{13,9},{17,21},{21,17},{10,14... | collective-permute-start | bytes 1572872 | tf_op jit(solution)/shard_map/ppermute | solution.py:327
  56.6 0.7 copy-start.3
  58.0 19.4 %collective-permute-start.16 = (bf16[2,32,4096]{2,1,0:T(8,128)(2,1)S(1)}, bf16[2,32,4096]{2,1,0:T(8,128)(2,1)S(1)}, u32[]{:S(2)}, u32[]{:S(2)}) collective-permute-start(bf16[2,32,4096]{2,1,0:T(8,128)(2,1)S(1)} %get-tuple-element.54), channel_id=1, source_target_pairs={{0,4},{4,0},{8,12},{12,8},{16,20},{20,16},{24,28},{28,24},{1,5},{5... | collective-permute-start | bytes 1572872 | tf_op jit(solution)/shard_map/ppermute | solution.py:327
  66.5 10.9 %collective-permute-start.17 = (bf16[32,4096]{1,0:T(8,128)(2,1)S(1)}, bf16[32,4096]{1,0:T(8,128)(2,1)S(1)}, u32[]{:S(2)}, u32[]{:S(2)}) collective-permute-start(bf16[32,4096]{1,0:T(8,128)(2,1)S(1)} %get-tuple-element.59), channel_id=1, source_target_pairs={{0,4},{4,0},{24,28},{28,24},{1,5},{5,1},{25,29},{29,25},{2,6},{6,2... | collective-permute-start | bytes 786440 | tf_op jit(solution)/shard_map/ppermute | solution.py:350
  69.9 13.1 %collective-permute-start.14 = (bf16[32,4096]{1,0:T(8,128)(2,1)S(1)}, bf16[32,4096]{1,0:T(8,128)(2,1)S(1)}, u32[]{:S(2)}, u32[]{:S(2)}) collective-permute-start(bf16[32,4096]{1,0:T(8,128)(2,1)S(1)} %get-tuple-element.47), channel_id=1, source_target_pairs={{8,0},{12,4},{16,24},{20,28},{9,1},{13,5},{17,25},{21,29},{10,2},{... | collective-permute-start | bytes 786440 | tf_op jit(solution)/shard_map/ppermute | solution.py:349
  71.2 12.8 %collective-permute-start.15 = (bf16[32,4096]{1,0:T(8,128)(2,1)S(1)}, bf16[32,4096]{1,0:T(8,128)(2,1)S(1)}, u32[]{:S(2)}, u32[]{:S(2)}) collective-permute-start(bf16[32,4096]{1,0:T(8,128)(2,1)S(1)} %get-tuple-element.48), channel_id=1, source_target_pairs={{8,4},{12,0},{16,28},{20,24},{9,5},{13,1},{17,29},{21,25},{10,6},{... | collective-permute-start | bytes 786440 | tf_op jit(solution)/shard_map/ppermute | solution.py:349
  72.5 11.5 %copy-start.4 = (s32[1,8]{1,0:T(1,128)S(1)}, s32[1,8]{1,0:T(1,128)}, u32[]{:S(2)}) copy-start(s32[1,8]{1,0:T(1,128)} %get-tuple-element.56.refs_7_) | copy-start | bytes 100
  77.4 0.8 copy-start.5
  87.6 1.6 %collective-permute-start.18 = (f32[4,32,512]{2,1,0:T(8,128)S(1)}, f32[4,32,512]{2,1,0:T(8,128)S(1)}, u32[]{:S(2)}, u32[]{:S(2)}) collective-permute-start(f32[4,32,512]{2,1,0:T(8,128)S(1)} %get-tuple-element.58), channel_id=1, source_target_pairs={{0,1},{1,0},{2,3},{3,2},{4,5},{5,4},{6,7},{7,6},{8,9},{9,8},{10,11... | collective-permute-start | bytes 786440 | tf_op jit(solution)/shard_map/ppermute | solution.py:362
  89.3 5.6 %collective-permute-start.19 = (f32[2,32,512]{2,1,0:T(8,128)S(1)}, f32[2,32,512]{2,1,0:T(8,128)S(1)}, u32[]{:S(2)}, u32[]{:S(2)}) collective-permute-start(f32[2,32,512]{2,1,0:T(8,128)S(1)} %slice.17), channel_id=1, source_target_pairs={{0,2},{1,3},{2,0},{3,1},{4,6},{5,7},{6,4},{7,5},{8,10},{9,11},{10,... | collective-permute-start | bytes 393224 | tf_op jit(solution)/shard_map/ppermute | solution.py:367

commit v4 on v3

--- a/solution.py
+++ b/solution.py
@@ -317,12 +317,12 @@
         for j in range(count):
             blocks[d, j > 0] = list(made[2 * j : 2 * j + 2])
 
-    def receive(d):
+    def receive(d, after=()):
         for second in (False, True):
             if (d, second) in slots:
                 mine, theirs = blocks[d, second]
                 if second:
-                    theirs, blocks[d, False][1] = lax.optimization_barrier((theirs, blocks[d, False][1]))
+                    theirs, blocks[d, False][1], after = lax.optimization_barrier((theirs, blocks[d, False][1], after))
                 pairs = [(i, j) for i, j in across if not second or d <= i // PAIR < chain - d]
                 blocks[d, second] = [mine, lax.ppermute(theirs, "ex", pairs)]
 
@@ -338,16 +338,22 @@
                 for slot, block in zip(early, gate):
                     blocks[slot][1] = block
             along(s, h)
-    receive(1)
 
     straight = [(j, i) for i, j in ends]
     diagonal = [(j, i ^ 1) for i, j in ends]
     beyond = [(i, j) for i, j in across if not PAIR <= i < peers - PAIR]
-    both = [lax.ppermute(hand(notes, above[last, h], below[last, h], chain, True), "ex", straight) for h in parts[:-1]]
-    mine, theirs = hand(notes, above[last, PARTS - 1], below[last, PARTS - 1], chain, False)
-    both, mine, theirs = lax.optimization_barrier((both, mine, theirs))
-    tail = {PARTS - 1: (lax.ppermute(mine, "ex", straight), lax.ppermute(theirs, "ex", diagonal))}
-    away = {h: (b[0], lax.ppermute(b[1], "ex", beyond)) for h, b in enumerate(both)}
+    away = {}
+    for h in parts:
+        up, down = above[last, h], below[last, h]
+        if h > 0:
+            mine, theirs = away[h - 1]
+            up, down, theirs = lax.optimization_barrier((up, down, theirs))
+            away[h - 1] = mine, theirs
+        mine, theirs = hand(notes, up, down, chain, False)
+        if h == 0:
+            receive(1, (mine, theirs))
+        away[h] = lax.ppermute(mine, "ex", straight), lax.ppermute(theirs, "ex", diagonal)
+    tail = {PARTS - 1: away.pop(PARTS - 1)}
 
     for d in range(2, chain - 1):
         hand_over(d)

time: 96 us -> 92.1 us (0.959)
  waiting for transfers between devices: 33.9 us -> 31.6 us
    ppermute x2 -> x0, waiting for transfers between devices: 6.22 us -> none  [the longest x1 6.22 us: shards(): lax.ppermute(hand(notes, above[last, h], below[last, h], chain, True), 'e...]
    ppermute x2 -> x0, starting transfers between devices: 4.69 us -> none  [the longest x1 3.4 us: shards(): lax.ppermute(b[1], 'ex', beyond)]
    ppermute x4, waiting for transfers between devices: 14.9 us -> 19.6 us  [along(): lax.ppermute(above[s - 1, h], 'ex', downward[:len(downward) - (s - 1) * P...]
    ppermute x4, waiting for transfers between devices: 3.68 us -> 0.01 us  [along(): below[s, h] = lax.ppermute(below[s - 1, h], 'ex', upward[(s - 1) * PAIR:])]
    ppermute x4, waiting for transfers between devices: 0.4 us -> 3.31 us  [receive(): blocks[d, second] = [mine, lax.ppermute(theirs, 'ex', pairs)]]
    ppermute x1 -> x2, starting transfers between devices: 1.29 us -> 2.58 us  [shards(): lax.ppermute(theirs, 'ex', diagonal)]
    ppermute x1 -> x2, starting transfers between devices: 1.29 us -> 2.57 us  [shards(): lax.ppermute(mine, 'ex', straight)]
    ppermute x1, starting transfers between devices: 4.61 us -> 3.42 us  [shards(): notes = lax.ppermute(jnp.concatenate([wanted, asked]), 'ex', ends)]
  transfers between devices with their start and end apart: 20 -> 20, of which waited for: 11 -> 10; matrix products, arithmetic and copies ran while one was open for 1% -> 1% of each run, Pallas kernels for 15% -> 16%
where the time goes in v4:
time: 92.1 us; the launch traced here: 91.7 us
  starting transfers between devices  35.5 us (39%)
  waiting for transfers between devices  31.6 us (34%)
  Pallas kernels  19.4 us (21%)
  local copies, waits for them, and re-layouts  2.77 us (3%)
  other arithmetic  1.37 us (1%)
  between operations  0.94 us (1%)
    ppermute x4, waiting for transfers between devices, along(): lax.ppermute(above[s - 1, h], 'ex', downward[:len(downward) - (s - 1) * P...  19.6 us
    pallas_call x3, Pallas kernels, product(): pl.pallas_call(functools.partial(product_kernel, chain, full, last_parts,...  13.4 us
    ppermute x4, starting transfers between devices, along(): below[s, h] = lax.ppermute(below[s - 1, h], 'ex', upward[(s - 1) * PAIR:])  11.6 us
    ppermute x4, starting transfers between devices, receive(): blocks[d, second] = [mine, lax.ppermute(theirs, 'ex', pairs)]  6.05 us
    ppermute x4, starting transfers between devices, along(): lax.ppermute(above[s - 1, h], 'ex', downward[:len(downward) - (s - 1) * P...  5.14 us
    ppermute x1, waiting for transfers between devices, shards(): lax.ppermute(send, 'feat', [(i, (i + 2 * away) % feats) for i in range(fe...  3.8 us
    ppermute x1, starting transfers between devices, shards(): notes = lax.ppermute(jnp.concatenate([wanted, asked]), 'ex', ends)  3.42 us
    ppermute x4, waiting for transfers between devices, receive(): blocks[d, second] = [mine, lax.ppermute(theirs, 'ex', pairs)]  3.31 us
  transfers between devices with their start and end apart: 20, of which 10 were waited for; matrix products, arithmetic and copies ran while one was open for 1% of the time, Pallas kernels for 16%

profile of v4, /device:TPU:0, one launch (start us, length us, event | category | flops | bytes accessed | tf_op | source)
XLA Modules:
  0.0 91.7 jit_solution(9544525441922283103)
XLA Ops:
  0.0 1.2 %shard_map.56 = (bf16[2,32,4096]{2,1,0:T(8,128)(2,1)S(1)}, bf16[2,32,4096]{2,1,0:T(8,128)(2,1)S(1)}) custom-call(bf16[2,32,8192]{2,1,0:T(8,128)(2,1)} %bitcast.3), custom_call_target="tpu_custom_call" | custom-call | tf_op jit(solution)/shard_map/pallas_call | solution.py:123
  1.2 1.3 %collective-permute-start.1 = (bf16[2,32,4096]{2,1,0:T(8,128)(2,1)S(1)}, bf16[2,32,4096]{2,1,0:T(8,128)(2,1)S(1)}, u32[]{:S(2)}, u32[]{:S(2)}) collective-permute-start(bf16[2,32,4096]{2,1,0:T(8,128)(2,1)S(1)} %get-tuple-element.35.refs_0_), channel_id=1, source_target_pairs={{8,0},{12,4},{16,8},{20,12},{24,16},{28,20},{9,1},{13,5},{17,9},{2... | collective-permute-start | bytes 1572872 | tf_op jit(solution)/shard_map/ppermute | solution.py:301
  2.5 5.6 %collective-permute-start.3 = (bf16[2,32,4096]{2,1,0:T(8,128)(2,1)S(1)}, bf16[2,32,4096]{2,1,0:T(8,128)(2,1)S(1)}, u32[]{:S(2)}, u32[]{:S(2)}) collective-permute-start(bf16[2,32,4096]{2,1,0:T(8,128)(2,1)S(1)} %get-tuple-element.35.refs_0_), channel_id=1, source_target_pairs={{0,8},{4,12},{8,16},{12,20},{16,24},{20,28},{1,9},{5,13},{9,17},{1... | collective-permute-start | bytes 1572872 | tf_op jit(solution)/shard_map/ppermute | solution.py:300
  8.1 1.3 %collective-permute-start.2 = (bf16[2,32,4096]{2,1,0:T(8,128)(2,1)S(1)}, bf16[2,32,4096]{2,1,0:T(8,128)(2,1)S(1)}, u32[]{:S(2)}, u32[]{:S(2)}) collective-permute-start(bf16[2,32,4096]{2,1,0:T(8,128)(2,1)S(1)} %get-tuple-element.36.refs_1_), channel_id=1, source_target_pairs={{8,0},{12,4},{16,8},{20,12},{24,16},{28,20},{9,1},{13,5},{17,9},{2... | collective-permute-start | bytes 1572872 | tf_op jit(solution)/shard_map/ppermute | solution.py:301
  9.4 4.6 %collective-permute-start.4 = (bf16[2,32,4096]{2,1,0:T(8,128)(2,1)S(1)}, bf16[2,32,4096]{2,1,0:T(8,128)(2,1)S(1)}, u32[]{:S(2)}, u32[]{:S(2)}) collective-permute-start(bf16[2,32,4096]{2,1,0:T(8,128)(2,1)S(1)} %get-tuple-element.36.refs_1_), channel_id=1, source_target_pairs={{0,8},{4,12},{8,16},{12,20},{16,24},{20,28},{1,9},{5,13},{9,17},{1... | collective-permute-start | bytes 1572872 | tf_op jit(solution)/shard_map/ppermute | solution.py:300
  14.7 1.4 %shard_map.55 = (s32[1,8]{1,0:T(1,128)}, s32[1,8]{1,0:T(1,128)}) custom-call(s32[16]{0:T(128)} %owner_ref.1, s32[1,8]{1,0:T(1,128)} %pairs_ref.1, s32[1]{0:T(128)S(6)} %copy.6.counts_ref), custom_call_target="tpu_custom_call" | custom-call | tf_op jit(solution)/shard_map/pallas_call | solution.py:49
  16.0 1.9 %collective-permute-start = (s32[1,8]{1,0:T(1,128)}, s32[1,8]{1,0:T(1,128)S(1)}, u32[]{:S(2)}, u32[]{:S(2)}) collective-permute-start(s32[1,8]{1,0:T(1,128)} %get-tuple-element.34.wanted_ref), channel_id=1, source_target_pairs={{0,4},{4,0},{8,12},{12,8},{16,20},{20,16},{24,28},{28,24},{1,5},{5... | collective-permute-start | bytes 104 | tf_op jit(solution)/shard_map/ppermute | solution.py:306
  18.0 1.7 %collective-permute-done.asked_ref = s32[1,8]{1,0:T(1,128)S(1)} collective-permute-done((s32[1,8]{1,0:T(1,128)}, s32[1,8]{1,0:T(1,128)S(1)}, u32[]{:S(2)}, u32[]{:S(2)}) %collective-permute-start) | collective-permute-done | bytes 64 | tf_op jit(solution)/shard_map/ppermute | solution.py:306
  21.0 2.0 %collective-permute-start.6 = (bf16[2,32,4096]{2,1,0:T(8,128)(2,1)S(1)}, bf16[2,32,4096]{2,1,0:T(8,128)(2,1)S(1)}, u32[]{:S(2)}, u32[]{:S(2)}) collective-permute-start(bf16[2,32,4096]{2,1,0:T(8,128)(2,1)S(1)} %get-tuple-element.38), channel_id=1, source_target_pairs={{0,4},{4,0},{8,12},{12,8},{16,20},{20,16},{24,28},{28,24},{1,5},{5... | collective-permute-start | bytes 1572872 | tf_op jit(solution)/shard_map/ppermute | solution.py:327
  23.7 3.4 %collective-permute-start.5 = (s32[2,8]{1,0:T(2,128)S(1)}, s32[2,8]{1,0:T(2,128)S(1)}, u32[]{:S(2)}, u32[]{:S(2)}) collective-permute-start(s32[2,8]{1,0:T(2,128)S(1)} %pad_add_fusion), channel_id=1, source_target_pairs={{0,8},{4,12},{24,16},{28,20},{1,9},{5,13},{25,17},{29,21},{2,10},{... | collective-permute-start | bytes 200 | tf_op jit(solution)/shard_map/ppermute | solution.py:308
  27.1 2.2 %collective-permute-done.2.refs_1_ = bf16[2,32,4096]{2,1,0:T(8,128)(2,1)S(1)} collective-permute-done((bf16[2,32,4096]{2,1,0:T(8,128)(2,1)S(1)}, bf16[2,32,4096]{2,1,0:T(8,128)(2,1)S(1)}, u32[]{:S(2)}, u32[]{:S(2)}) %collective-permute-start.2) | collective-permute-done | bytes 524320 | tf_op jit(solution)/shard_map/ppermute | solution.py:301
  29.3 1.3 %collective-permute-start.8 = (bf16[2,32,4096]{2,1,0:T(8,128)(2,1)S(1)}, bf16[2,32,4096]{2,1,0:T(8,128)(2,1)S(1)}, u32[]{:S(2)}, u32[]{:S(2)}) collective-permute-start(bf16[2,32,4096]{2,1,0:T(8,128)(2,1)S(1)} %collective-permute-done.1.refs_0_), channel_id=1, source_target_pairs={{8,0},{12,4},{16,8},{20,12},{9,1},{13,5},{17,9},{21,13},{10,2},{14... | collective-permute-start | bytes 1572872 | tf_op jit(solution)/shard_map/ppermute | solution.py:301
  32.0 0.8 shard_map.57
  32.8 0.8 copy-done
  33.6 1.6 %collective-permute-start.7 = (bf16[2,32,4096]{2,1,0:T(8,128)(2,1)S(1)}, bf16[2,32,4096]{2,1,0:T(8,128)(2,1)S(1)}, u32[]{:S(2)}, u32[]{:S(2)}) collective-permute-start(bf16[2,32,4096]{2,1,0:T(8,128)(2,1)S(1)} %get-tuple-element.42), channel_id=1, source_target_pairs={{0,4},{4,0},{8,12},{12,8},{16,20},{20,16},{24,28},{28,24},{1,5},{5... | collective-permute-start | bytes 1572872 | tf_op jit(solution)/shard_map/ppermute | solution.py:327
  35.2 1.3 %collective-permute-start.11 = (bf16[2,32,4096]{2,1,0:T(8,128)(2,1)S(1)}, bf16[2,32,4096]{2,1,0:T(8,128)(2,1)S(1)}, u32[]{:S(2)}, u32[]{:S(2)}) collective-permute-start(bf16[2,32,4096]{2,1,0:T(8,128)(2,1)S(1)} %collective-permute-done.2.refs_1_), channel_id=1, source_target_pairs={{8,0},{12,4},{16,8},{20,12},{9,1},{13,5},{17,9},{21,13},{10,2},{14... | collective-permute-start | bytes 1572872 | tf_op jit(solution)/shard_map/ppermute | solution.py:301
  36.5 0.7 collective-permute-start.12
  37.2 8.8 %collective-permute-done.8.above_ref.refs_0_ = bf16[2,32,4096]{2,1,0:T(8,128)(2,1)S(1)} collective-permute-done((bf16[2,32,4096]{2,1,0:T(8,128)(2,1)S(1)}, bf16[2,32,4096]{2,1,0:T(8,128)(2,1)S(1)}, u32[]{:S(2)}, u32[]{:S(2)}) %collective-permute-start.8) | collective-permute-done | bytes 524320 | tf_op jit(solution)/shard_map/ppermute | solution.py:301
  46.7 1.3 %collective-permute-start.13 = (bf16[32,4096]{1,0:T(8,128)(2,1)S(1)}, bf16[32,4096]{1,0:T(8,128)(2,1)S(1)}, u32[]{:S(2)}, u32[]{:S(2)}) collective-permute-start(bf16[32,4096]{1,0:T(8,128)(2,1)S(1)} %get-tuple-element.45), channel_id=1, source_target_pairs={{8,4},{12,0},{16,28},{20,24},{9,5},{13,1},{17,29},{21,25},{10,6},{... | collective-permute-start | bytes 786440 | tf_op jit(solution)/shard_map/ppermute | solution.py:355
  48.7 8.6 %collective-permute-done.11.above_ref.refs_1_ = bf16[2,32,4096]{2,1,0:T(8,128)(2,1)S(1)} collective-permute-done((bf16[2,32,4096]{2,1,0:T(8,128)(2,1)S(1)}, bf16[2,32,4096]{2,1,0:T(8,128)(2,1)S(1)}, u32[]{:S(2)}, u32[]{:S(2)}) %collective-permute-start.11) | collective-permute-done | bytes 524320 | tf_op jit(solution)/shard_map/ppermute | solution.py:301
  58.6 1.7 %collective-permute-start.16 = (bf16[2,32,4096]{2,1,0:T(8,128)(2,1)S(1)}, bf16[2,32,4096]{2,1,0:T(8,128)(2,1)S(1)}, u32[]{:S(2)}, u32[]{:S(2)}) collective-permute-start(bf16[2,32,4096]{2,1,0:T(8,128)(2,1)S(1)} %get-tuple-element.58), channel_id=1, source_target_pairs={{0,4},{4,0},{8,12},{12,8},{16,20},{20,16},{24,28},{28,24},{1,5},{5... | collective-permute-start | bytes 1572872 | tf_op jit(solution)/shard_map/ppermute | solution.py:327
  60.4 1.3 %collective-permute-start.17 = (bf16[32,4096]{1,0:T(8,128)(2,1)S(1)}, bf16[32,4096]{1,0:T(8,128)(2,1)S(1)}, u32[]{:S(2)}, u32[]{:S(2)}) collective-permute-start(bf16[32,4096]{1,0:T(8,128)(2,1)S(1)} %get-tuple-element.44), channel_id=1, source_target_pairs={{8,0},{12,4},{16,24},{20,28},{9,1},{13,5},{17,25},{21,29},{10,2},{... | collective-permute-start | bytes 786440 | tf_op jit(solution)/shard_map/ppermute | solution.py:355
  61.6 1.3 %collective-permute-done.13.refs_5_ = bf16[32,4096]{1,0:T(8,128)(2,1)S(1)} collective-permute-done((bf16[32,4096]{1,0:T(8,128)(2,1)S(1)}, bf16[32,4096]{1,0:T(8,128)(2,1)S(1)}, u32[]{:S(2)}, u32[]{:S(2)}) %collective-permute-start.13) | collective-permute-done | bytes 262176 | tf_op jit(solution)/shard_map/ppermute | solution.py:355
  63.5 1.3 %collective-permute-start.14 = (bf16[32,4096]{1,0:T(8,128)(2,1)S(1)}, bf16[32,4096]{1,0:T(8,128)(2,1)S(1)}, u32[]{:S(2)}, u32[]{:S(2)}) collective-permute-start(bf16[32,4096]{1,0:T(8,128)(2,1)S(1)} %get-tuple-element.51), channel_id=1, source_target_pairs={{8,0},{12,4},{16,24},{20,28},{9,1},{13,5},{17,25},{21,29},{10,2},{... | collective-permute-start | bytes 786440 | tf_op jit(solution)/shard_map/ppermute | solution.py:355
  64.8 1.3 %collective-permute-start.15 = (bf16[32,4096]{1,0:T(8,128)(2,1)S(1)}, bf16[32,4096]{1,0:T(8,128)(2,1)S(1)}, u32[]{:S(2)}, u32[]{:S(2)}) collective-permute-start(bf16[32,4096]{1,0:T(8,128)(2,1)S(1)} %get-tuple-element.52), channel_id=1, source_target_pairs={{8,4},{12,0},{16,28},{20,24},{9,5},{13,1},{17,29},{21,25},{10,6},{... | collective-permute-start | bytes 786440 | tf_op jit(solution)/shard_map/ppermute | solution.py:355
  66.2 4.9 %shard_map.61.refs_5_ = f32[128,512]{1,0:T(8,128)S(1)} custom-call(bf16[2,32,4096]{2,1,0:T(8,128)(2,1)S(1)} %get-tuple-element.53.refs_0_, bf16[2,32,4096]{2,1,0:T(8,128)(2,1)S(1)} %collective-permute-done.6.refs_1_, bf16[2,32,4096]{2,1,0:T(8,128)(2,1)S(1)} %get-tuple-element.55.refs_2_, bf16[2,32,4096]{2,1,0:T(8,128)(2,1)} %copy-done.6, ...), custom_call_target="tpu_custom_call" | custom-call | tf_op jit(solution)/shard_map/pallas_call | solution.py:276
  71.4 3.3 %collective-permute-done.16.refs_1_ = bf16[2,32,4096]{2,1,0:T(8,128)(2,1)S(1)} collective-permute-done((bf16[2,32,4096]{2,1,0:T(8,128)(2,1)S(1)}, bf16[2,32,4096]{2,1,0:T(8,128)(2,1)S(1)}, u32[]{:S(2)}, u32[]{:S(2)}) %collective-permute-start.16) | collective-permute-done | bytes 524320 | tf_op jit(solution)/shard_map/ppermute | solution.py:327
  74.7 4.8 %shard_map.63.refs_6_ = f32[128,512]{1,0:T(8,128)S(1)} custom-call(bf16[2,32,4096]{2,1,0:T(8,128)(2,1)S(1)} %get-tuple-element.57.refs_0_, bf16[2,32,4096]{2,1,0:T(8,128)(2,1)S(1)} %collective-permute-done.16.refs_1_, bf16[2,32,4096]{2,1,0:T(8,128)(2,1)} %copy-done, bf16[2,32,4096]{2,1,0:T(8,128)(2,1)} %copy-done.5, ...), custom_call_target="tpu_custom_call" | custom-call | tf_op jit(solution)/shard_map/pallas_call | solution.py:276
  79.6 3.7 %shard_map.64 = (f32[4,32,512]{2,1,0:T(8,128)S(1)}, f32[4,32,512]{2,1,0:T(8,128)S(1)}) custom-call(bf16[2,32,4096]{2,1,0:T(8,128)(2,1)} %copy-done, bf16[2,32,4096]{2,1,0:T(8,128)(2,1)} %copy-done.5, bf16[32,4096]{1,0:T(8,128)(2,1)S(1)} %collective-permute-done.14.refs_2_, bf16[32,4096]{1,0:T(8,128)(2,1)S(1)} %collective-permute-done.15.refs_3_, ...), custom_call_target="tpu_custom_call" | custom-call | tf_op jit(solution)/shard_map/pallas_call | solution.py:276
  83.4 1.5 %collective-permute-done.18 = f32[4,32,512]{2,1,0:T(8,128)S(1)} collective-permute-done((f32[4,32,512]{2,1,0:T(8,128)S(1)}, f32[4,32,512]{2,1,0:T(8,128)S(1)}, u32[]{:S(2)}, u32[]{:S(2)}) %collective-permute-start.18) | collective-permute-done | bytes 262176 | tf_op jit(solution)/shard_map/ppermute | solution.py:368
  85.0 2.2 %collective-permute-start.19 = (f32[2,32,512]{2,1,0:T(8,128)S(1)}, f32[2,32,512]{2,1,0:T(8,128)S(1)}, u32[]{:S(2)}, u32[]{:S(2)}) collective-permute-start(f32[2,32,512]{2,1,0:T(8,128)S(1)} %slice.9), channel_id=1, source_target_pairs={{0,2},{1,3},{2,0},{3,1},{4,6},{5,7},{6,4},{7,5},{8,10},{9,11},{10,... | collective-permute-start | bytes 393224 | tf_op jit(solution)/shard_map/ppermute | solution.py:373
  87.2 3.8 %collective-permute-done.19 = f32[2,32,512]{2,1,0:T(8,128)S(1)} collective-permute-done((f32[2,32,512]{2,1,0:T(8,128)S(1)}, f32[2,32,512]{2,1,0:T(8,128)S(1)}, u32[]{:S(2)}, u32[]{:S(2)}) %collective-permute-start.19) | collective-permute-done | bytes 131104 | tf_op jit(solution)/shard_map/ppermute | solution.py:373
  (36 shorter events, 7.9 us)
Async XLA Ops:
  1.2 22.5 %collective-permute-start.1 = (bf16[2,32,4096]{2,1,0:T(8,128)(2,1)S(1)}, bf16[2,32,4096]{2,1,0:T(8,128)(2,1)S(1)}, u32[]{:S(2)}, u32[]{:S(2)}) collective-permute-start(bf16[2,32,4096]{2,1,0:T(8,128)(2,1)S(1)} %get-tuple-element.35.refs_0_), channel_id=1, source_target_pairs={{8,0},{12,4},{16,8},{20,12},{24,16},{28,20},{9,1},{13,5},{17,9},{2... | collective-permute-start | bytes 1572872 | tf_op jit(solution)/shard_map/ppermute | solution.py:301
  2.5 28.1 %collective-permute-start.3 = (bf16[2,32,4096]{2,1,0:T(8,128)(2,1)S(1)}, bf16[2,32,4096]{2,1,0:T(8,128)(2,1)S(1)}, u32[]{:S(2)}, u32[]{:S(2)}) collective-permute-start(bf16[2,32,4096]{2,1,0:T(8,128)(2,1)S(1)} %get-tuple-element.35.refs_0_), channel_id=1, source_target_pairs={{0,8},{4,12},{8,16},{12,20},{16,24},{20,28},{1,9},{5,13},{9,17},{1... | collective-permute-start | bytes 1572872 | tf_op jit(solution)/shard_map/ppermute | solution.py:300
  8.1 21.2 %collective-permute-start.2 = (bf16[2,32,4096]{2,1,0:T(8,128)(2,1)S(1)}, bf16[2,32,4096]{2,1,0:T(8,128)(2,1)S(1)}, u32[]{:S(2)}, u32[]{:S(2)}) collective-permute-start(bf16[2,32,4096]{2,1,0:T(8,128)(2,1)S(1)} %get-tuple-element.36.refs_1_), channel_id=1, source_target_pairs={{8,0},{12,4},{16,8},{20,12},{24,16},{28,20},{9,1},{13,5},{17,9},{2... | collective-permute-start | bytes 1572872 | tf_op jit(solution)/shard_map/ppermute | solution.py:301
  9.4 21.9 %collective-permute-start.4 = (bf16[2,32,4096]{2,1,0:T(8,128)(2,1)S(1)}, bf16[2,32,4096]{2,1,0:T(8,128)(2,1)S(1)}, u32[]{:S(2)}, u32[]{:S(2)}) collective-permute-start(bf16[2,32,4096]{2,1,0:T(8,128)(2,1)S(1)} %get-tuple-element.36.refs_1_), channel_id=1, source_target_pairs={{0,8},{4,12},{8,16},{12,20},{16,24},{20,28},{1,9},{5,13},{9,17},{1... | collective-permute-start | bytes 1572872 | tf_op jit(solution)/shard_map/ppermute | solution.py:300
  16.0 3.7 %collective-permute-start = (s32[1,8]{1,0:T(1,128)}, s32[1,8]{1,0:T(1,128)S(1)}, u32[]{:S(2)}, u32[]{:S(2)}) collective-permute-start(s32[1,8]{1,0:T(1,128)} %get-tuple-element.34.wanted_ref), channel_id=1, source_target_pairs={{0,4},{4,0},{8,12},{12,8},{16,20},{20,16},{24,28},{28,24},{1,5},{5... | collective-permute-start | bytes 104 | tf_op jit(solution)/shard_map/ppermute | solution.py:306
  19.7 0.7 copy-start.1
  21.0 12.5 %collective-permute-start.6 = (bf16[2,32,4096]{2,1,0:T(8,128)(2,1)S(1)}, bf16[2,32,4096]{2,1,0:T(8,128)(2,1)S(1)}, u32[]{:S(2)}, u32[]{:S(2)}) collective-permute-start(bf16[2,32,4096]{2,1,0:T(8,128)(2,1)S(1)} %get-tuple-element.38), channel_id=1, source_target_pairs={{0,4},{4,0},{8,12},{12,8},{16,20},{20,16},{24,28},{28,24},{1,5},{5... | collective-permute-start | bytes 1572872 | tf_op jit(solution)/shard_map/ppermute | solution.py:327
  23.7 9.9 %collective-permute-start.5 = (s32[2,8]{1,0:T(2,128)S(1)}, s32[2,8]{1,0:T(2,128)S(1)}, u32[]{:S(2)}, u32[]{:S(2)}) collective-permute-start(s32[2,8]{1,0:T(2,128)S(1)} %pad_add_fusion), channel_id=1, source_target_pairs={{0,8},{4,12},{24,16},{28,20},{1,9},{5,13},{25,17},{29,21},{2,10},{... | collective-permute-start | bytes 200 | tf_op jit(solution)/shard_map/ppermute | solution.py:308
  29.3 16.7 %collective-permute-start.8 = (bf16[2,32,4096]{2,1,0:T(8,128)(2,1)S(1)}, bf16[2,32,4096]{2,1,0:T(8,128)(2,1)S(1)}, u32[]{:S(2)}, u32[]{:S(2)}) collective-permute-start(bf16[2,32,4096]{2,1,0:T(8,128)(2,1)S(1)} %collective-permute-done.1.refs_0_), channel_id=1, source_target_pairs={{8,0},{12,4},{16,8},{20,12},{9,1},{13,5},{17,9},{21,13},{10,2},{14... | collective-permute-start | bytes 1572872 | tf_op jit(solution)/shard_map/ppermute | solution.py:301
  30.6 15.4 %collective-permute-start.9 = (bf16[2,32,4096]{2,1,0:T(8,128)(2,1)S(1)}, bf16[2,32,4096]{2,1,0:T(8,128)(2,1)S(1)}, u32[]{:S(2)}, u32[]{:S(2)}) collective-permute-start(bf16[2,32,4096]{2,1,0:T(8,128)(2,1)S(1)} %collective-permute-done.3.refs_2_), channel_id=1, source_target_pairs={{8,16},{12,20},{16,24},{20,28},{9,17},{13,21},{17,25},{21,29},{10,... | collective-permute-start | bytes 1572872 | tf_op jit(solution)/shard_map/ppermute | solution.py:300
  31.3 0.7 copy-start.2
  32.8 0.8 copy-start
  33.6 14.4 %collective-permute-start.7 = (bf16[2,32,4096]{2,1,0:T(8,128)(2,1)S(1)}, bf16[2,32,4096]{2,1,0:T(8,128)(2,1)S(1)}, u32[]{:S(2)}, u32[]{:S(2)}) collective-permute-start(bf16[2,32,4096]{2,1,0:T(8,128)(2,1)S(1)} %get-tuple-element.42), channel_id=1, source_target_pairs={{0,4},{4,0},{8,12},{12,8},{16,20},{20,16},{24,28},{28,24},{1,5},{5... | collective-permute-start | bytes 1572872 | tf_op jit(solution)/shard_map/ppermute | solution.py:327
  35.2 22.0 %collective-permute-start.11 = (bf16[2,32,4096]{2,1,0:T(8,128)(2,1)S(1)}, bf16[2,32,4096]{2,1,0:T(8,128)(2,1)S(1)}, u32[]{:S(2)}, u32[]{:S(2)}) collective-permute-start(bf16[2,32,4096]{2,1,0:T(8,128)(2,1)S(1)} %collective-permute-done.2.refs_1_), channel_id=1, source_target_pairs={{8,0},{12,4},{16,8},{20,12},{9,1},{13,5},{17,9},{21,13},{10,2},{14... | collective-permute-start | bytes 1572872 | tf_op jit(solution)/shard_map/ppermute | solution.py:301
  36.5 20.8 %collective-permute-start.12 = (bf16[2,32,4096]{2,1,0:T(8,128)(2,1)S(1)}, bf16[2,32,4096]{2,1,0:T(8,128)(2,1)S(1)}, u32[]{:S(2)}, u32[]{:S(2)}) collective-permute-start(bf16[2,32,4096]{2,1,0:T(8,128)(2,1)S(1)} %collective-permute-done.4.refs_3_), channel_id=1, source_target_pairs={{8,16},{12,20},{16,24},{20,28},{9,17},{13,21},{17,25},{21,29},{10,... | collective-permute-start | bytes 1572872 | tf_op jit(solution)/shard_map/ppermute | solution.py:300
  46.7 16.2 %collective-permute-start.13 = (bf16[32,4096]{1,0:T(8,128)(2,1)S(1)}, bf16[32,4096]{1,0:T(8,128)(2,1)S(1)}, u32[]{:S(2)}, u32[]{:S(2)}) collective-permute-start(bf16[32,4096]{1,0:T(8,128)(2,1)S(1)} %get-tuple-element.45), channel_id=1, source_target_pairs={{8,4},{12,0},{16,28},{20,24},{9,5},{13,1},{17,29},{21,25},{10,6},{... | collective-permute-start | bytes 786440 | tf_op jit(solution)/shard_map/ppermute | solution.py:355
  48.0 18.1 %copy-start.6 = (bf16[2,32,4096]{2,1,0:T(8,128)(2,1)}, bf16[2,32,4096]{2,1,0:T(8,128)(2,1)S(1)}, u32[]{:S(2)}) copy-start(bf16[2,32,4096]{2,1,0:T(8,128)(2,1)S(1)} %collective-permute-done.7.refs_3_) | copy-start | bytes 1572868
  48.0 23.3 %collective-permute-start.10 = (bf16[2,32,4096]{2,1,0:T(8,128)(2,1)S(1)}, bf16[2,32,4096]{2,1,0:T(8,128)(2,1)S(1)}, u32[]{:S(2)}, u32[]{:S(2)}) collective-permute-start(bf16[2,32,4096]{2,1,0:T(8,128)(2,1)S(1)} %get-tuple-element.46), channel_id=1, source_target_pairs={{8,12},{12,8},{16,20},{20,16},{9,13},{13,9},{17,21},{21,17},{10,14... | collective-permute-start | bytes 1572872 | tf_op jit(solution)/shard_map/ppermute | solution.py:327
  57.3 0.7 copy-start.3
  58.6 16.0 %collective-permute-start.16 = (bf16[2,32,4096]{2,1,0:T(8,128)(2,1)S(1)}, bf16[2,32,4096]{2,1,0:T(8,128)(2,1)S(1)}, u32[]{:S(2)}, u32[]{:S(2)}) collective-permute-start(bf16[2,32,4096]{2,1,0:T(8,128)(2,1)S(1)} %get-tuple-element.58), channel_id=1, source_target_pairs={{0,4},{4,0},{8,12},{12,8},{16,20},{20,16},{24,28},{28,24},{1,5},{5... | collective-permute-start | bytes 1572872 | tf_op jit(solution)/shard_map/ppermute | solution.py:327
  60.4 11.0 %collective-permute-start.17 = (bf16[32,4096]{1,0:T(8,128)(2,1)S(1)}, bf16[32,4096]{1,0:T(8,128)(2,1)S(1)}, u32[]{:S(2)}, u32[]{:S(2)}) collective-permute-start(bf16[32,4096]{1,0:T(8,128)(2,1)S(1)} %get-tuple-element.44), channel_id=1, source_target_pairs={{8,0},{12,4},{16,24},{20,28},{9,1},{13,5},{17,25},{21,29},{10,2},{... | collective-permute-start | bytes 786440 | tf_op jit(solution)/shard_map/ppermute | solution.py:355
  63.5 16.0 %collective-permute-start.14 = (bf16[32,4096]{1,0:T(8,128)(2,1)S(1)}, bf16[32,4096]{1,0:T(8,128)(2,1)S(1)}, u32[]{:S(2)}, u32[]{:S(2)}) collective-permute-start(bf16[32,4096]{1,0:T(8,128)(2,1)S(1)} %get-tuple-element.51), channel_id=1, source_target_pairs={{8,0},{12,4},{16,24},{20,28},{9,1},{13,5},{17,25},{21,29},{10,2},{... | collective-permute-start | bytes 786440 | tf_op jit(solution)/shard_map/ppermute | solution.py:355
  64.8 14.8 %collective-permute-start.15 = (bf16[32,4096]{1,0:T(8,128)(2,1)S(1)}, bf16[32,4096]{1,0:T(8,128)(2,1)S(1)}, u32[]{:S(2)}, u32[]{:S(2)}) collective-permute-start(bf16[32,4096]{1,0:T(8,128)(2,1)S(1)} %get-tuple-element.52), channel_id=1, source_target_pairs={{8,4},{12,0},{16,28},{20,24},{9,5},{13,1},{17,29},{21,25},{10,6},{... | collective-permute-start | bytes 786440 | tf_op jit(solution)/shard_map/ppermute | solution.py:355
  66.1 13.5 %copy-start.4 = (s32[1,8]{1,0:T(1,128)S(1)}, s32[1,8]{1,0:T(1,128)}, u32[]{:S(2)}) copy-start(s32[1,8]{1,0:T(1,128)} %get-tuple-element.60.refs_7_) | copy-start | bytes 100
  71.4 3.3 %copy-start.5 = (bf16[2,32,4096]{2,1,0:T(8,128)(2,1)}, bf16[2,32,4096]{2,1,0:T(8,128)(2,1)S(1)}, u32[]{:S(2)}) copy-start(bf16[2,32,4096]{2,1,0:T(8,128)(2,1)S(1)} %collective-permute-done.10.refs_3_.refs_1_) | copy-start | bytes 1572868
  83.3 1.6 %collective-permute-start.18 = (f32[4,32,512]{2,1,0:T(8,128)S(1)}, f32[4,32,512]{2,1,0:T(8,128)S(1)}, u32[]{:S(2)}, u32[]{:S(2)}) collective-permute-start(f32[4,32,512]{2,1,0:T(8,128)S(1)} %get-tuple-element.62), channel_id=1, source_target_pairs={{0,1},{1,0},{2,3},{3,2},{4,5},{5,4},{6,7},{7,6},{8,9},{9,8},{10,11... | collective-permute-start | bytes 786440 | tf_op jit(solution)/shard_map/ppermute | solution.py:368
  85.0 6.0 %collective-permute-start.19 = (f32[2,32,512]{2,1,0:T(8,128)S(1)}, f32[2,32,512]{2,1,0:T(8,128)S(1)}, u32[]{:S(2)}, u32[]{:S(2)}) collective-permute-start(f32[2,32,512]{2,1,0:T(8,128)S(1)} %slice.9), channel_id=1, source_target_pairs={{0,2},{1,3},{2,0},{3,1},{4,6},{5,7},{6,4},{7,5},{8,10},{9,11},{10,... | collective-permute-start | bytes 393224 | tf_op jit(solution)/shard_map/ppermute | solution.py:373

commit v5 on v4

--- a/solution.py
+++ b/solution.py
@@ -1,4 +1,5 @@
 import functools
+import math
 
 import jax
 import jax.numpy as jnp
@@ -9,13 +10,18 @@
 
 PAIR = 2
 PARTS = 2
+EIGHTHS = 3
 STEP = 1024
 SMALL_LIMIT = 8 * 2**20
-VMEM_LIMIT = 52 * 2**20
+VMEM_LIMIT = 46 * 2**20
 COST = pl.CostEstimate(flops=0, bytes_accessed=0, transcendentals=0)
 SMEM = pl.BlockSpec(memory_space=pltpu.SMEM)
 VMEM = pl.BlockSpec(memory_space=pltpu.VMEM)
 ANY = pl.BlockSpec(memory_space=pl.ANY)
+
+
+def cuts_of(features):
+    return 0, features - features * EIGHTHS // 8, features
 
 
 def slots_of(chain):
@@ -51,7 +57,7 @@
     )(owner_map, pair_blocks, pair_counts)
 
 
-def relay_kernel(chain, d, count, wanted_ref, asked_ref, *refs):
+def relay_kernel(chain, d, count, wants_ref, *refs):
     sources, outs, sems = refs[: -2 * count - 1], refs[-2 * count - 1 : -1], refs[-1]
     above_refs, below_refs = sources[:PARTS], sources[PARTS:]
     me = lax.axis_index("ex")
@@ -59,10 +65,12 @@
 
     def copies(j, blocks, source):
         made = []
+        cuts = cuts_of(outs[0].shape[-1])
         for h, ref in enumerate(blocks):
+            at = slice(cuts[h], cuts[h + 1])
             made += [
-                pltpu.make_async_copy(ref.at[asked_ref[0, source]], outs[2 * j + 1].at[h], sems.at[j, 2 * h]),
-                pltpu.make_async_copy(ref.at[wanted_ref[0, source]], outs[2 * j].at[h], sems.at[j, 2 * h + 1]),
+                pltpu.make_async_copy(ref.at[wants_ref[1, source]], outs[2 * j + 1].at[:, at], sems.at[j, 2 * h]),
+                pltpu.make_async_copy(ref.at[wants_ref[0, source]], outs[2 * j].at[:, at], sems.at[j, 2 * h + 1]),
             ]
         return made
 
@@ -91,26 +99,26 @@
         copy.wait()
 
 
-def relay(wanted, asked, above, below, d, count, chain):
+def relay(wants, above, below, d, count, chain):
     blocks = [above[d, h] for h in range(PARTS)] + ([below[d, h] for h in range(PARTS)] if d else [])
-    shape = jax.ShapeDtypeStruct((PARTS,) + blocks[0].shape[1:], blocks[0].dtype)
+    features = sum(b.shape[2] for b in blocks[:PARTS])
+    shape = jax.ShapeDtypeStruct((blocks[0].shape[1], features), blocks[0].dtype)
     return pl.pallas_call(
         functools.partial(relay_kernel, chain, d, count),
-        in_specs=[SMEM] * 2 + [ANY] * len(blocks),
+        in_specs=[SMEM] + [ANY] * len(blocks),
         out_specs=[VMEM] * (2 * count),
         out_shape=[shape] * (2 * count),
         scratch_shapes=[pltpu.SemaphoreType.DMA((count, 2 * PARTS))],
         cost_estimate=COST,
         compiler_params=pltpu.CompilerParams(vmem_limit_bytes=SMALL_LIMIT),
-    )(wanted, asked, *blocks)
+    )(wants, *blocks)
 
 
 def cut_kernel(own_ref, *refs):
     outs, sems = refs[:-1], refs[-1]
-    width = outs[0].shape[-1]
+    cuts = cuts_of(own_ref.shape[-1])
     copies = [
-        pltpu.make_async_copy(own_ref.at[:, :, h * width : (h + 1) * width], out, sems.at[h])
-        for h, out in enumerate(outs)
+        pltpu.make_async_copy(own_ref.at[:, :, cuts[h] : cuts[h + 1]], out, sems.at[h]) for h, out in enumerate(outs)
     ]
     for copy in copies:
         copy.start()
@@ -119,12 +127,14 @@
 
 
 def cut(own):
-    shape = jax.ShapeDtypeStruct(own.shape[:2] + (own.shape[2] // PARTS,), own.dtype)
+    cuts = cuts_of(own.shape[2])
     return pl.pallas_call(
         cut_kernel,
         in_specs=[ANY],
         out_specs=[VMEM] * PARTS,
-        out_shape=[shape] * PARTS,
+        out_shape=[
+            jax.ShapeDtypeStruct(own.shape[:2] + (stop - start,), own.dtype) for start, stop in zip(cuts, cuts[1:])
+        ],
         scratch_shapes=[pltpu.SemaphoreType.DMA((PARTS,))],
         cost_estimate=COST,
         compiler_params=pltpu.CompilerParams(vmem_limit_bytes=VMEM_LIMIT),
@@ -170,28 +180,30 @@
     away_refs, refs = refs[: PAIR * len(last_parts)], refs[PAIR * len(last_parts) :]
     train_ref, refs = refs[0], refs[1:]
     rows_v, train_v, sems = refs[-3:]
-    size, width = (blocks or near_refs)[0].shape[1:]
-    step = min(width, STEP)
+    size, features = (blocks or near_refs)[0].shape
+    cuts = cuts_of(features)
     place = lax.axis_index("ex") // PAIR
     end = jnp.logical_or(place == 0, place == chain - 1)
     chunks, near, away, starts = [], [], [], []
     for h in range(PARTS):
         if not full and h not in last_parts:
             continue
-        for at in range(0, width, step):
+        step = math.gcd(cuts[h + 1] - cuts[h], STEP)
+        for at in range(cuts[h], cuts[h + 1], step):
             i = len(chunks)
-            to = slice(h * width + at, h * width + at + step)
+            to = slice(at, at + step)
 
             def rows(b, source):
                 return pltpu.make_async_copy(source, rows_v.at[b * size : (b + 1) * size, to], sems.at[i, b])
 
             copies = [pltpu.make_async_copy(train_ref.at[:, to], train_v.at[:, to], sems.at[i, full + PAIR])]
-            copies += [rows(b, ref.at[h, :, at : at + step]) for b, ref in enumerate(blocks)]
+            copies += [rows(b, ref.at[:, to]) for b, ref in enumerate(blocks)]
             starts.append(list(copies))
             if h in last_parts:
                 pair = away_refs[last_parts.index(h) * PAIR :][:PAIR]
-                away.append([rows(full + b, ref.at[:, at : at + step]) for b, ref in enumerate(pair)])
-                near.append([rows(full + b, ref.at[h, :, at : at + step]) for b, ref in enumerate(near_refs)])
+                of_part = slice(at - cuts[h], at - cuts[h] + step)
+                away.append([rows(full + b, ref.at[:, of_part]) for b, ref in enumerate(pair)])
+                near.append([rows(full + b, ref.at[:, to]) for b, ref in enumerate(near_refs)])
                 copies += near[-1]
             chunks.append((to, slice(0 if full else full * size, (full + PAIR * (h in last_parts)) * size), copies))
 
@@ -215,15 +227,17 @@
         total_ref, base = refs[0], 0
         total_ref[...] = jnp.zeros_like(total_ref)
     else:
-        peers, feats, early = finish
-        early_refs, (rows_ref, keep_ref, give_ref, total_ref, early_sems) = refs[:early], refs[early:-3]
-        base = total_ref.shape[0] - PAIR * size
-        copies, at = [], 0
-        for i, ref in enumerate(early_refs):
-            copies.append(pltpu.make_async_copy(ref, total_ref.at[at : at + ref.shape[0]], early_sems.at[i]))
-            at += ref.shape[0]
+        peers, feats = finish
+        early_ref, rows_ref, keep_ref, give_ref, total_ref, early_sems = refs[:-3]
+        last = total_ref.shape[0] - PAIR * size
+        base = last - full * size
+        copies = [
+            pltpu.make_async_copy(early_ref.at[:base], total_ref.at[:base], early_sems.at[0]),
+            pltpu.make_async_copy(early_ref.at[base:], total_ref.at[last:], early_sems.at[1]),
+        ]
         for copy in copies:
             copy.start()
+        total_ref[base:last] = jnp.zeros((full * size, total_ref.shape[1]), total_ref.dtype)
         for copy in copies:
             copy.wait()
 
@@ -248,7 +262,7 @@
 
 
 def product(blocks, last, away, train, chain, finish=None):
-    size, width = last[0].shape[1:]
+    size = last[0].shape[0]
     examples, features = train.shape
     full, last_parts = len(blocks), sorted(away)
     operands = [*blocks, *(last if away else ()), *[a for h in last_parts for a in away[h]], train]
@@ -256,7 +270,7 @@
     scratch = [
         pltpu.VMEM((count, features), train.dtype),
         pltpu.VMEM((examples, features), train.dtype),
-        pltpu.SemaphoreType.DMA((PARTS * (width // min(width, STEP)), full + PAIR + 1)),
+        pltpu.SemaphoreType.DMA((features // math.gcd(features // 8, STEP), full + PAIR + 1)),
     ]
     in_specs = [ANY] * len(operands)
     if finish is None:
@@ -264,14 +278,14 @@
         sizes = None
     else:
         peers, feats, early, rows = finish
-        sizes = peers, feats, len(early)
-        operands += [*early, rows]
-        in_specs += [ANY] * len(early) + [SMEM]
+        sizes = peers, feats
+        operands += [early, rows]
+        in_specs += [ANY, SMEM]
         out_shape = [jax.ShapeDtypeStruct((peers // 2, size, examples), jnp.float32)] * 2
         out_specs = [VMEM] * 2
         scratch = [
             pltpu.VMEM((len(slots_of(chain)) * PAIR * size, examples), jnp.float32),
-            pltpu.SemaphoreType.DMA((len(early),)),
+            pltpu.SemaphoreType.DMA((2,)),
         ] + scratch
     return pl.pallas_call(
         functools.partial(product_kernel, chain, full, last_parts, sizes),
@@ -305,7 +319,8 @@
     wanted, rows = plan(owner_map, pair_blocks, pair_counts, peers)
     asked = lax.ppermute(wanted, "ex", across)
     ends = [(i, i + PAIR) for i in range(PAIR)] + [(i, i - PAIR) for i in range(peers - PAIR, peers)]
-    notes = lax.ppermute(jnp.concatenate([wanted, asked]), "ex", ends)
+    wants = jnp.concatenate([wanted, asked])
+    notes = lax.ppermute(wants, "ex", ends)
     last = chain - 2
 
     slots = slots_of(chain)
@@ -313,7 +328,7 @@
 
     def hand_over(d):
         count = 1 + ((d, True) in slots)
-        made = relay(wanted, asked, above, below, d, count, chain)
+        made = relay(wants, above, below, d, count, chain)
         for j in range(count):
             blocks[d, j > 0] = list(made[2 * j : 2 * j + 2])
 
@@ -362,8 +377,8 @@
     def scores(group, away, finish=None):
         return product([b for s in group for b in blocks[s]], blocks[slots[-1]], away, train_grads, chain, finish)
 
-    early = [scores(slots[:2], {}), scores(slots[2:-1], away)]
-    keep, give = scores([], tail, (peers, feats, early, rows))
+    early = scores(slots[:2], away)
+    keep, give = scores(slots[2:-1], tail, (peers, feats, early, rows))
 
     total = keep + lax.ppermute(give, "feat", [(i, i ^ 1) for i in range(feats)])
     lines, each = feats // 2, peers // feats

time: 92.1 us -> 90.3 us (0.980)
  waiting for transfers between devices: 31.6 us -> 35.8 us
  Pallas kernels: 19.4 us -> 16.6 us
  starting transfers between devices: 35.5 us -> 33.9 us
  local copies, waits for them, and re-layouts: 2.77 us -> 1.24 us
    ppermute x4, waiting for transfers between devices: 19.6 us -> 12.7 us  [along(): lax.ppermute(above[s - 1, h], 'ex', downward[:len(downward) - (s - 1) * P...]
    ppermute x4, waiting for transfers between devices: 0.01 us -> 6.43 us  [along(): below[s, h] = lax.ppermute(below[s - 1, h], 'ex', upward[(s - 1) * PAIR:])]
    ppermute x2, waiting for transfers between devices: 1.35 us -> 5.72 us  [shards(): lax.ppermute(theirs, 'ex', diagonal)]
    ppermute x4, waiting for transfers between devices: 3.31 us -> 0.3 us  [receive(): blocks[d, second] = [mine, lax.ppermute(theirs, 'ex', pairs)]]
    ppermute x2, waiting for transfers between devices: 0.34 us -> 3.18 us  [shards(): lax.ppermute(mine, 'ex', straight)]
    pallas_call x3 -> x2, Pallas kernels: 13.4 us -> 10.6 us  [product(): pl.pallas_call(functools.partial(product_kernel, chain, full, last_parts,...]
    ppermute x1, starting transfers between devices: 3.42 us -> 5.09 us  [shards(): notes = lax.ppermute(wants, 'ex', ends)]
    ppermute x4, starting transfers between devices: 6.05 us -> 4.45 us  [receive(): blocks[d, second] = [mine, lax.ppermute(theirs, 'ex', pairs)]]
  transfers between devices with their start and end apart: 20 -> 20, of which waited for: 10 -> 11; matrix products, arithmetic and copies ran while one was open for 1% -> 1% of each run, Pallas kernels for 16% -> 13%
where the time goes in v5:
time: 90.3 us; the launch traced here: 89.8 us
  waiting for transfers between devices  35.8 us (40%)
  starting transfers between devices  33.9 us (38%)
  Pallas kernels  16.6 us (18%)
  other arithmetic  1.37 us (2%)
  local copies, waits for them, and re-layouts  1.24 us (1%)
    ppermute x4, waiting for transfers between devices, along(): lax.ppermute(above[s - 1, h], 'ex', downward[:len(downward) - (s - 1) * P...  12.7 us
    pallas_call x2, Pallas kernels, product(): pl.pallas_call(functools.partial(product_kernel, chain, full, last_parts,...  10.6 us
    ppermute x4, starting transfers between devices, along(): below[s, h] = lax.ppermute(below[s - 1, h], 'ex', upward[(s - 1) * PAIR:])  10.4 us
    ppermute x4, waiting for transfers between devices, along(): below[s, h] = lax.ppermute(below[s - 1, h], 'ex', upward[(s - 1) * PAIR:])  6.43 us
    ppermute x2, waiting for transfers between devices, shards(): lax.ppermute(theirs, 'ex', diagonal)  5.72 us
    ppermute x4, starting transfers between devices, along(): lax.ppermute(above[s - 1, h], 'ex', downward[:len(downward) - (s - 1) * P...  5.17 us
    ppermute x1, starting transfers between devices, shards(): notes = lax.ppermute(wants, 'ex', ends)  5.09 us
    ppermute x4, starting transfers between devices, receive(): blocks[d, second] = [mine, lax.ppermute(theirs, 'ex', pairs)]  4.45 us
  transfers between devices with their start and end apart: 20, of which 11 were waited for; matrix products, arithmetic and copies ran while one was open for 1% of the time, Pallas kernels for 13%

profile of v5, /device:TPU:0, one launch (start us, length us, event | category | flops | bytes accessed | tf_op | source)
XLA Modules:
  0.0 89.8 jit_solution(11627214789440978696)
XLA Ops:
  0.0 1.2 %copy-done = bf16[2,1,32,8192]{3,2,1,0:T(8,128)(2,1)S(1)} copy-done((bf16[2,1,32,8192]{3,2,1,0:T(8,128)(2,1)S(1)}, bf16[2,1,32,8192]{3,2,1,0:T(8,128)(2,1)}, u32[]{:S(2)}) %copy-start) | copy-done | bytes 1048600
  1.3 1.3 %collective-permute-start.1 = (bf16[2,32,5120]{2,1,0:T(8,128)(2,1)S(1)}, bf16[2,32,5120]{2,1,0:T(8,128)(2,1)S(1)}, u32[]{:S(2)}, u32[]{:S(2)}) collective-permute-start(bf16[2,32,5120]{2,1,0:T(8,128)(2,1)S(1)} %get-tuple-element.35.refs_0_), channel_id=1, source_target_pairs={{8,0},{12,4},{16,8},{20,12},{24,16},{28,20},{9,1},{13,5},{17,9},{2... | collective-permute-start | bytes 1966088 | tf_op jit(solution)/shard_map/ppermute | solution.py:315
  2.6 5.6 %collective-permute-start.7 = (bf16[2,32,5120]{2,1,0:T(8,128)(2,1)S(1)}, bf16[2,32,5120]{2,1,0:T(8,128)(2,1)S(1)}, u32[]{:S(2)}, u32[]{:S(2)}) collective-permute-start(bf16[2,32,5120]{2,1,0:T(8,128)(2,1)S(1)} %get-tuple-element.35.refs_0_), channel_id=1, source_target_pairs={{0,8},{4,12},{8,16},{12,20},{16,24},{20,28},{1,9},{5,13},{9,17},{1... | collective-permute-start | bytes 1966088 | tf_op jit(solution)/shard_map/ppermute | solution.py:314
  8.9 1.3 %shard_map.55 = (s32[1,8]{1,0:T(1,128)}, s32[1,8]{1,0:T(1,128)}) custom-call(s32[16]{0:T(128)} %owner_ref.1, s32[1,8]{1,0:T(1,128)} %pairs_ref.1, s32[1]{0:T(128)S(6)} %copy.6.counts_ref), custom_call_target="tpu_custom_call" | custom-call | tf_op jit(solution)/shard_map/pallas_call | solution.py:55
  10.2 1.9 %collective-permute-start = (s32[1,8]{1,0:T(1,128)}, s32[1,8]{1,0:T(1,128)S(1)}, u32[]{:S(2)}, u32[]{:S(2)}) collective-permute-start(s32[1,8]{1,0:T(1,128)} %get-tuple-element.34), channel_id=1, source_target_pairs={{0,4},{4,0},{8,12},{12,8},{16,20},{20,16},{24,28},{28,24},{1,5},{5... | collective-permute-start | bytes 104 | tf_op jit(solution)/shard_map/ppermute | solution.py:320
  12.2 1.7 %collective-permute-done = s32[1,8]{1,0:T(1,128)S(1)} collective-permute-done((s32[1,8]{1,0:T(1,128)}, s32[1,8]{1,0:T(1,128)S(1)}, u32[]{:S(2)}, u32[]{:S(2)}) %collective-permute-start) | collective-permute-done | bytes 64 | tf_op jit(solution)/shard_map/ppermute | solution.py:320
  14.6 0.8 shard_map.57
  15.4 2.0 %collective-permute-start.6 = (bf16[32,8192]{1,0:T(8,128)(2,1)S(1)}, bf16[32,8192]{1,0:T(8,128)(2,1)S(1)}, u32[]{:S(2)}, u32[]{:S(2)}) collective-permute-start(bf16[32,8192]{1,0:T(8,128)(2,1)S(1)} %get-tuple-element.37), channel_id=1, source_target_pairs={{0,4},{4,0},{8,12},{12,8},{16,20},{20,16},{24,28},{28,24},{1,5},{5... | collective-permute-start | bytes 1572872 | tf_op jit(solution)/shard_map/ppermute | solution.py:342
  17.4 3.5 %collective-permute-start.3 = (bf16[2,32,3072]{2,1,0:T(8,128)(2,1)S(1)}, bf16[2,32,3072]{2,1,0:T(8,128)(2,1)S(1)}, u32[]{:S(2)}, u32[]{:S(2)}) collective-permute-start(bf16[2,32,3072]{2,1,0:T(8,128)(2,1)S(1)} %get-tuple-element.36.refs_1_), channel_id=1, source_target_pairs={{0,8},{4,12},{8,16},{12,20},{16,24},{20,28},{1,9},{5,13},{9,17},{1... | collective-permute-start | bytes 1179656 | tf_op jit(solution)/shard_map/ppermute | solution.py:314
  20.9 1.3 %collective-permute-start.4 = (bf16[2,32,3072]{2,1,0:T(8,128)(2,1)S(1)}, bf16[2,32,3072]{2,1,0:T(8,128)(2,1)S(1)}, u32[]{:S(2)}, u32[]{:S(2)}) collective-permute-start(bf16[2,32,3072]{2,1,0:T(8,128)(2,1)S(1)} %get-tuple-element.36.refs_1_), channel_id=1, source_target_pairs={{8,0},{12,4},{16,8},{20,12},{24,16},{28,20},{9,1},{13,5},{17,9},{2... | collective-permute-start | bytes 1179656 | tf_op jit(solution)/shard_map/ppermute | solution.py:315
  22.2 1.3 %collective-permute-start.2 = (bf16[2,32,5120]{2,1,0:T(8,128)(2,1)S(1)}, bf16[2,32,5120]{2,1,0:T(8,128)(2,1)S(1)}, u32[]{:S(2)}, u32[]{:S(2)}) collective-permute-start(bf16[2,32,5120]{2,1,0:T(8,128)(2,1)S(1)} %collective-permute-done.1.refs_0_), channel_id=1, source_target_pairs={{8,0},{12,4},{16,8},{20,12},{9,1},{13,5},{17,9},{21,13},{10,2},{14... | collective-permute-start | bytes 1966088 | tf_op jit(solution)/shard_map/ppermute | solution.py:315
  24.2 6.4 %collective-permute-done.3.refs_3_ = bf16[2,32,3072]{2,1,0:T(8,128)(2,1)S(1)} collective-permute-done((bf16[2,32,3072]{2,1,0:T(8,128)(2,1)S(1)}, bf16[2,32,3072]{2,1,0:T(8,128)(2,1)S(1)}, u32[]{:S(2)}, u32[]{:S(2)}) %collective-permute-start.3) | collective-permute-done | bytes 393248 | tf_op jit(solution)/shard_map/ppermute | solution.py:314
  30.6 5.1 %collective-permute-start.5 = (s32[2,8]{1,0:T(2,128)S(1)}, s32[2,8]{1,0:T(2,128)S(1)}, u32[]{:S(2)}, u32[]{:S(2)}) collective-permute-start(s32[2,8]{1,0:T(2,128)S(1)} %pad_add_fusion.wants_ref), channel_id=1, source_target_pairs={{0,8},{4,12},{24,16},{28,20},{1,9},{5,13},{25,17},{29,21},{2,10},{... | collective-permute-start | bytes 200 | tf_op jit(solution)/shard_map/ppermute | solution.py:323
  35.7 1.1 %shard_map.58 = (bf16[32,8192]{1,0:T(8,128)(2,1)S(1)}, bf16[32,8192]{1,0:T(8,128)(2,1)S(1)}, bf16[32,8192]{1,0:T(8,128)(2,1)S(1)}, bf16[32,8192]{1,0:T(8,128)(2,1)S(1)}) custom-call(s32[2,8]{1,0:T(2,128)S(1)} %pad_add_fusion.wants_ref, bf16[2,32,5120]{2,1,0:T(8,128)(2,1)S(1)} %collective-permute-done.1.refs_0_, ...), custom_call_target="tpu_custom_call" | custom-call | tf_op jit(solution)/shard_map/pallas_call | solution.py:106
  37.0 1.5 %collective-permute-start.12 = (bf16[32,8192]{1,0:T(8,128)(2,1)S(1)}, bf16[32,8192]{1,0:T(8,128)(2,1)S(1)}, u32[]{:S(2)}, u32[]{:S(2)}) collective-permute-start(bf16[32,8192]{1,0:T(8,128)(2,1)S(1)} %get-tuple-element.46), channel_id=1, source_target_pairs={{0,4},{4,0},{8,12},{12,8},{16,20},{20,16},{24,28},{28,24},{1,5},{5... | collective-permute-start | bytes 1572872 | tf_op jit(solution)/shard_map/ppermute | solution.py:342
  39.2 1.3 %collective-permute-start.8 = (bf16[2,32,3072]{2,1,0:T(8,128)(2,1)S(1)}, bf16[2,32,3072]{2,1,0:T(8,128)(2,1)S(1)}, u32[]{:S(2)}, u32[]{:S(2)}) collective-permute-start(bf16[2,32,3072]{2,1,0:T(8,128)(2,1)S(1)} %collective-permute-done.4.refs_1_), channel_id=1, source_target_pairs={{8,0},{12,4},{16,8},{20,12},{9,1},{13,5},{17,9},{21,13},{10,2},{14... | collective-permute-start | bytes 1179656 | tf_op jit(solution)/shard_map/ppermute | solution.py:315
  40.5 7.1 %collective-permute-done.2.refs_0_.above_ref = bf16[2,32,5120]{2,1,0:T(8,128)(2,1)S(1)} collective-permute-done((bf16[2,32,5120]{2,1,0:T(8,128)(2,1)S(1)}, bf16[2,32,5120]{2,1,0:T(8,128)(2,1)S(1)}, u32[]{:S(2)}, u32[]{:S(2)}) %collective-permute-start.2) | collective-permute-done | bytes 655392 | tf_op jit(solution)/shard_map/ppermute | solution.py:315
  47.6 0.8 shard_map.60
  49.4 1.3 %collective-permute-start.14 = (bf16[32,5120]{1,0:T(8,128)(2,1)S(1)}, bf16[32,5120]{1,0:T(8,128)(2,1)S(1)}, u32[]{:S(2)}, u32[]{:S(2)}) collective-permute-start(bf16[32,5120]{1,0:T(8,128)(2,1)S(1)} %get-tuple-element.49), channel_id=1, source_target_pairs={{8,4},{12,0},{16,28},{20,24},{9,5},{13,1},{17,29},{21,25},{10,6},{... | collective-permute-start | bytes 983048 | tf_op jit(solution)/shard_map/ppermute | solution.py:370
  50.7 5.6 %collective-permute-done.8.refs_1_.above_ref = bf16[2,32,3072]{2,1,0:T(8,128)(2,1)S(1)} collective-permute-done((bf16[2,32,3072]{2,1,0:T(8,128)(2,1)S(1)}, bf16[2,32,3072]{2,1,0:T(8,128)(2,1)S(1)}, u32[]{:S(2)}, u32[]{:S(2)}) %collective-permute-start.8) | collective-permute-done | bytes 393248 | tf_op jit(solution)/shard_map/ppermute | solution.py:315
  56.3 0.8 shard_map.59
  57.4 1.3 %collective-permute-start.17 = (bf16[32,5120]{1,0:T(8,128)(2,1)S(1)}, bf16[32,5120]{1,0:T(8,128)(2,1)S(1)}, u32[]{:S(2)}, u32[]{:S(2)}) collective-permute-start(bf16[32,5120]{1,0:T(8,128)(2,1)S(1)} %get-tuple-element.48), channel_id=1, source_target_pairs={{8,0},{12,4},{16,24},{20,28},{9,1},{13,5},{17,25},{21,29},{10,2},{... | collective-permute-start | bytes 983048 | tf_op jit(solution)/shard_map/ppermute | solution.py:370
  58.7 5.1 %collective-permute-done.14.refs_7_ = bf16[32,5120]{1,0:T(8,128)(2,1)S(1)} collective-permute-done((bf16[32,5120]{1,0:T(8,128)(2,1)S(1)}, bf16[32,5120]{1,0:T(8,128)(2,1)S(1)}, u32[]{:S(2)}, u32[]{:S(2)}) %collective-permute-start.14) | collective-permute-done | bytes 327712 | tf_op jit(solution)/shard_map/ppermute | solution.py:370
  63.8 1.1 %shard_map.61 = (bf16[32,3072]{1,0:T(8,128)(2,1)S(1)}, bf16[32,3072]{1,0:T(8,128)(2,1)S(1)}) custom-call(s32[2,8]{1,0:T(2,128)S(1)} %collective-permute-done.5.notes_ref, bf16[2,32,3072]{2,1,0:T(8,128)(2,1)S(1)} %collective-permute-done.8.refs_1_.above_ref, bf16[2,32,3072]{2,1,0:T(8,128)(2,1)S(1)} %collective-permute-done.10.refs_3_.below_ref), custom_call_target="tpu_custom_call" | custom-call | tf_op jit(solution)/shard_map/pallas_call | solution.py:164
  64.9 1.3 %collective-permute-start.15 = (bf16[32,3072]{1,0:T(8,128)(2,1)S(1)}, bf16[32,3072]{1,0:T(8,128)(2,1)S(1)}, u32[]{:S(2)}, u32[]{:S(2)}) collective-permute-start(bf16[32,3072]{1,0:T(8,128)(2,1)S(1)} %get-tuple-element.53), channel_id=1, source_target_pairs={{8,0},{12,4},{16,24},{20,28},{9,1},{13,5},{17,25},{21,29},{10,2},{... | collective-permute-start | bytes 589832 | tf_op jit(solution)/shard_map/ppermute | solution.py:370
  66.2 1.3 %collective-permute-start.16 = (bf16[32,3072]{1,0:T(8,128)(2,1)S(1)}, bf16[32,3072]{1,0:T(8,128)(2,1)S(1)}, u32[]{:S(2)}, u32[]{:S(2)}) collective-permute-start(bf16[32,3072]{1,0:T(8,128)(2,1)S(1)} %get-tuple-element.54), channel_id=1, source_target_pairs={{8,4},{12,0},{16,28},{20,24},{9,5},{13,1},{17,29},{21,25},{10,6},{... | collective-permute-start | bytes 589832 | tf_op jit(solution)/shard_map/ppermute | solution.py:370
  67.5 3.2 %collective-permute-done.17.refs_6_ = bf16[32,5120]{1,0:T(8,128)(2,1)S(1)} collective-permute-done((bf16[32,5120]{1,0:T(8,128)(2,1)S(1)}, bf16[32,5120]{1,0:T(8,128)(2,1)S(1)}, u32[]{:S(2)}, u32[]{:S(2)}) %collective-permute-start.17) | collective-permute-done | bytes 327712 | tf_op jit(solution)/shard_map/ppermute | solution.py:370
  70.7 5.3 %shard_map.62.refs_7_ = f32[192,512]{1,0:T(8,128)S(1)} custom-call(bf16[32,8192]{1,0:T(8,128)(2,1)S(1)} %get-tuple-element.55.refs_0_, bf16[32,8192]{1,0:T(8,128)(2,1)S(1)} %collective-permute-done.6.refs_1_, bf16[32,8192]{1,0:T(8,128)(2,1)S(1)} %get-tuple-element.57.refs_2_, bf16[32,8192]{1,0:T(8,128)(2,1)S(1)} %collective-permute-done.12.refs_3_, ...), custom_call_target="tpu_custom_call" | custom-call | tf_op jit(solution)/shard_map/pallas_call | solution.py:290
  76.6 5.3 %shard_map.63 = (f32[4,32,512]{2,1,0:T(8,128)S(1)}, f32[4,32,512]{2,1,0:T(8,128)S(1)}) custom-call(bf16[32,8192]{1,0:T(8,128)(2,1)S(1)} %get-tuple-element.42.refs_0_, bf16[32,8192]{1,0:T(8,128)(2,1)S(1)} %collective-permute-done.11.refs_1_, bf16[32,8192]{1,0:T(8,128)(2,1)S(1)} %get-tuple-element.44.refs_4_.refs_2_, ...), custom_call_target="tpu_custom_call" | custom-call | tf_op jit(solution)/shard_map/pallas_call | solution.py:290
  81.9 1.5 %collective-permute-done.18 = f32[4,32,512]{2,1,0:T(8,128)S(1)} collective-permute-done((f32[4,32,512]{2,1,0:T(8,128)S(1)}, f32[4,32,512]{2,1,0:T(8,128)S(1)}, u32[]{:S(2)}, u32[]{:S(2)}) %collective-permute-start.18) | collective-permute-done | bytes 262176 | tf_op jit(solution)/shard_map/ppermute | solution.py:383
  83.5 1.6 %collective-permute-start.19 = (f32[2,32,512]{2,1,0:T(8,128)S(1)}, f32[2,32,512]{2,1,0:T(8,128)S(1)}, u32[]{:S(2)}, u32[]{:S(2)}) collective-permute-start(f32[2,32,512]{2,1,0:T(8,128)S(1)} %slice.9), channel_id=1, source_target_pairs={{0,2},{1,3},{2,0},{3,1},{4,6},{5,7},{6,4},{7,5},{8,10},{9,11},{10,... | collective-permute-start | bytes 393224 | tf_op jit(solution)/shard_map/ppermute | solution.py:388
  85.1 4.0 %collective-permute-done.19 = f32[2,32,512]{2,1,0:T(8,128)S(1)} collective-permute-done((f32[2,32,512]{2,1,0:T(8,128)S(1)}, f32[2,32,512]{2,1,0:T(8,128)S(1)}, u32[]{:S(2)}, u32[]{:S(2)}) %collective-permute-start.19) | collective-permute-done | bytes 131104 | tf_op jit(solution)/shard_map/ppermute | solution.py:388
  (25 shorter events, 5.0 us)
Async XLA Ops:
  0.0 1.2 %copy-start = (bf16[2,1,32,8192]{3,2,1,0:T(8,128)(2,1)S(1)}, bf16[2,1,32,8192]{3,2,1,0:T(8,128)(2,1)}, u32[]{:S(2)}) copy-start(bf16[2,1,32,8192]{3,2,1,0:T(8,128)(2,1)} %param.6) | copy-start | bytes 3145732
  1.3 20.8 %collective-permute-start.1 = (bf16[2,32,5120]{2,1,0:T(8,128)(2,1)S(1)}, bf16[2,32,5120]{2,1,0:T(8,128)(2,1)S(1)}, u32[]{:S(2)}, u32[]{:S(2)}) collective-permute-start(bf16[2,32,5120]{2,1,0:T(8,128)(2,1)S(1)} %get-tuple-element.35.refs_0_), channel_id=1, source_target_pairs={{8,0},{12,4},{16,8},{20,12},{24,16},{28,20},{9,1},{13,5},{17,9},{2... | collective-permute-start | bytes 1966088 | tf_op jit(solution)/shard_map/ppermute | solution.py:315
  2.6 20.8 %collective-permute-start.7 = (bf16[2,32,5120]{2,1,0:T(8,128)(2,1)S(1)}, bf16[2,32,5120]{2,1,0:T(8,128)(2,1)S(1)}, u32[]{:S(2)}, u32[]{:S(2)}) collective-permute-start(bf16[2,32,5120]{2,1,0:T(8,128)(2,1)S(1)} %get-tuple-element.35.refs_0_), channel_id=1, source_target_pairs={{0,8},{4,12},{8,16},{12,20},{16,24},{20,28},{1,9},{5,13},{9,17},{1... | collective-permute-start | bytes 1966088 | tf_op jit(solution)/shard_map/ppermute | solution.py:314
  10.2 3.7 %collective-permute-start = (s32[1,8]{1,0:T(1,128)}, s32[1,8]{1,0:T(1,128)S(1)}, u32[]{:S(2)}, u32[]{:S(2)}) collective-permute-start(s32[1,8]{1,0:T(1,128)} %get-tuple-element.34), channel_id=1, source_target_pairs={{0,4},{4,0},{8,12},{12,8},{16,20},{20,16},{24,28},{28,24},{1,5},{5... | collective-permute-start | bytes 104 | tf_op jit(solution)/shard_map/ppermute | solution.py:320
  15.4 21.6 %collective-permute-start.6 = (bf16[32,8192]{1,0:T(8,128)(2,1)S(1)}, bf16[32,8192]{1,0:T(8,128)(2,1)S(1)}, u32[]{:S(2)}, u32[]{:S(2)}) collective-permute-start(bf16[32,8192]{1,0:T(8,128)(2,1)S(1)} %get-tuple-element.37), channel_id=1, source_target_pairs={{0,4},{4,0},{8,12},{12,8},{16,20},{20,16},{24,28},{28,24},{1,5},{5... | collective-permute-start | bytes 1572872 | tf_op jit(solution)/shard_map/ppermute | solution.py:342
  17.4 13.2 %collective-permute-start.3 = (bf16[2,32,3072]{2,1,0:T(8,128)(2,1)S(1)}, bf16[2,32,3072]{2,1,0:T(8,128)(2,1)S(1)}, u32[]{:S(2)}, u32[]{:S(2)}) collective-permute-start(bf16[2,32,3072]{2,1,0:T(8,128)(2,1)S(1)} %get-tuple-element.36.refs_1_), channel_id=1, source_target_pairs={{0,8},{4,12},{8,16},{12,20},{16,24},{20,28},{1,9},{5,13},{9,17},{1... | collective-permute-start | bytes 1179656 | tf_op jit(solution)/shard_map/ppermute | solution.py:314
  20.9 14.9 %collective-permute-start.4 = (bf16[2,32,3072]{2,1,0:T(8,128)(2,1)S(1)}, bf16[2,32,3072]{2,1,0:T(8,128)(2,1)S(1)}, u32[]{:S(2)}, u32[]{:S(2)}) collective-permute-start(bf16[2,32,3072]{2,1,0:T(8,128)(2,1)S(1)} %get-tuple-element.36.refs_1_), channel_id=1, source_target_pairs={{8,0},{12,4},{16,8},{20,12},{24,16},{28,20},{9,1},{13,5},{17,9},{2... | collective-permute-start | bytes 1179656 | tf_op jit(solution)/shard_map/ppermute | solution.py:315
  22.2 25.4 %collective-permute-start.2 = (bf16[2,32,5120]{2,1,0:T(8,128)(2,1)S(1)}, bf16[2,32,5120]{2,1,0:T(8,128)(2,1)S(1)}, u32[]{:S(2)}, u32[]{:S(2)}) collective-permute-start(bf16[2,32,5120]{2,1,0:T(8,128)(2,1)S(1)} %collective-permute-done.1.refs_0_), channel_id=1, source_target_pairs={{8,0},{12,4},{16,8},{20,12},{9,1},{13,5},{17,9},{21,13},{10,2},{14... | collective-permute-start | bytes 1966088 | tf_op jit(solution)/shard_map/ppermute | solution.py:315
  23.5 24.1 %collective-permute-start.9 = (bf16[2,32,5120]{2,1,0:T(8,128)(2,1)S(1)}, bf16[2,32,5120]{2,1,0:T(8,128)(2,1)S(1)}, u32[]{:S(2)}, u32[]{:S(2)}) collective-permute-start(bf16[2,32,5120]{2,1,0:T(8,128)(2,1)S(1)} %collective-permute-done.7.refs_2_), channel_id=1, source_target_pairs={{8,16},{12,20},{16,24},{20,28},{9,17},{13,21},{17,25},{21,29},{10,... | collective-permute-start | bytes 1966088 | tf_op jit(solution)/shard_map/ppermute | solution.py:314
  30.6 6.4 %collective-permute-start.5 = (s32[2,8]{1,0:T(2,128)S(1)}, s32[2,8]{1,0:T(2,128)S(1)}, u32[]{:S(2)}, u32[]{:S(2)}) collective-permute-start(s32[2,8]{1,0:T(2,128)S(1)} %pad_add_fusion.wants_ref), channel_id=1, source_target_pairs={{0,8},{4,12},{24,16},{28,20},{1,9},{5,13},{25,17},{29,21},{2,10},{... | collective-permute-start | bytes 200 | tf_op jit(solution)/shard_map/ppermute | solution.py:323
  37.0 39.6 %copy-start.1 = (s32[1,8]{1,0:T(1,128)S(1)}, s32[1,8]{1,0:T(1,128)}, u32[]{:S(2)}) copy-start(s32[1,8]{1,0:T(1,128)} %get-tuple-element.60.refs_8_) | copy-start | bytes 100
  37.0 11.7 %collective-permute-start.12 = (bf16[32,8192]{1,0:T(8,128)(2,1)S(1)}, bf16[32,8192]{1,0:T(8,128)(2,1)S(1)}, u32[]{:S(2)}, u32[]{:S(2)}) collective-permute-start(bf16[32,8192]{1,0:T(8,128)(2,1)S(1)} %get-tuple-element.46), channel_id=1, source_target_pairs={{0,4},{4,0},{8,12},{12,8},{16,20},{20,16},{24,28},{28,24},{1,5},{5... | collective-permute-start | bytes 1572872 | tf_op jit(solution)/shard_map/ppermute | solution.py:342
  38.5 12.2 %collective-permute-start.10 = (bf16[2,32,3072]{2,1,0:T(8,128)(2,1)S(1)}, bf16[2,32,3072]{2,1,0:T(8,128)(2,1)S(1)}, u32[]{:S(2)}, u32[]{:S(2)}) collective-permute-start(bf16[2,32,3072]{2,1,0:T(8,128)(2,1)S(1)} %collective-permute-done.3.refs_3_), channel_id=1, source_target_pairs={{8,16},{12,20},{16,24},{20,28},{9,17},{13,21},{17,25},{21,29},{10,... | collective-permute-start | bytes 1179656 | tf_op jit(solution)/shard_map/ppermute | solution.py:314
  39.2 17.1 %collective-permute-start.8 = (bf16[2,32,3072]{2,1,0:T(8,128)(2,1)S(1)}, bf16[2,32,3072]{2,1,0:T(8,128)(2,1)S(1)}, u32[]{:S(2)}, u32[]{:S(2)}) collective-permute-start(bf16[2,32,3072]{2,1,0:T(8,128)(2,1)S(1)} %collective-permute-done.4.refs_1_), channel_id=1, source_target_pairs={{8,0},{12,4},{16,8},{20,12},{9,1},{13,5},{17,9},{21,13},{10,2},{14... | collective-permute-start | bytes 1179656 | tf_op jit(solution)/shard_map/ppermute | solution.py:315
  48.7 22.0 %collective-permute-start.13 = (bf16[32,8192]{1,0:T(8,128)(2,1)S(1)}, bf16[32,8192]{1,0:T(8,128)(2,1)S(1)}, u32[]{:S(2)}, u32[]{:S(2)}) collective-permute-start(bf16[32,8192]{1,0:T(8,128)(2,1)S(1)} %get-tuple-element.50), channel_id=1, source_target_pairs={{8,12},{12,8},{16,20},{20,16},{9,13},{13,9},{17,21},{21,17},{10,14... | collective-permute-start | bytes 1572872 | tf_op jit(solution)/shard_map/ppermute | solution.py:342
  49.4 14.4 %collective-permute-start.14 = (bf16[32,5120]{1,0:T(8,128)(2,1)S(1)}, bf16[32,5120]{1,0:T(8,128)(2,1)S(1)}, u32[]{:S(2)}, u32[]{:S(2)}) collective-permute-start(bf16[32,5120]{1,0:T(8,128)(2,1)S(1)} %get-tuple-element.49), channel_id=1, source_target_pairs={{8,4},{12,0},{16,28},{20,24},{9,5},{13,1},{17,29},{21,25},{10,6},{... | collective-permute-start | bytes 983048 | tf_op jit(solution)/shard_map/ppermute | solution.py:370
  57.1 19.5 %collective-permute-start.11 = (bf16[32,8192]{1,0:T(8,128)(2,1)S(1)}, bf16[32,8192]{1,0:T(8,128)(2,1)S(1)}, u32[]{:S(2)}, u32[]{:S(2)}) collective-permute-start(bf16[32,8192]{1,0:T(8,128)(2,1)S(1)} %get-tuple-element.43), channel_id=1, source_target_pairs={{0,4},{4,0},{8,12},{12,8},{16,20},{20,16},{24,28},{28,24},{1,5},{5... | collective-permute-start | bytes 1572872 | tf_op jit(solution)/shard_map/ppermute | solution.py:342
  57.4 13.3 %collective-permute-start.17 = (bf16[32,5120]{1,0:T(8,128)(2,1)S(1)}, bf16[32,5120]{1,0:T(8,128)(2,1)S(1)}, u32[]{:S(2)}, u32[]{:S(2)}) collective-permute-start(bf16[32,5120]{1,0:T(8,128)(2,1)S(1)} %get-tuple-element.48), channel_id=1, source_target_pairs={{8,0},{12,4},{16,24},{20,28},{9,1},{13,5},{17,25},{21,29},{10,2},{... | collective-permute-start | bytes 983048 | tf_op jit(solution)/shard_map/ppermute | solution.py:370
  64.9 11.1 %collective-permute-start.15 = (bf16[32,3072]{1,0:T(8,128)(2,1)S(1)}, bf16[32,3072]{1,0:T(8,128)(2,1)S(1)}, u32[]{:S(2)}, u32[]{:S(2)}) collective-permute-start(bf16[32,3072]{1,0:T(8,128)(2,1)S(1)} %get-tuple-element.53), channel_id=1, source_target_pairs={{8,0},{12,4},{16,24},{20,28},{9,1},{13,5},{17,25},{21,29},{10,2},{... | collective-permute-start | bytes 589832 | tf_op jit(solution)/shard_map/ppermute | solution.py:370
  66.2 10.4 %collective-permute-start.16 = (bf16[32,3072]{1,0:T(8,128)(2,1)S(1)}, bf16[32,3072]{1,0:T(8,128)(2,1)S(1)}, u32[]{:S(2)}, u32[]{:S(2)}) collective-permute-start(bf16[32,3072]{1,0:T(8,128)(2,1)S(1)} %get-tuple-element.54), channel_id=1, source_target_pairs={{8,4},{12,0},{16,28},{20,24},{9,5},{13,1},{17,29},{21,25},{10,6},{... | collective-permute-start | bytes 589832 | tf_op jit(solution)/shard_map/ppermute | solution.py:370
  81.9 1.6 %collective-permute-start.18 = (f32[4,32,512]{2,1,0:T(8,128)S(1)}, f32[4,32,512]{2,1,0:T(8,128)S(1)}, u32[]{:S(2)}, u32[]{:S(2)}) collective-permute-start(f32[4,32,512]{2,1,0:T(8,128)S(1)} %get-tuple-element.62), channel_id=1, source_target_pairs={{0,1},{1,0},{2,3},{3,2},{4,5},{5,4},{6,7},{7,6},{8,9},{9,8},{10,11... | collective-permute-start | bytes 786440 | tf_op jit(solution)/shard_map/ppermute | solution.py:383
  83.5 5.6 %collective-permute-start.19 = (f32[2,32,512]{2,1,0:T(8,128)S(1)}, f32[2,32,512]{2,1,0:T(8,128)S(1)}, u32[]{:S(2)}, u32[]{:S(2)}) collective-permute-start(f32[2,32,512]{2,1,0:T(8,128)S(1)} %slice.9), channel_id=1, source_target_pairs={{0,2},{1,3},{2,0},{3,1},{4,6},{5,7},{6,4},{7,5},{8,10},{9,11},{10,... | collective-permute-start | bytes 393224 | tf_op jit(solution)/shard_map/ppermute | solution.py:388

commit v6 on v5

--- a/solution.py
+++ b/solution.py
@@ -227,17 +227,15 @@
         total_ref, base = refs[0], 0
         total_ref[...] = jnp.zeros_like(total_ref)
     else:
-        peers, feats = finish
-        early_ref, rows_ref, keep_ref, give_ref, total_ref, early_sems = refs[:-3]
-        last = total_ref.shape[0] - PAIR * size
-        base = last - full * size
-        copies = [
-            pltpu.make_async_copy(early_ref.at[:base], total_ref.at[:base], early_sems.at[0]),
-            pltpu.make_async_copy(early_ref.at[base:], total_ref.at[last:], early_sems.at[1]),
-        ]
+        peers, feats, early = finish
+        early_refs, (rows_ref, keep_ref, give_ref, total_ref, early_sems) = refs[:early], refs[early:-3]
+        base = total_ref.shape[0] - PAIR * size
+        copies, at = [], 0
+        for i, ref in enumerate(early_refs):
+            copies.append(pltpu.make_async_copy(ref, total_ref.at[at : at + ref.shape[0]], early_sems.at[i]))
+            at += ref.shape[0]
         for copy in copies:
             copy.start()
-        total_ref[base:last] = jnp.zeros((full * size, total_ref.shape[1]), total_ref.dtype)
         for copy in copies:
             copy.wait()
 
@@ -278,14 +276,14 @@
         sizes = None
     else:
         peers, feats, early, rows = finish
-        sizes = peers, feats
-        operands += [early, rows]
-        in_specs += [ANY, SMEM]
+        sizes = peers, feats, len(early)
+        operands += [*early, rows]
+        in_specs += [ANY] * len(early) + [SMEM]
         out_shape = [jax.ShapeDtypeStruct((peers // 2, size, examples), jnp.float32)] * 2
         out_specs = [VMEM] * 2
         scratch = [
             pltpu.VMEM((len(slots_of(chain)) * PAIR * size, examples), jnp.float32),
-            pltpu.SemaphoreType.DMA((2,)),
+            pltpu.SemaphoreType.DMA((len(early),)),
         ] + scratch
     return pl.pallas_call(
         functools.partial(product_kernel, chain, full, last_parts, sizes),
@@ -366,7 +364,7 @@
             away[h - 1] = mine, theirs
         mine, theirs = hand(notes, up, down, chain, False)
         if h == 0:
-            receive(1, (mine, theirs))
+            receive(1)
         away[h] = lax.ppermute(mine, "ex", straight), lax.ppermute(theirs, "ex", diagonal)
     tail = {PARTS - 1: away.pop(PARTS - 1)}
 
@@ -377,8 +375,8 @@
     def scores(group, away, finish=None):
         return product([b for s in group for b in blocks[s]], blocks[slots[-1]], away, train_grads, chain, finish)
 
-    early = scores(slots[:2], away)
-    keep, give = scores(slots[2:-1], tail, (peers, feats, early, rows))
+    early = [scores(slots[:2], {}), scores(slots[2:-1], away)]
+    keep, give = scores([], tail, (peers, feats, early, rows))
 
     total = keep + lax.ppermute(give, "feat", [(i, i ^ 1) for i in range(feats)])
     lines, each = feats // 2, peers // feats

time: 90.3 us -> 90 us (level)
  waiting for transfers between devices: 35.8 us -> 32.6 us
  Pallas kernels: 16.6 us -> 19.2 us
    ppermute x4, waiting for transfers between devices: 0.3 us -> 9.83 us  [receive(): blocks[d, second] = [mine, lax.ppermute(theirs, 'ex', pairs)]]
    ppermute x4, waiting for transfers between devices: 6.43 us -> 0.01 us  [along(): below[s, h] = lax.ppermute(below[s - 1, h], 'ex', upward[(s - 1) * PAIR:])]
    ppermute x2, waiting for transfers between devices: 3.18 us -> 0.01 us  [shards(): lax.ppermute(mine, 'ex', straight)]
    ppermute x4, waiting for transfers between devices: 12.7 us -> 9.77 us  [along(): lax.ppermute(above[s - 1, h], 'ex', downward[:len(downward) - (s - 1) * P...]
    pallas_call x2 -> x3, Pallas kernels: 10.6 us -> 13.1 us  [product(): pl.pallas_call(functools.partial(product_kernel, chain, full, last_parts,...]
    ppermute x1, starting transfers between devices: 5.09 us -> 3.43 us  [shards(): notes = lax.ppermute(wants, 'ex', ends)]
    ppermute x4, starting transfers between devices: 10.4 us -> 11.6 us  [along(): below[s, h] = lax.ppermute(below[s - 1, h], 'ex', upward[(s - 1) * PAIR:])]
  transfers between devices with their start and end apart: 20 -> 20, of which waited for: 11 -> 9; matrix products, arithmetic and copies ran while one was open for 1% -> 1% of each run, Pallas kernels for 13% -> 18%
where the time goes in v6:
time: 90 us; the launch traced here: 89.6 us
  starting transfers between devices  34.2 us (38%)
  waiting for transfers between devices  32.6 us (36%)
  Pallas kernels  19.2 us (21%)
  other arithmetic  1.37 us (2%)
  local copies, waits for them, and re-layouts  1.24 us (1%)
  between operations  0.94 us (1%)
    pallas_call x3, Pallas kernels, product(): pl.pallas_call(functools.partial(product_kernel, chain, full, last_parts,...  13.1 us
    ppermute x4, starting transfers between devices, along(): below[s, h] = lax.ppermute(below[s - 1, h], 'ex', upward[(s - 1) * PAIR:])  11.6 us
    ppermute x4, waiting for transfers between devices, receive(): blocks[d, second] = [mine, lax.ppermute(theirs, 'ex', pairs)]  9.83 us
    ppermute x4, waiting for transfers between devices, along(): lax.ppermute(above[s - 1, h], 'ex', downward[:len(downward) - (s - 1) * P...  9.77 us
    ppermute x2, waiting for transfers between devices, shards(): lax.ppermute(theirs, 'ex', diagonal)  5.56 us
    ppermute x4, starting transfers between devices, receive(): blocks[d, second] = [mine, lax.ppermute(theirs, 'ex', pairs)]  5.31 us
    ppermute x4, starting transfers between devices, along(): lax.ppermute(above[s - 1, h], 'ex', downward[:len(downward) - (s - 1) * P...  5.14 us
    ppermute x1, waiting for transfers between devices, shards(): lax.ppermute(send, 'feat', [(i, (i + 2 * away) % feats) for i in range(fe...  4.02 us
  transfers between devices with their start and end apart: 20, of which 9 were waited for; matrix products, arithmetic and copies ran while one was open for 1% of the time, Pallas kernels for 18%

profile of v6, /device:TPU:0, one launch (start us, length us, event | category | flops | bytes accessed | tf_op | source)
XLA Modules:
  0.0 89.6 jit_solution(2182714968293628095)
XLA Ops:
  0.0 1.2 %copy-done = bf16[2,1,32,8192]{3,2,1,0:T(8,128)(2,1)S(1)} copy-done((bf16[2,1,32,8192]{3,2,1,0:T(8,128)(2,1)S(1)}, bf16[2,1,32,8192]{3,2,1,0:T(8,128)(2,1)}, u32[]{:S(2)}) %copy-start) | copy-done | bytes 1048600
  1.3 1.3 %collective-permute-start.1 = (bf16[2,32,5120]{2,1,0:T(8,128)(2,1)S(1)}, bf16[2,32,5120]{2,1,0:T(8,128)(2,1)S(1)}, u32[]{:S(2)}, u32[]{:S(2)}) collective-permute-start(bf16[2,32,5120]{2,1,0:T(8,128)(2,1)S(1)} %get-tuple-element.35.refs_0_), channel_id=1, source_target_pairs={{8,0},{12,4},{16,8},{20,12},{24,16},{28,20},{9,1},{13,5},{17,9},{2... | collective-permute-start | bytes 1966088 | tf_op jit(solution)/shard_map/ppermute | solution.py:313
  2.6 5.6 %collective-permute-start.3 = (bf16[2,32,5120]{2,1,0:T(8,128)(2,1)S(1)}, bf16[2,32,5120]{2,1,0:T(8,128)(2,1)S(1)}, u32[]{:S(2)}, u32[]{:S(2)}) collective-permute-start(bf16[2,32,5120]{2,1,0:T(8,128)(2,1)S(1)} %get-tuple-element.35.refs_0_), channel_id=1, source_target_pairs={{0,8},{4,12},{8,16},{12,20},{16,24},{20,28},{1,9},{5,13},{9,17},{1... | collective-permute-start | bytes 1966088 | tf_op jit(solution)/shard_map/ppermute | solution.py:312
  8.9 1.3 %shard_map.55 = (s32[1,8]{1,0:T(1,128)}, s32[1,8]{1,0:T(1,128)}) custom-call(s32[16]{0:T(128)} %owner_ref.1, s32[1,8]{1,0:T(1,128)} %pairs_ref.1, s32[1]{0:T(128)S(6)} %copy.6.counts_ref), custom_call_target="tpu_custom_call" | custom-call | tf_op jit(solution)/shard_map/pallas_call | solution.py:55
  10.2 1.9 %collective-permute-start = (s32[1,8]{1,0:T(1,128)}, s32[1,8]{1,0:T(1,128)S(1)}, u32[]{:S(2)}, u32[]{:S(2)}) collective-permute-start(s32[1,8]{1,0:T(1,128)} %get-tuple-element.34), channel_id=1, source_target_pairs={{0,4},{4,0},{8,12},{12,8},{16,20},{20,16},{24,28},{28,24},{1,5},{5... | collective-permute-start | bytes 104 | tf_op jit(solution)/shard_map/ppermute | solution.py:318
  12.2 1.7 %collective-permute-done = s32[1,8]{1,0:T(1,128)S(1)} collective-permute-done((s32[1,8]{1,0:T(1,128)}, s32[1,8]{1,0:T(1,128)S(1)}, u32[]{:S(2)}, u32[]{:S(2)}) %collective-permute-start) | collective-permute-done | bytes 64 | tf_op jit(solution)/shard_map/ppermute | solution.py:318
  15.4 2.0 %collective-permute-start.6 = (bf16[32,8192]{1,0:T(8,128)(2,1)S(1)}, bf16[32,8192]{1,0:T(8,128)(2,1)S(1)}, u32[]{:S(2)}, u32[]{:S(2)}) collective-permute-start(bf16[32,8192]{1,0:T(8,128)(2,1)S(1)} %get-tuple-element.38), channel_id=1, source_target_pairs={{0,4},{4,0},{8,12},{12,8},{16,20},{20,16},{24,28},{28,24},{1,5},{5... | collective-permute-start | bytes 1572872 | tf_op jit(solution)/shard_map/ppermute | solution.py:340
  17.4 1.3 %collective-permute-start.2 = (bf16[2,32,3072]{2,1,0:T(8,128)(2,1)S(1)}, bf16[2,32,3072]{2,1,0:T(8,128)(2,1)S(1)}, u32[]{:S(2)}, u32[]{:S(2)}) collective-permute-start(bf16[2,32,3072]{2,1,0:T(8,128)(2,1)S(1)} %get-tuple-element.36.refs_1_), channel_id=1, source_target_pairs={{8,0},{12,4},{16,8},{20,12},{24,16},{28,20},{9,1},{13,5},{17,9},{2... | collective-permute-start | bytes 1179656 | tf_op jit(solution)/shard_map/ppermute | solution.py:313
  18.7 4.6 %collective-permute-start.4 = (bf16[2,32,3072]{2,1,0:T(8,128)(2,1)S(1)}, bf16[2,32,3072]{2,1,0:T(8,128)(2,1)S(1)}, u32[]{:S(2)}, u32[]{:S(2)}) collective-permute-start(bf16[2,32,3072]{2,1,0:T(8,128)(2,1)S(1)} %get-tuple-element.36.refs_1_), channel_id=1, source_target_pairs={{0,8},{4,12},{8,16},{12,20},{16,24},{20,28},{1,9},{5,13},{9,17},{1... | collective-permute-start | bytes 1179656 | tf_op jit(solution)/shard_map/ppermute | solution.py:312
  23.3 1.3 %collective-permute-start.11 = (bf16[2,32,5120]{2,1,0:T(8,128)(2,1)S(1)}, bf16[2,32,5120]{2,1,0:T(8,128)(2,1)S(1)}, u32[]{:S(2)}, u32[]{:S(2)}) collective-permute-start(bf16[2,32,5120]{2,1,0:T(8,128)(2,1)S(1)} %collective-permute-done.1.refs_0_), channel_id=1, source_target_pairs={{8,0},{12,4},{16,8},{20,12},{9,1},{13,5},{17,9},{21,13},{10,2},{14... | collective-permute-start | bytes 1966088 | tf_op jit(solution)/shard_map/ppermute | solution.py:313
  25.3 6.0 %collective-permute-done.2.refs_1_ = bf16[2,32,3072]{2,1,0:T(8,128)(2,1)S(1)} collective-permute-done((bf16[2,32,3072]{2,1,0:T(8,128)(2,1)S(1)}, bf16[2,32,3072]{2,1,0:T(8,128)(2,1)S(1)}, u32[]{:S(2)}, u32[]{:S(2)}) %collective-permute-start.2) | collective-permute-done | bytes 393248 | tf_op jit(solution)/shard_map/ppermute | solution.py:313
  31.3 3.4 %collective-permute-start.5 = (s32[2,8]{1,0:T(2,128)S(1)}, s32[2,8]{1,0:T(2,128)S(1)}, u32[]{:S(2)}, u32[]{:S(2)}) collective-permute-start(s32[2,8]{1,0:T(2,128)S(1)} %pad_add_fusion.wants_ref), channel_id=1, source_target_pairs={{0,8},{4,12},{24,16},{28,20},{1,9},{5,13},{25,17},{29,21},{2,10},{... | collective-permute-start | bytes 200 | tf_op jit(solution)/shard_map/ppermute | solution.py:321
  34.8 1.1 %shard_map.57 = (bf16[32,8192]{1,0:T(8,128)(2,1)S(1)}, bf16[32,8192]{1,0:T(8,128)(2,1)S(1)}, bf16[32,8192]{1,0:T(8,128)(2,1)S(1)}, bf16[32,8192]{1,0:T(8,128)(2,1)S(1)}) custom-call(s32[2,8]{1,0:T(2,128)S(1)} %pad_add_fusion.wants_ref, bf16[2,32,5120]{2,1,0:T(8,128)(2,1)S(1)} %collective-permute-done.1.refs_0_, ...), custom_call_target="tpu_custom_call" | custom-call | tf_op jit(solution)/shard_map/pallas_call | solution.py:106
  36.1 0.9 %collective-permute-start.7 = (bf16[32,8192]{1,0:T(8,128)(2,1)S(1)}, bf16[32,8192]{1,0:T(8,128)(2,1)S(1)}, u32[]{:S(2)}, u32[]{:S(2)}) collective-permute-start(bf16[32,8192]{1,0:T(8,128)(2,1)S(1)} %get-tuple-element.42), channel_id=1, source_target_pairs={{0,4},{4,0},{8,12},{12,8},{16,20},{20,16},{24,28},{28,24},{1,5},{5... | collective-permute-start | bytes 1572872 | tf_op jit(solution)/shard_map/ppermute | solution.py:340
  37.0 1.3 %collective-permute-start.9 = (bf16[2,32,3072]{2,1,0:T(8,128)(2,1)S(1)}, bf16[2,32,3072]{2,1,0:T(8,128)(2,1)S(1)}, u32[]{:S(2)}, u32[]{:S(2)}) collective-permute-start(bf16[2,32,3072]{2,1,0:T(8,128)(2,1)S(1)} %collective-permute-done.2.refs_1_), channel_id=1, source_target_pairs={{8,0},{12,4},{16,8},{20,12},{9,1},{13,5},{17,9},{21,13},{10,2},{14... | collective-permute-start | bytes 1179656 | tf_op jit(solution)/shard_map/ppermute | solution.py:313
  39.0 7.5 %collective-permute-done.7.refs_3_ = bf16[32,8192]{1,0:T(8,128)(2,1)S(1)} collective-permute-done((bf16[32,8192]{1,0:T(8,128)(2,1)S(1)}, bf16[32,8192]{1,0:T(8,128)(2,1)S(1)}, u32[]{:S(2)}, u32[]{:S(2)}) %collective-permute-start.7) | collective-permute-done | bytes 524320 | tf_op jit(solution)/shard_map/ppermute | solution.py:340
  48.0 1.3 %collective-permute-start.13 = (bf16[32,5120]{1,0:T(8,128)(2,1)S(1)}, bf16[32,5120]{1,0:T(8,128)(2,1)S(1)}, u32[]{:S(2)}, u32[]{:S(2)}) collective-permute-start(bf16[32,5120]{1,0:T(8,128)(2,1)S(1)} %get-tuple-element.47), channel_id=1, source_target_pairs={{8,4},{12,0},{16,28},{20,24},{9,5},{13,1},{17,29},{21,25},{10,6},{... | collective-permute-start | bytes 983048 | tf_op jit(solution)/shard_map/ppermute | solution.py:368
  49.3 3.7 %collective-permute-done.9.above_ref.refs_1_ = bf16[2,32,3072]{2,1,0:T(8,128)(2,1)S(1)} collective-permute-done((bf16[2,32,3072]{2,1,0:T(8,128)(2,1)S(1)}, bf16[2,32,3072]{2,1,0:T(8,128)(2,1)S(1)}, u32[]{:S(2)}, u32[]{:S(2)}) %collective-permute-start.9) | collective-permute-done | bytes 393248 | tf_op jit(solution)/shard_map/ppermute | solution.py:313
  53.1 0.8 shard_map.62
  53.9 1.7 %collective-permute-start.16 = (bf16[32,8192]{1,0:T(8,128)(2,1)S(1)}, bf16[32,8192]{1,0:T(8,128)(2,1)S(1)}, u32[]{:S(2)}, u32[]{:S(2)}) collective-permute-start(bf16[32,8192]{1,0:T(8,128)(2,1)S(1)} %get-tuple-element.57), channel_id=1, source_target_pairs={{0,4},{4,0},{8,12},{12,8},{16,20},{20,16},{24,28},{28,24},{1,5},{5... | collective-permute-start | bytes 1572872 | tf_op jit(solution)/shard_map/ppermute | solution.py:340
  55.6 1.3 %collective-permute-start.17 = (bf16[32,5120]{1,0:T(8,128)(2,1)S(1)}, bf16[32,5120]{1,0:T(8,128)(2,1)S(1)}, u32[]{:S(2)}, u32[]{:S(2)}) collective-permute-start(bf16[32,5120]{1,0:T(8,128)(2,1)S(1)} %get-tuple-element.58), channel_id=1, source_target_pairs={{8,0},{12,4},{16,24},{20,28},{9,1},{13,5},{17,25},{21,29},{10,2},{... | collective-permute-start | bytes 983048 | tf_op jit(solution)/shard_map/ppermute | solution.py:368
  56.9 5.6 %collective-permute-done.13.refs_5_ = bf16[32,5120]{1,0:T(8,128)(2,1)S(1)} collective-permute-done((bf16[32,5120]{1,0:T(8,128)(2,1)S(1)}, bf16[32,5120]{1,0:T(8,128)(2,1)S(1)}, u32[]{:S(2)}, u32[]{:S(2)}) %collective-permute-start.13) | collective-permute-done | bytes 327712 | tf_op jit(solution)/shard_map/ppermute | solution.py:368
  62.4 1.1 %shard_map.60 = (bf16[32,3072]{1,0:T(8,128)(2,1)S(1)}, bf16[32,3072]{1,0:T(8,128)(2,1)S(1)}) custom-call(s32[2,8]{1,0:T(2,128)S(1)} %collective-permute-done.5.notes_ref, bf16[2,32,3072]{2,1,0:T(8,128)(2,1)S(1)} %collective-permute-done.9.above_ref.refs_1_, bf16[2,32,3072]{2,1,0:T(8,128)(2,1)S(1)} %collective-permute-done.10.below_ref.refs_3_), custom_call_target="tpu_custom_call" | custom-call | tf_op jit(solution)/shard_map/pallas_call | solution.py:164
  63.6 1.3 %collective-permute-start.14 = (bf16[32,3072]{1,0:T(8,128)(2,1)S(1)}, bf16[32,3072]{1,0:T(8,128)(2,1)S(1)}, u32[]{:S(2)}, u32[]{:S(2)}) collective-permute-start(bf16[32,3072]{1,0:T(8,128)(2,1)S(1)} %get-tuple-element.50), channel_id=1, source_target_pairs={{8,0},{12,4},{16,24},{20,28},{9,1},{13,5},{17,25},{21,29},{10,2},{... | collective-permute-start | bytes 589832 | tf_op jit(solution)/shard_map/ppermute | solution.py:368
  64.9 1.3 %collective-permute-start.15 = (bf16[32,3072]{1,0:T(8,128)(2,1)S(1)}, bf16[32,3072]{1,0:T(8,128)(2,1)S(1)}, u32[]{:S(2)}, u32[]{:S(2)}) collective-permute-start(bf16[32,3072]{1,0:T(8,128)(2,1)S(1)} %get-tuple-element.51), channel_id=1, source_target_pairs={{8,4},{12,0},{16,28},{20,24},{9,5},{13,1},{17,29},{21,25},{10,6},{... | collective-permute-start | bytes 589832 | tf_op jit(solution)/shard_map/ppermute | solution.py:368
  66.2 4.9 %shard_map.61.refs_5_ = f32[128,512]{1,0:T(8,128)S(1)} custom-call(bf16[32,8192]{1,0:T(8,128)(2,1)S(1)} %get-tuple-element.52.refs_0_, bf16[32,8192]{1,0:T(8,128)(2,1)S(1)} %collective-permute-done.6.refs_1_, bf16[32,8192]{1,0:T(8,128)(2,1)S(1)} %get-tuple-element.54.refs_2_, bf16[32,8192]{1,0:T(8,128)(2,1)S(1)} %collective-permute-done.7.refs_3_, ...), custom_call_target="tpu_custom_call" | custom-call | tf_op jit(solution)/shard_map/pallas_call | solution.py:288
  71.1 2.3 %collective-permute-done.16.refs_1_ = bf16[32,8192]{1,0:T(8,128)(2,1)S(1)} collective-permute-done((bf16[32,8192]{1,0:T(8,128)(2,1)S(1)}, bf16[32,8192]{1,0:T(8,128)(2,1)S(1)}, u32[]{:S(2)}, u32[]{:S(2)}) %collective-permute-start.16) | collective-permute-done | bytes 524320 | tf_op jit(solution)/shard_map/ppermute | solution.py:340
  73.3 4.9 %shard_map.63.refs_6_ = f32[128,512]{1,0:T(8,128)S(1)} custom-call(bf16[32,8192]{1,0:T(8,128)(2,1)S(1)} %get-tuple-element.56.refs_0_, bf16[32,8192]{1,0:T(8,128)(2,1)S(1)} %collective-permute-done.16.refs_1_, bf16[32,8192]{1,0:T(8,128)(2,1)S(1)} %get-tuple-element.37.refs_2_.refs_0_, bf16[32,8192]{1,0:T(8,128)(2,1)S(1)} %collective-permute-done.8.refs_3_.refs_1_, ...), custom_call_target="tpu_custom_call" | custom-call | tf_op jit(solution)/shard_map/pallas_call | solution.py:288
  78.3 3.3 %shard_map.64 = (f32[4,32,512]{2,1,0:T(8,128)S(1)}, f32[4,32,512]{2,1,0:T(8,128)S(1)}) custom-call(bf16[32,8192]{1,0:T(8,128)(2,1)S(1)} %get-tuple-element.37.refs_2_.refs_0_, bf16[32,8192]{1,0:T(8,128)(2,1)S(1)} %collective-permute-done.8.refs_3_.refs_1_, bf16[32,3072]{1,0:T(8,128)(2,1)S(1)} %collective-permute-done.14.refs_2_, ...), custom_call_target="tpu_custom_call" | custom-call | tf_op jit(solution)/shard_map/pallas_call | solution.py:288
  81.7 1.5 %collective-permute-done.18 = f32[4,32,512]{2,1,0:T(8,128)S(1)} collective-permute-done((f32[4,32,512]{2,1,0:T(8,128)S(1)}, f32[4,32,512]{2,1,0:T(8,128)S(1)}, u32[]{:S(2)}, u32[]{:S(2)}) %collective-permute-start.18) | collective-permute-done | bytes 262176 | tf_op jit(solution)/shard_map/ppermute | solution.py:381
  83.3 1.6 %collective-permute-start.19 = (f32[2,32,512]{2,1,0:T(8,128)S(1)}, f32[2,32,512]{2,1,0:T(8,128)S(1)}, u32[]{:S(2)}, u32[]{:S(2)}) collective-permute-start(f32[2,32,512]{2,1,0:T(8,128)S(1)} %slice.9), channel_id=1, source_target_pairs={{0,2},{1,3},{2,0},{3,1},{4,6},{5,7},{6,4},{7,5},{8,10},{9,11},{10,... | collective-permute-start | bytes 393224 | tf_op jit(solution)/shard_map/ppermute | solution.py:386
  84.9 4.0 %collective-permute-done.19 = f32[2,32,512]{2,1,0:T(8,128)S(1)} collective-permute-done((f32[2,32,512]{2,1,0:T(8,128)S(1)}, f32[2,32,512]{2,1,0:T(8,128)S(1)}, u32[]{:S(2)}, u32[]{:S(2)}) %collective-permute-start.19) | collective-permute-done | bytes 131104 | tf_op jit(solution)/shard_map/ppermute | solution.py:386
  (26 shorter events, 5.5 us)
Async XLA Ops:
  0.0 1.2 %copy-start = (bf16[2,1,32,8192]{3,2,1,0:T(8,128)(2,1)S(1)}, bf16[2,1,32,8192]{3,2,1,0:T(8,128)(2,1)}, u32[]{:S(2)}) copy-start(bf16[2,1,32,8192]{3,2,1,0:T(8,128)(2,1)} %param.6) | copy-start | bytes 3145732
  1.3 21.9 %collective-permute-start.1 = (bf16[2,32,5120]{2,1,0:T(8,128)(2,1)S(1)}, bf16[2,32,5120]{2,1,0:T(8,128)(2,1)S(1)}, u32[]{:S(2)}, u32[]{:S(2)}) collective-permute-start(bf16[2,32,5120]{2,1,0:T(8,128)(2,1)S(1)} %get-tuple-element.35.refs_0_), channel_id=1, source_target_pairs={{8,0},{12,4},{16,8},{20,12},{24,16},{28,20},{9,1},{13,5},{17,9},{2... | collective-permute-start | bytes 1966088 | tf_op jit(solution)/shard_map/ppermute | solution.py:313
  2.6 21.9 %collective-permute-start.3 = (bf16[2,32,5120]{2,1,0:T(8,128)(2,1)S(1)}, bf16[2,32,5120]{2,1,0:T(8,128)(2,1)S(1)}, u32[]{:S(2)}, u32[]{:S(2)}) collective-permute-start(bf16[2,32,5120]{2,1,0:T(8,128)(2,1)S(1)} %get-tuple-element.35.refs_0_), channel_id=1, source_target_pairs={{0,8},{4,12},{8,16},{12,20},{16,24},{20,28},{1,9},{5,13},{9,17},{1... | collective-permute-start | bytes 1966088 | tf_op jit(solution)/shard_map/ppermute | solution.py:312
  10.2 3.7 %collective-permute-start = (s32[1,8]{1,0:T(1,128)}, s32[1,8]{1,0:T(1,128)S(1)}, u32[]{:S(2)}, u32[]{:S(2)}) collective-permute-start(s32[1,8]{1,0:T(1,128)} %get-tuple-element.34), channel_id=1, source_target_pairs={{0,4},{4,0},{8,12},{12,8},{16,20},{20,16},{24,28},{28,24},{1,5},{5... | collective-permute-start | bytes 104 | tf_op jit(solution)/shard_map/ppermute | solution.py:318
  15.4 20.7 %collective-permute-start.6 = (bf16[32,8192]{1,0:T(8,128)(2,1)S(1)}, bf16[32,8192]{1,0:T(8,128)(2,1)S(1)}, u32[]{:S(2)}, u32[]{:S(2)}) collective-permute-start(bf16[32,8192]{1,0:T(8,128)(2,1)S(1)} %get-tuple-element.38), channel_id=1, source_target_pairs={{0,4},{4,0},{8,12},{12,8},{16,20},{20,16},{24,28},{28,24},{1,5},{5... | collective-permute-start | bytes 1572872 | tf_op jit(solution)/shard_map/ppermute | solution.py:340
  17.4 13.9 %collective-permute-start.2 = (bf16[2,32,3072]{2,1,0:T(8,128)(2,1)S(1)}, bf16[2,32,3072]{2,1,0:T(8,128)(2,1)S(1)}, u32[]{:S(2)}, u32[]{:S(2)}) collective-permute-start(bf16[2,32,3072]{2,1,0:T(8,128)(2,1)S(1)} %get-tuple-element.36.refs_1_), channel_id=1, source_target_pairs={{8,0},{12,4},{16,8},{20,12},{24,16},{28,20},{9,1},{13,5},{17,9},{2... | collective-permute-start | bytes 1179656 | tf_op jit(solution)/shard_map/ppermute | solution.py:313
  18.7 16.1 %collective-permute-start.4 = (bf16[2,32,3072]{2,1,0:T(8,128)(2,1)S(1)}, bf16[2,32,3072]{2,1,0:T(8,128)(2,1)S(1)}, u32[]{:S(2)}, u32[]{:S(2)}) collective-permute-start(bf16[2,32,3072]{2,1,0:T(8,128)(2,1)S(1)} %get-tuple-element.36.refs_1_), channel_id=1, source_target_pairs={{0,8},{4,12},{8,16},{12,20},{16,24},{20,28},{1,9},{5,13},{9,17},{1... | collective-permute-start | bytes 1179656 | tf_op jit(solution)/shard_map/ppermute | solution.py:312
  23.3 23.9 %collective-permute-start.11 = (bf16[2,32,5120]{2,1,0:T(8,128)(2,1)S(1)}, bf16[2,32,5120]{2,1,0:T(8,128)(2,1)S(1)}, u32[]{:S(2)}, u32[]{:S(2)}) collective-permute-start(bf16[2,32,5120]{2,1,0:T(8,128)(2,1)S(1)} %collective-permute-done.1.refs_0_), channel_id=1, source_target_pairs={{8,0},{12,4},{16,8},{20,12},{9,1},{13,5},{17,9},{21,13},{10,2},{14... | collective-permute-start | bytes 1966088 | tf_op jit(solution)/shard_map/ppermute | solution.py:313
  24.6 22.6 %collective-permute-start.12 = (bf16[2,32,5120]{2,1,0:T(8,128)(2,1)S(1)}, bf16[2,32,5120]{2,1,0:T(8,128)(2,1)S(1)}, u32[]{:S(2)}, u32[]{:S(2)}) collective-permute-start(bf16[2,32,5120]{2,1,0:T(8,128)(2,1)S(1)} %collective-permute-done.3.refs_2_), channel_id=1, source_target_pairs={{8,16},{12,20},{16,24},{20,28},{9,17},{13,21},{17,25},{21,29},{10,... | collective-permute-start | bytes 1966088 | tf_op jit(solution)/shard_map/ppermute | solution.py:312
  31.3 4.7 %collective-permute-start.5 = (s32[2,8]{1,0:T(2,128)S(1)}, s32[2,8]{1,0:T(2,128)S(1)}, u32[]{:S(2)}, u32[]{:S(2)}) collective-permute-start(s32[2,8]{1,0:T(2,128)S(1)} %pad_add_fusion.wants_ref), channel_id=1, source_target_pairs={{0,8},{4,12},{24,16},{28,20},{1,9},{5,13},{25,17},{29,21},{2,10},{... | collective-permute-start | bytes 200 | tf_op jit(solution)/shard_map/ppermute | solution.py:321
  36.1 10.5 %collective-permute-start.7 = (bf16[32,8192]{1,0:T(8,128)(2,1)S(1)}, bf16[32,8192]{1,0:T(8,128)(2,1)S(1)}, u32[]{:S(2)}, u32[]{:S(2)}) collective-permute-start(bf16[32,8192]{1,0:T(8,128)(2,1)S(1)} %get-tuple-element.42), channel_id=1, source_target_pairs={{0,4},{4,0},{8,12},{12,8},{16,20},{20,16},{24,28},{28,24},{1,5},{5... | collective-permute-start | bytes 1572872 | tf_op jit(solution)/shard_map/ppermute | solution.py:340
  37.0 16.1 %collective-permute-start.9 = (bf16[2,32,3072]{2,1,0:T(8,128)(2,1)S(1)}, bf16[2,32,3072]{2,1,0:T(8,128)(2,1)S(1)}, u32[]{:S(2)}, u32[]{:S(2)}) collective-permute-start(bf16[2,32,3072]{2,1,0:T(8,128)(2,1)S(1)} %collective-permute-done.2.refs_1_), channel_id=1, source_target_pairs={{8,0},{12,4},{16,8},{20,12},{9,1},{13,5},{17,9},{21,13},{10,2},{14... | collective-permute-start | bytes 1179656 | tf_op jit(solution)/shard_map/ppermute | solution.py:313
  38.3 14.8 %collective-permute-start.10 = (bf16[2,32,3072]{2,1,0:T(8,128)(2,1)S(1)}, bf16[2,32,3072]{2,1,0:T(8,128)(2,1)S(1)}, u32[]{:S(2)}, u32[]{:S(2)}) collective-permute-start(bf16[2,32,3072]{2,1,0:T(8,128)(2,1)S(1)} %collective-permute-done.4.refs_3_), channel_id=1, source_target_pairs={{8,16},{12,20},{16,24},{20,28},{9,17},{13,21},{17,25},{21,29},{10,... | collective-permute-start | bytes 1179656 | tf_op jit(solution)/shard_map/ppermute | solution.py:312
  46.5 24.5 %collective-permute-start.8 = (bf16[32,8192]{1,0:T(8,128)(2,1)S(1)}, bf16[32,8192]{1,0:T(8,128)(2,1)S(1)}, u32[]{:S(2)}, u32[]{:S(2)}) collective-permute-start(bf16[32,8192]{1,0:T(8,128)(2,1)S(1)} %get-tuple-element.43), channel_id=1, source_target_pairs={{8,12},{12,8},{16,20},{20,16},{9,13},{13,9},{17,21},{21,17},{10,14... | collective-permute-start | bytes 1572872 | tf_op jit(solution)/shard_map/ppermute | solution.py:340
  48.0 14.4 %collective-permute-start.13 = (bf16[32,5120]{1,0:T(8,128)(2,1)S(1)}, bf16[32,5120]{1,0:T(8,128)(2,1)S(1)}, u32[]{:S(2)}, u32[]{:S(2)}) collective-permute-start(bf16[32,5120]{1,0:T(8,128)(2,1)S(1)} %get-tuple-element.47), channel_id=1, source_target_pairs={{8,4},{12,0},{16,28},{20,24},{9,5},{13,1},{17,29},{21,25},{10,6},{... | collective-permute-start | bytes 983048 | tf_op jit(solution)/shard_map/ppermute | solution.py:368
  53.9 19.4 %collective-permute-start.16 = (bf16[32,8192]{1,0:T(8,128)(2,1)S(1)}, bf16[32,8192]{1,0:T(8,128)(2,1)S(1)}, u32[]{:S(2)}, u32[]{:S(2)}) collective-permute-start(bf16[32,8192]{1,0:T(8,128)(2,1)S(1)} %get-tuple-element.57), channel_id=1, source_target_pairs={{0,4},{4,0},{8,12},{12,8},{16,20},{20,16},{24,28},{28,24},{1,5},{5... | collective-permute-start | bytes 1572872 | tf_op jit(solution)/shard_map/ppermute | solution.py:340
  55.6 15.4 %collective-permute-start.17 = (bf16[32,5120]{1,0:T(8,128)(2,1)S(1)}, bf16[32,5120]{1,0:T(8,128)(2,1)S(1)}, u32[]{:S(2)}, u32[]{:S(2)}) collective-permute-start(bf16[32,5120]{1,0:T(8,128)(2,1)S(1)} %get-tuple-element.58), channel_id=1, source_target_pairs={{8,0},{12,4},{16,24},{20,28},{9,1},{13,5},{17,25},{21,29},{10,2},{... | collective-permute-start | bytes 983048 | tf_op jit(solution)/shard_map/ppermute | solution.py:368
  63.6 14.7 %collective-permute-start.14 = (bf16[32,3072]{1,0:T(8,128)(2,1)S(1)}, bf16[32,3072]{1,0:T(8,128)(2,1)S(1)}, u32[]{:S(2)}, u32[]{:S(2)}) collective-permute-start(bf16[32,3072]{1,0:T(8,128)(2,1)S(1)} %get-tuple-element.50), channel_id=1, source_target_pairs={{8,0},{12,4},{16,24},{20,28},{9,1},{13,5},{17,25},{21,29},{10,2},{... | collective-permute-start | bytes 589832 | tf_op jit(solution)/shard_map/ppermute | solution.py:368
  64.9 13.4 %collective-permute-start.15 = (bf16[32,3072]{1,0:T(8,128)(2,1)S(1)}, bf16[32,3072]{1,0:T(8,128)(2,1)S(1)}, u32[]{:S(2)}, u32[]{:S(2)}) collective-permute-start(bf16[32,3072]{1,0:T(8,128)(2,1)S(1)} %get-tuple-element.51), channel_id=1, source_target_pairs={{8,4},{12,0},{16,28},{20,24},{9,5},{13,1},{17,29},{21,25},{10,6},{... | collective-permute-start | bytes 589832 | tf_op jit(solution)/shard_map/ppermute | solution.py:368
  71.0 7.3 %copy-start.1 = (s32[1,8]{1,0:T(1,128)S(1)}, s32[1,8]{1,0:T(1,128)}, u32[]{:S(2)}) copy-start(s32[1,8]{1,0:T(1,128)} %get-tuple-element.60.refs_7_) | copy-start | bytes 100
  81.6 1.6 %collective-permute-start.18 = (f32[4,32,512]{2,1,0:T(8,128)S(1)}, f32[4,32,512]{2,1,0:T(8,128)S(1)}, u32[]{:S(2)}, u32[]{:S(2)}) collective-permute-start(f32[4,32,512]{2,1,0:T(8,128)S(1)} %get-tuple-element.62), channel_id=1, source_target_pairs={{0,1},{1,0},{2,3},{3,2},{4,5},{5,4},{6,7},{7,6},{8,9},{9,8},{10,11... | collective-permute-start | bytes 786440 | tf_op jit(solution)/shard_map/ppermute | solution.py:381
  83.3 5.6 %collective-permute-start.19 = (f32[2,32,512]{2,1,0:T(8,128)S(1)}, f32[2,32,512]{2,1,0:T(8,128)S(1)}, u32[]{:S(2)}, u32[]{:S(2)}) collective-permute-start(f32[2,32,512]{2,1,0:T(8,128)S(1)} %slice.9), channel_id=1, source_target_pairs={{0,2},{1,3},{2,0},{3,1},{4,6},{5,7},{6,4},{7,5},{8,10},{9,11},{10,... | collective-permute-start | bytes 393224 | tf_op jit(solution)/shard_map/ppermute | solution.py:386

commit v7 on v5

--- a/solution.py
+++ b/solution.py
@@ -366,7 +366,7 @@
             away[h - 1] = mine, theirs
         mine, theirs = hand(notes, up, down, chain, False)
         if h == 0:
-            receive(1, (mine, theirs))
+            receive(1)
         away[h] = lax.ppermute(mine, "ex", straight), lax.ppermute(theirs, "ex", diagonal)
     tail = {PARTS - 1: away.pop(PARTS - 1)}
 

time: 90.3 us -> 90.5 us (level)
    ppermute x4, waiting for transfers between devices: 12.7 us -> 3.9 us  [along(): lax.ppermute(above[s - 1, h], 'ex', downward[:len(downward) - (s - 1) * P...]
    ppermute x4, waiting for transfers between devices: 0.3 us -> 8.24 us  [receive(): blocks[d, second] = [mine, lax.ppermute(theirs, 'ex', pairs)]]
    ppermute x2, waiting for transfers between devices: 5.72 us -> 6.68 us  [shards(): lax.ppermute(theirs, 'ex', diagonal)]
  transfers between devices with their start and end apart: 20 -> 20, of which waited for: 11 -> 9; matrix products, arithmetic and copies ran while one was open for 1% -> 1% of each run, Pallas kernels for 13% -> 13%
where the time goes in v7:
time: 90.5 us; the launch traced here: 90 us
  waiting for transfers between devices  36 us (40%)
  starting transfers between devices  33.9 us (37%)
  Pallas kernels  16.6 us (18%)
  other arithmetic  1.37 us (2%)
  local copies, waits for them, and re-layouts  1.24 us (1%)
  between operations  0.93 us (1%)
    pallas_call x2, Pallas kernels, product(): pl.pallas_call(functools.partial(product_kernel, chain, full, last_parts,...  10.6 us
    ppermute x4, starting transfers between devices, along(): below[s, h] = lax.ppermute(below[s - 1, h], 'ex', upward[(s - 1) * PAIR:])  10.4 us
    ppermute x4, waiting for transfers between devices, receive(): blocks[d, second] = [mine, lax.ppermute(theirs, 'ex', pairs)]  8.24 us
    ppermute x2, waiting for transfers between devices, shards(): lax.ppermute(theirs, 'ex', diagonal)  6.68 us
    ppermute x4, waiting for transfers between devices, along(): below[s, h] = lax.ppermute(below[s - 1, h], 'ex', upward[(s - 1) * PAIR:])  6.43 us
    ppermute x4, starting transfers between devices, along(): lax.ppermute(above[s - 1, h], 'ex', downward[:len(downward) - (s - 1) * P...  5.17 us
    ppermute x1, starting transfers between devices, shards(): notes = lax.ppermute(wants, 'ex', ends)  5.09 us
    ppermute x4, starting transfers between devices, receive(): blocks[d, second] = [mine, lax.ppermute(theirs, 'ex', pairs)]  4.45 us
  transfers between devices with their start and end apart: 20, of which 9 were waited for; matrix products, arithmetic and copies ran while one was open for 1% of the time, Pallas kernels for 13%

profile of v7, /device:TPU:0, one launch (start us, length us, event | category | flops | bytes accessed | tf_op | source)
XLA Modules:
  0.0 90.0 jit_solution(5611745376633898002)
XLA Ops:
  0.0 1.2 %copy-done = bf16[2,1,32,8192]{3,2,1,0:T(8,128)(2,1)S(1)} copy-done((bf16[2,1,32,8192]{3,2,1,0:T(8,128)(2,1)S(1)}, bf16[2,1,32,8192]{3,2,1,0:T(8,128)(2,1)}, u32[]{:S(2)}) %copy-start) | copy-done | bytes 1048600
  1.3 1.3 %collective-permute-start.1 = (bf16[2,32,5120]{2,1,0:T(8,128)(2,1)S(1)}, bf16[2,32,5120]{2,1,0:T(8,128)(2,1)S(1)}, u32[]{:S(2)}, u32[]{:S(2)}) collective-permute-start(bf16[2,32,5120]{2,1,0:T(8,128)(2,1)S(1)} %get-tuple-element.35.refs_0_), channel_id=1, source_target_pairs={{8,0},{12,4},{16,8},{20,12},{24,16},{28,20},{9,1},{13,5},{17,9},{2... | collective-permute-start | bytes 1966088 | tf_op jit(solution)/shard_map/ppermute | solution.py:315
  2.6 5.6 %collective-permute-start.7 = (bf16[2,32,5120]{2,1,0:T(8,128)(2,1)S(1)}, bf16[2,32,5120]{2,1,0:T(8,128)(2,1)S(1)}, u32[]{:S(2)}, u32[]{:S(2)}) collective-permute-start(bf16[2,32,5120]{2,1,0:T(8,128)(2,1)S(1)} %get-tuple-element.35.refs_0_), channel_id=1, source_target_pairs={{0,8},{4,12},{8,16},{12,20},{16,24},{20,28},{1,9},{5,13},{9,17},{1... | collective-permute-start | bytes 1966088 | tf_op jit(solution)/shard_map/ppermute | solution.py:314
  8.9 1.3 %shard_map.55 = (s32[1,8]{1,0:T(1,128)}, s32[1,8]{1,0:T(1,128)}) custom-call(s32[16]{0:T(128)} %owner_ref.1, s32[1,8]{1,0:T(1,128)} %pairs_ref.1, s32[1]{0:T(128)S(6)} %copy.6.counts_ref), custom_call_target="tpu_custom_call" | custom-call | tf_op jit(solution)/shard_map/pallas_call | solution.py:55
  10.2 1.9 %collective-permute-start = (s32[1,8]{1,0:T(1,128)}, s32[1,8]{1,0:T(1,128)S(1)}, u32[]{:S(2)}, u32[]{:S(2)}) collective-permute-start(s32[1,8]{1,0:T(1,128)} %get-tuple-element.34), channel_id=1, source_target_pairs={{0,4},{4,0},{8,12},{12,8},{16,20},{20,16},{24,28},{28,24},{1,5},{5... | collective-permute-start | bytes 104 | tf_op jit(solution)/shard_map/ppermute | solution.py:320
  12.2 1.7 %collective-permute-done = s32[1,8]{1,0:T(1,128)S(1)} collective-permute-done((s32[1,8]{1,0:T(1,128)}, s32[1,8]{1,0:T(1,128)S(1)}, u32[]{:S(2)}, u32[]{:S(2)}) %collective-permute-start) | collective-permute-done | bytes 64 | tf_op jit(solution)/shard_map/ppermute | solution.py:320
  14.6 0.8 shard_map.57
  15.4 2.0 %collective-permute-start.6 = (bf16[32,8192]{1,0:T(8,128)(2,1)S(1)}, bf16[32,8192]{1,0:T(8,128)(2,1)S(1)}, u32[]{:S(2)}, u32[]{:S(2)}) collective-permute-start(bf16[32,8192]{1,0:T(8,128)(2,1)S(1)} %get-tuple-element.37), channel_id=1, source_target_pairs={{0,4},{4,0},{8,12},{12,8},{16,20},{20,16},{24,28},{28,24},{1,5},{5... | collective-permute-start | bytes 1572872 | tf_op jit(solution)/shard_map/ppermute | solution.py:342
  17.4 3.5 %collective-permute-start.3 = (bf16[2,32,3072]{2,1,0:T(8,128)(2,1)S(1)}, bf16[2,32,3072]{2,1,0:T(8,128)(2,1)S(1)}, u32[]{:S(2)}, u32[]{:S(2)}) collective-permute-start(bf16[2,32,3072]{2,1,0:T(8,128)(2,1)S(1)} %get-tuple-element.36.refs_1_), channel_id=1, source_target_pairs={{0,8},{4,12},{8,16},{12,20},{16,24},{20,28},{1,9},{5,13},{9,17},{1... | collective-permute-start | bytes 1179656 | tf_op jit(solution)/shard_map/ppermute | solution.py:314
  20.9 1.3 %collective-permute-start.4 = (bf16[2,32,3072]{2,1,0:T(8,128)(2,1)S(1)}, bf16[2,32,3072]{2,1,0:T(8,128)(2,1)S(1)}, u32[]{:S(2)}, u32[]{:S(2)}) collective-permute-start(bf16[2,32,3072]{2,1,0:T(8,128)(2,1)S(1)} %get-tuple-element.36.refs_1_), channel_id=1, source_target_pairs={{8,0},{12,4},{16,8},{20,12},{24,16},{28,20},{9,1},{13,5},{17,9},{2... | collective-permute-start | bytes 1179656 | tf_op jit(solution)/shard_map/ppermute | solution.py:315
  22.2 1.3 %collective-permute-start.2 = (bf16[2,32,5120]{2,1,0:T(8,128)(2,1)S(1)}, bf16[2,32,5120]{2,1,0:T(8,128)(2,1)S(1)}, u32[]{:S(2)}, u32[]{:S(2)}) collective-permute-start(bf16[2,32,5120]{2,1,0:T(8,128)(2,1)S(1)} %collective-permute-done.1.refs_0_), channel_id=1, source_target_pairs={{8,0},{12,4},{16,8},{20,12},{9,1},{13,5},{17,9},{21,13},{10,2},{14... | collective-permute-start | bytes 1966088 | tf_op jit(solution)/shard_map/ppermute | solution.py:315
  24.2 6.4 %collective-permute-done.3.refs_3_ = bf16[2,32,3072]{2,1,0:T(8,128)(2,1)S(1)} collective-permute-done((bf16[2,32,3072]{2,1,0:T(8,128)(2,1)S(1)}, bf16[2,32,3072]{2,1,0:T(8,128)(2,1)S(1)}, u32[]{:S(2)}, u32[]{:S(2)}) %collective-permute-start.3) | collective-permute-done | bytes 393248 | tf_op jit(solution)/shard_map/ppermute | solution.py:314
  30.6 5.1 %collective-permute-start.5 = (s32[2,8]{1,0:T(2,128)S(1)}, s32[2,8]{1,0:T(2,128)S(1)}, u32[]{:S(2)}, u32[]{:S(2)}) collective-permute-start(s32[2,8]{1,0:T(2,128)S(1)} %pad_add_fusion.wants_ref), channel_id=1, source_target_pairs={{0,8},{4,12},{24,16},{28,20},{1,9},{5,13},{25,17},{29,21},{2,10},{... | collective-permute-start | bytes 200 | tf_op jit(solution)/shard_map/ppermute | solution.py:323
  35.7 1.1 %shard_map.58 = (bf16[32,8192]{1,0:T(8,128)(2,1)S(1)}, bf16[32,8192]{1,0:T(8,128)(2,1)S(1)}, bf16[32,8192]{1,0:T(8,128)(2,1)S(1)}, bf16[32,8192]{1,0:T(8,128)(2,1)S(1)}) custom-call(s32[2,8]{1,0:T(2,128)S(1)} %pad_add_fusion.wants_ref, bf16[2,32,5120]{2,1,0:T(8,128)(2,1)S(1)} %collective-permute-done.1.refs_0_, ...), custom_call_target="tpu_custom_call" | custom-call | tf_op jit(solution)/shard_map/pallas_call | solution.py:106
  37.0 1.5 %collective-permute-start.12 = (bf16[32,8192]{1,0:T(8,128)(2,1)S(1)}, bf16[32,8192]{1,0:T(8,128)(2,1)S(1)}, u32[]{:S(2)}, u32[]{:S(2)}) collective-permute-start(bf16[32,8192]{1,0:T(8,128)(2,1)S(1)} %get-tuple-element.46), channel_id=1, source_target_pairs={{0,4},{4,0},{8,12},{12,8},{16,20},{20,16},{24,28},{28,24},{1,5},{5... | collective-permute-start | bytes 1572872 | tf_op jit(solution)/shard_map/ppermute | solution.py:342
  39.2 1.3 %collective-permute-start.8 = (bf16[2,32,3072]{2,1,0:T(8,128)(2,1)S(1)}, bf16[2,32,3072]{2,1,0:T(8,128)(2,1)S(1)}, u32[]{:S(2)}, u32[]{:S(2)}) collective-permute-start(bf16[2,32,3072]{2,1,0:T(8,128)(2,1)S(1)} %collective-permute-done.4.refs_1_), channel_id=1, source_target_pairs={{8,0},{12,4},{16,8},{20,12},{9,1},{13,5},{17,9},{21,13},{10,2},{14... | collective-permute-start | bytes 1179656 | tf_op jit(solution)/shard_map/ppermute | solution.py:315
  40.5 8.2 %collective-permute-done.12.refs_3_ = bf16[32,8192]{1,0:T(8,128)(2,1)S(1)} collective-permute-done((bf16[32,8192]{1,0:T(8,128)(2,1)S(1)}, bf16[32,8192]{1,0:T(8,128)(2,1)S(1)}, u32[]{:S(2)}, u32[]{:S(2)}) %collective-permute-start.12) | collective-permute-done | bytes 524320 | tf_op jit(solution)/shard_map/ppermute | solution.py:342
  49.4 0.8 shard_map.60
  50.2 1.3 %collective-permute-start.14 = (bf16[32,5120]{1,0:T(8,128)(2,1)S(1)}, bf16[32,5120]{1,0:T(8,128)(2,1)S(1)}, u32[]{:S(2)}, u32[]{:S(2)}) collective-permute-start(bf16[32,5120]{1,0:T(8,128)(2,1)S(1)} %get-tuple-element.49), channel_id=1, source_target_pairs={{8,4},{12,0},{16,28},{20,24},{9,5},{13,1},{17,29},{21,25},{10,6},{... | collective-permute-start | bytes 983048 | tf_op jit(solution)/shard_map/ppermute | solution.py:370
  51.5 3.9 %collective-permute-done.8.refs_1_.above_ref = bf16[2,32,3072]{2,1,0:T(8,128)(2,1)S(1)} collective-permute-done((bf16[2,32,3072]{2,1,0:T(8,128)(2,1)S(1)}, bf16[2,32,3072]{2,1,0:T(8,128)(2,1)S(1)}, u32[]{:S(2)}, u32[]{:S(2)}) %collective-permute-start.8) | collective-permute-done | bytes 393248 | tf_op jit(solution)/shard_map/ppermute | solution.py:315
  55.4 0.8 shard_map.59
  56.5 1.3 %collective-permute-start.17 = (bf16[32,5120]{1,0:T(8,128)(2,1)S(1)}, bf16[32,5120]{1,0:T(8,128)(2,1)S(1)}, u32[]{:S(2)}, u32[]{:S(2)}) collective-permute-start(bf16[32,5120]{1,0:T(8,128)(2,1)S(1)} %get-tuple-element.58), channel_id=1, source_target_pairs={{8,0},{12,4},{16,24},{20,28},{9,1},{13,5},{17,25},{21,29},{10,2},{... | collective-permute-start | bytes 983048 | tf_op jit(solution)/shard_map/ppermute | solution.py:370
  57.8 6.7 %collective-permute-done.14.refs_7_ = bf16[32,5120]{1,0:T(8,128)(2,1)S(1)} collective-permute-done((bf16[32,5120]{1,0:T(8,128)(2,1)S(1)}, bf16[32,5120]{1,0:T(8,128)(2,1)S(1)}, u32[]{:S(2)}, u32[]{:S(2)}) %collective-permute-start.14) | collective-permute-done | bytes 327712 | tf_op jit(solution)/shard_map/ppermute | solution.py:370
  64.5 1.1 %shard_map.61 = (bf16[32,3072]{1,0:T(8,128)(2,1)S(1)}, bf16[32,3072]{1,0:T(8,128)(2,1)S(1)}) custom-call(s32[2,8]{1,0:T(2,128)S(1)} %collective-permute-done.5.notes_ref, bf16[2,32,3072]{2,1,0:T(8,128)(2,1)S(1)} %collective-permute-done.8.refs_1_.above_ref, bf16[2,32,3072]{2,1,0:T(8,128)(2,1)S(1)} %collective-permute-done.10.refs_3_.below_ref), custom_call_target="tpu_custom_call" | custom-call | tf_op jit(solution)/shard_map/pallas_call | solution.py:164
  65.6 1.3 %collective-permute-start.15 = (bf16[32,3072]{1,0:T(8,128)(2,1)S(1)}, bf16[32,3072]{1,0:T(8,128)(2,1)S(1)}, u32[]{:S(2)}, u32[]{:S(2)}) collective-permute-start(bf16[32,3072]{1,0:T(8,128)(2,1)S(1)} %get-tuple-element.52), channel_id=1, source_target_pairs={{8,0},{12,4},{16,24},{20,28},{9,1},{13,5},{17,25},{21,29},{10,2},{... | collective-permute-start | bytes 589832 | tf_op jit(solution)/shard_map/ppermute | solution.py:370
  66.9 1.3 %collective-permute-start.16 = (bf16[32,3072]{1,0:T(8,128)(2,1)S(1)}, bf16[32,3072]{1,0:T(8,128)(2,1)S(1)}, u32[]{:S(2)}, u32[]{:S(2)}) collective-permute-start(bf16[32,3072]{1,0:T(8,128)(2,1)S(1)} %get-tuple-element.53), channel_id=1, source_target_pairs={{8,4},{12,0},{16,28},{20,24},{9,5},{13,1},{17,29},{21,25},{10,6},{... | collective-permute-start | bytes 589832 | tf_op jit(solution)/shard_map/ppermute | solution.py:370
  68.2 3.3 %collective-permute-done.17.refs_6_ = bf16[32,5120]{1,0:T(8,128)(2,1)S(1)} collective-permute-done((bf16[32,5120]{1,0:T(8,128)(2,1)S(1)}, bf16[32,5120]{1,0:T(8,128)(2,1)S(1)}, u32[]{:S(2)}, u32[]{:S(2)}) %collective-permute-start.17) | collective-permute-done | bytes 327712 | tf_op jit(solution)/shard_map/ppermute | solution.py:370
  71.5 5.3 %shard_map.62.refs_7_ = f32[192,512]{1,0:T(8,128)S(1)} custom-call(bf16[32,8192]{1,0:T(8,128)(2,1)S(1)} %get-tuple-element.54.refs_0_, bf16[32,8192]{1,0:T(8,128)(2,1)S(1)} %collective-permute-done.6.refs_1_, bf16[32,8192]{1,0:T(8,128)(2,1)S(1)} %get-tuple-element.56.refs_2_, bf16[32,8192]{1,0:T(8,128)(2,1)S(1)} %collective-permute-done.12.refs_3_, ...), custom_call_target="tpu_custom_call" | custom-call | tf_op jit(solution)/shard_map/pallas_call | solution.py:290
  76.8 5.3 %shard_map.63 = (f32[4,32,512]{2,1,0:T(8,128)S(1)}, f32[4,32,512]{2,1,0:T(8,128)S(1)}) custom-call(bf16[32,8192]{1,0:T(8,128)(2,1)S(1)} %get-tuple-element.42.refs_0_, bf16[32,8192]{1,0:T(8,128)(2,1)S(1)} %collective-permute-done.11.refs_1_, bf16[32,8192]{1,0:T(8,128)(2,1)S(1)} %get-tuple-element.44.refs_4_.refs_2_, ...), custom_call_target="tpu_custom_call" | custom-call | tf_op jit(solution)/shard_map/pallas_call | solution.py:290
  82.2 1.5 %collective-permute-done.18 = f32[4,32,512]{2,1,0:T(8,128)S(1)} collective-permute-done((f32[4,32,512]{2,1,0:T(8,128)S(1)}, f32[4,32,512]{2,1,0:T(8,128)S(1)}, u32[]{:S(2)}, u32[]{:S(2)}) %collective-permute-start.18) | collective-permute-done | bytes 262176 | tf_op jit(solution)/shard_map/ppermute | solution.py:383
  83.8 1.6 %collective-permute-start.19 = (f32[2,32,512]{2,1,0:T(8,128)S(1)}, f32[2,32,512]{2,1,0:T(8,128)S(1)}, u32[]{:S(2)}, u32[]{:S(2)}) collective-permute-start(f32[2,32,512]{2,1,0:T(8,128)S(1)} %slice.9), channel_id=1, source_target_pairs={{0,2},{1,3},{2,0},{3,1},{4,6},{5,7},{6,4},{7,5},{8,10},{9,11},{10,... | collective-permute-start | bytes 393224 | tf_op jit(solution)/shard_map/ppermute | solution.py:388
  85.3 4.0 %collective-permute-done.19 = f32[2,32,512]{2,1,0:T(8,128)S(1)} collective-permute-done((f32[2,32,512]{2,1,0:T(8,128)S(1)}, f32[2,32,512]{2,1,0:T(8,128)S(1)}, u32[]{:S(2)}, u32[]{:S(2)}) %collective-permute-start.19) | collective-permute-done | bytes 131104 | tf_op jit(solution)/shard_map/ppermute | solution.py:388
  (25 shorter events, 4.1 us)
Async XLA Ops:
  0.0 1.2 %copy-start = (bf16[2,1,32,8192]{3,2,1,0:T(8,128)(2,1)S(1)}, bf16[2,1,32,8192]{3,2,1,0:T(8,128)(2,1)}, u32[]{:S(2)}) copy-start(bf16[2,1,32,8192]{3,2,1,0:T(8,128)(2,1)} %param.6) | copy-start | bytes 3145732
  1.3 20.8 %collective-permute-start.1 = (bf16[2,32,5120]{2,1,0:T(8,128)(2,1)S(1)}, bf16[2,32,5120]{2,1,0:T(8,128)(2,1)S(1)}, u32[]{:S(2)}, u32[]{:S(2)}) collective-permute-start(bf16[2,32,5120]{2,1,0:T(8,128)(2,1)S(1)} %get-tuple-element.35.refs_0_), channel_id=1, source_target_pairs={{8,0},{12,4},{16,8},{20,12},{24,16},{28,20},{9,1},{13,5},{17,9},{2... | collective-permute-start | bytes 1966088 | tf_op jit(solution)/shard_map/ppermute | solution.py:315
  2.6 20.8 %collective-permute-start.7 = (bf16[2,32,5120]{2,1,0:T(8,128)(2,1)S(1)}, bf16[2,32,5120]{2,1,0:T(8,128)(2,1)S(1)}, u32[]{:S(2)}, u32[]{:S(2)}) collective-permute-start(bf16[2,32,5120]{2,1,0:T(8,128)(2,1)S(1)} %get-tuple-element.35.refs_0_), channel_id=1, source_target_pairs={{0,8},{4,12},{8,16},{12,20},{16,24},{20,28},{1,9},{5,13},{9,17},{1... | collective-permute-start | bytes 1966088 | tf_op jit(solution)/shard_map/ppermute | solution.py:314
  10.2 3.7 %collective-permute-start = (s32[1,8]{1,0:T(1,128)}, s32[1,8]{1,0:T(1,128)S(1)}, u32[]{:S(2)}, u32[]{:S(2)}) collective-permute-start(s32[1,8]{1,0:T(1,128)} %get-tuple-element.34), channel_id=1, source_target_pairs={{0,4},{4,0},{8,12},{12,8},{16,20},{20,16},{24,28},{28,24},{1,5},{5... | collective-permute-start | bytes 104 | tf_op jit(solution)/shard_map/ppermute | solution.py:320
  15.4 21.6 %collective-permute-start.6 = (bf16[32,8192]{1,0:T(8,128)(2,1)S(1)}, bf16[32,8192]{1,0:T(8,128)(2,1)S(1)}, u32[]{:S(2)}, u32[]{:S(2)}) collective-permute-start(bf16[32,8192]{1,0:T(8,128)(2,1)S(1)} %get-tuple-element.37), channel_id=1, source_target_pairs={{0,4},{4,0},{8,12},{12,8},{16,20},{20,16},{24,28},{28,24},{1,5},{5... | collective-permute-start | bytes 1572872 | tf_op jit(solution)/shard_map/ppermute | solution.py:342
  17.4 13.2 %collective-permute-start.3 = (bf16[2,32,3072]{2,1,0:T(8,128)(2,1)S(1)}, bf16[2,32,3072]{2,1,0:T(8,128)(2,1)S(1)}, u32[]{:S(2)}, u32[]{:S(2)}) collective-permute-start(bf16[2,32,3072]{2,1,0:T(8,128)(2,1)S(1)} %get-tuple-element.36.refs_1_), channel_id=1, source_target_pairs={{0,8},{4,12},{8,16},{12,20},{16,24},{20,28},{1,9},{5,13},{9,17},{1... | collective-permute-start | bytes 1179656 | tf_op jit(solution)/shard_map/ppermute | solution.py:314
  20.9 14.9 %collective-permute-start.4 = (bf16[2,32,3072]{2,1,0:T(8,128)(2,1)S(1)}, bf16[2,32,3072]{2,1,0:T(8,128)(2,1)S(1)}, u32[]{:S(2)}, u32[]{:S(2)}) collective-permute-start(bf16[2,32,3072]{2,1,0:T(8,128)(2,1)S(1)} %get-tuple-element.36.refs_1_), channel_id=1, source_target_pairs={{8,0},{12,4},{16,8},{20,12},{24,16},{28,20},{9,1},{13,5},{17,9},{2... | collective-permute-start | bytes 1179656 | tf_op jit(solution)/shard_map/ppermute | solution.py:315
  22.2 27.2 %collective-permute-start.2 = (bf16[2,32,5120]{2,1,0:T(8,128)(2,1)S(1)}, bf16[2,32,5120]{2,1,0:T(8,128)(2,1)S(1)}, u32[]{:S(2)}, u32[]{:S(2)}) collective-permute-start(bf16[2,32,5120]{2,1,0:T(8,128)(2,1)S(1)} %collective-permute-done.1.refs_0_), channel_id=1, source_target_pairs={{8,0},{12,4},{16,8},{20,12},{9,1},{13,5},{17,9},{21,13},{10,2},{14... | collective-permute-start | bytes 1966088 | tf_op jit(solution)/shard_map/ppermute | solution.py:315
  23.5 25.9 %collective-permute-start.9 = (bf16[2,32,5120]{2,1,0:T(8,128)(2,1)S(1)}, bf16[2,32,5120]{2,1,0:T(8,128)(2,1)S(1)}, u32[]{:S(2)}, u32[]{:S(2)}) collective-permute-start(bf16[2,32,5120]{2,1,0:T(8,128)(2,1)S(1)} %collective-permute-done.7.refs_2_), channel_id=1, source_target_pairs={{8,16},{12,20},{16,24},{20,28},{9,17},{13,21},{17,25},{21,29},{10,... | collective-permute-start | bytes 1966088 | tf_op jit(solution)/shard_map/ppermute | solution.py:314
  30.6 6.4 %collective-permute-start.5 = (s32[2,8]{1,0:T(2,128)S(1)}, s32[2,8]{1,0:T(2,128)S(1)}, u32[]{:S(2)}, u32[]{:S(2)}) collective-permute-start(s32[2,8]{1,0:T(2,128)S(1)} %pad_add_fusion.wants_ref), channel_id=1, source_target_pairs={{0,8},{4,12},{24,16},{28,20},{1,9},{5,13},{25,17},{29,21},{2,10},{... | collective-permute-start | bytes 200 | tf_op jit(solution)/shard_map/ppermute | solution.py:323
  37.0 39.8 %copy-start.1 = (s32[1,8]{1,0:T(1,128)S(1)}, s32[1,8]{1,0:T(1,128)}, u32[]{:S(2)}) copy-start(s32[1,8]{1,0:T(1,128)} %get-tuple-element.60.refs_8_) | copy-start | bytes 100
  37.0 11.7 %collective-permute-start.12 = (bf16[32,8192]{1,0:T(8,128)(2,1)S(1)}, bf16[32,8192]{1,0:T(8,128)(2,1)S(1)}, u32[]{:S(2)}, u32[]{:S(2)}) collective-permute-start(bf16[32,8192]{1,0:T(8,128)(2,1)S(1)} %get-tuple-element.46), channel_id=1, source_target_pairs={{0,4},{4,0},{8,12},{12,8},{16,20},{20,16},{24,28},{28,24},{1,5},{5... | collective-permute-start | bytes 1572872 | tf_op jit(solution)/shard_map/ppermute | solution.py:342
  38.5 13.0 %collective-permute-start.10 = (bf16[2,32,3072]{2,1,0:T(8,128)(2,1)S(1)}, bf16[2,32,3072]{2,1,0:T(8,128)(2,1)S(1)}, u32[]{:S(2)}, u32[]{:S(2)}) collective-permute-start(bf16[2,32,3072]{2,1,0:T(8,128)(2,1)S(1)} %collective-permute-done.3.refs_3_), channel_id=1, source_target_pairs={{8,16},{12,20},{16,24},{20,28},{9,17},{13,21},{17,25},{21,29},{10,... | collective-permute-start | bytes 1179656 | tf_op jit(solution)/shard_map/ppermute | solution.py:314
  39.2 16.3 %collective-permute-start.8 = (bf16[2,32,3072]{2,1,0:T(8,128)(2,1)S(1)}, bf16[2,32,3072]{2,1,0:T(8,128)(2,1)S(1)}, u32[]{:S(2)}, u32[]{:S(2)}) collective-permute-start(bf16[2,32,3072]{2,1,0:T(8,128)(2,1)S(1)} %collective-permute-done.4.refs_1_), channel_id=1, source_target_pairs={{8,0},{12,4},{16,8},{20,12},{9,1},{13,5},{17,9},{21,13},{10,2},{14... | collective-permute-start | bytes 1179656 | tf_op jit(solution)/shard_map/ppermute | solution.py:315
  48.7 22.8 %collective-permute-start.13 = (bf16[32,8192]{1,0:T(8,128)(2,1)S(1)}, bf16[32,8192]{1,0:T(8,128)(2,1)S(1)}, u32[]{:S(2)}, u32[]{:S(2)}) collective-permute-start(bf16[32,8192]{1,0:T(8,128)(2,1)S(1)} %get-tuple-element.47), channel_id=1, source_target_pairs={{8,12},{12,8},{16,20},{20,16},{9,13},{13,9},{17,21},{21,17},{10,14... | collective-permute-start | bytes 1572872 | tf_op jit(solution)/shard_map/ppermute | solution.py:342
  50.2 14.3 %collective-permute-start.14 = (bf16[32,5120]{1,0:T(8,128)(2,1)S(1)}, bf16[32,5120]{1,0:T(8,128)(2,1)S(1)}, u32[]{:S(2)}, u32[]{:S(2)}) collective-permute-start(bf16[32,5120]{1,0:T(8,128)(2,1)S(1)} %get-tuple-element.49), channel_id=1, source_target_pairs={{8,4},{12,0},{16,28},{20,24},{9,5},{13,1},{17,29},{21,25},{10,6},{... | collective-permute-start | bytes 983048 | tf_op jit(solution)/shard_map/ppermute | solution.py:370
  56.3 20.6 %collective-permute-start.11 = (bf16[32,8192]{1,0:T(8,128)(2,1)S(1)}, bf16[32,8192]{1,0:T(8,128)(2,1)S(1)}, u32[]{:S(2)}, u32[]{:S(2)}) collective-permute-start(bf16[32,8192]{1,0:T(8,128)(2,1)S(1)} %get-tuple-element.43), channel_id=1, source_target_pairs={{0,4},{4,0},{8,12},{12,8},{16,20},{20,16},{24,28},{28,24},{1,5},{5... | collective-permute-start | bytes 1572872 | tf_op jit(solution)/shard_map/ppermute | solution.py:342
  56.5 14.9 %collective-permute-start.17 = (bf16[32,5120]{1,0:T(8,128)(2,1)S(1)}, bf16[32,5120]{1,0:T(8,128)(2,1)S(1)}, u32[]{:S(2)}, u32[]{:S(2)}) collective-permute-start(bf16[32,5120]{1,0:T(8,128)(2,1)S(1)} %get-tuple-element.58), channel_id=1, source_target_pairs={{8,0},{12,4},{16,24},{20,28},{9,1},{13,5},{17,25},{21,29},{10,2},{... | collective-permute-start | bytes 983048 | tf_op jit(solution)/shard_map/ppermute | solution.py:370
  65.6 11.2 %collective-permute-start.15 = (bf16[32,3072]{1,0:T(8,128)(2,1)S(1)}, bf16[32,3072]{1,0:T(8,128)(2,1)S(1)}, u32[]{:S(2)}, u32[]{:S(2)}) collective-permute-start(bf16[32,3072]{1,0:T(8,128)(2,1)S(1)} %get-tuple-element.52), channel_id=1, source_target_pairs={{8,0},{12,4},{16,24},{20,28},{9,1},{13,5},{17,25},{21,29},{10,2},{... | collective-permute-start | bytes 589832 | tf_op jit(solution)/shard_map/ppermute | solution.py:370
  66.9 9.9 %collective-permute-start.16 = (bf16[32,3072]{1,0:T(8,128)(2,1)S(1)}, bf16[32,3072]{1,0:T(8,128)(2,1)S(1)}, u32[]{:S(2)}, u32[]{:S(2)}) collective-permute-start(bf16[32,3072]{1,0:T(8,128)(2,1)S(1)} %get-tuple-element.53), channel_id=1, source_target_pairs={{8,4},{12,0},{16,28},{20,24},{9,5},{13,1},{17,29},{21,25},{10,6},{... | collective-permute-start | bytes 589832 | tf_op jit(solution)/shard_map/ppermute | solution.py:370
  82.1 1.6 %collective-permute-start.18 = (f32[4,32,512]{2,1,0:T(8,128)S(1)}, f32[4,32,512]{2,1,0:T(8,128)S(1)}, u32[]{:S(2)}, u32[]{:S(2)}) collective-permute-start(f32[4,32,512]{2,1,0:T(8,128)S(1)} %get-tuple-element.62), channel_id=1, source_target_pairs={{0,1},{1,0},{2,3},{3,2},{4,5},{5,4},{6,7},{7,6},{8,9},{9,8},{10,11... | collective-permute-start | bytes 786440 | tf_op jit(solution)/shard_map/ppermute | solution.py:383
  83.8 5.6 %collective-permute-start.19 = (f32[2,32,512]{2,1,0:T(8,128)S(1)}, f32[2,32,512]{2,1,0:T(8,128)S(1)}, u32[]{:S(2)}, u32[]{:S(2)}) collective-permute-start(f32[2,32,512]{2,1,0:T(8,128)S(1)} %slice.9), channel_id=1, source_target_pairs={{0,2},{1,3},{2,0},{3,1},{4,6},{5,7},{6,4},{7,5},{8,10},{9,11},{10,... | collective-permute-start | bytes 393224 | tf_op jit(solution)/shard_map/ppermute | solution.py:388
